TPU v7x, 32 devices: a whole 2x2x4 slice. The times are simulated.
32 devices in a mesh: batch: 8 (over z, x), rows: 4 (over y, core).
Axes of the slice: x: 2, y: 2, z: 4, core: 2. Of those that a mesh axis runs over, the one named last changes fastest.
Arguments:
- images: bfloat16 [8, 32, 16, 512], P('batch', 'rows')
- heights: int32 [8], replicated, may hold values from 8 to 32, as said below
- groups: int32 [8], replicated, may hold values from 0 to 1, as said below
- ratios: float32 [3], replicated, may hold values from 0.5 to 1.5
- task_cotangent: bfloat16 [3, 8, 16, 8, 512], P(None, 'batch', 'rows'), may hold values from -6 to 6
- kernels: float32 [32, 5, 73728], P(('batch', 'rows')), may hold values from -0.09375 to 0.09375
- moment_kernels: float32 [32, 5, 73728], P(('batch', 'rows'))
- square_kernels: float32 [32, 5, 73728], P(('batch', 'rows'))
- attention: float32 [32, 2, 6144], P(('batch', 'rows')), may hold values from -0.375 to 0.375
- moment_attention: float32 [32, 2, 6144], P(('batch', 'rows'))
- square_attention: float32 [32, 2, 6144], P(('batch', 'rows'))
- affine: float32 [2, 4480], replicated
- moment_affine: float32 [2, 4480], replicated
- square_affine: float32 [2, 4480], replicated
Outputs:
- pooled: float32 [3, 8, 16, 8, 512], P(None, 'batch', 'rows')
- image_grad: float32 [8, 32, 16, 512], P('batch', 'rows')
- kernels_new: float32 [32, 5, 73728], P(('batch', 'rows'))
- kernels_moment: float32 [32, 5, 73728], P(('batch', 'rows'))
- kernels_square: float32 [32, 5, 73728], P(('batch', 'rows'))
- attention_new: float32 [32, 2, 6144], P(('batch', 'rows'))
- attention_moment: float32 [32, 2, 6144], P(('batch', 'rows'))
- attention_square: float32 [32, 2, 6144], P(('batch', 'rows'))
- affine_new: float32 [2, 4480], replicated
- affine_moment: float32 [2, 4480], replicated
- affine_square: float32 [2, 4480], replicated
Inputs may be any that keep to these rules, and one draw needn't show every extreme that they name: `heights`: each height is a multiple of 8, so each device of rows holds an even number of a slot's image rows. Slots of group 1 are no taller than 16. Some slot of group 0 has height 32 and some slot of group 1 the least height. 0: one image 16 columns wide; 1: two images of 8 columns and the slot's height side by side. Both groups occur.
All inputs are finite; a program needn't handle non-finite values.
Results may differ from a plain program's by a relative error of at most 0.012.
The roundings to bfloat16 on the way count: a program that leaves them out, or rounds other values in their place, can miss the bound.
Values may be sent and summed in bfloat16 or wider, within the bound.
No kernel may reach another device: no remote copies, remote signals or barrier semaphores. Data moves between devices by JAX's collectives and lax.ppermute only.
A program may use at most 320 MiB of HBM per device.

v0:
```python
import jax
import jax.numpy as jnp
from jax import lax
from jax.sharding import PartitionSpec as P

C = 512
B = 128
TASK_COUNT = 3
ADAM_STEP = 10


NORM_EPS = 1e-05
BETA_ONE = 0.9
BETA_TWO = 0.999
ADAM_EPS = 1e-08
DECAY = 0.01
RATE_KERNEL = 0.02
RATE_ATTEND = 0.08
RATE_AFFINE = 0.4
SOFTMAX_TEMP = 2.0


def with_halo(cells, sides, width):
    for axis, dim in sides:
        count = lax.axis_size(axis)
        ends = count - 1
        head = lax.slice_in_dim(cells, 0, width, axis=dim)
        tail = lax.slice_in_dim(cells, cells.shape[dim] - width, cells.shape[dim], axis=dim)
        cells = jnp.concatenate(
            [
                lax.ppermute(tail, axis, [(i, (i + 1) % count) for i in range(ends)]),
                cells,
                lax.ppermute(head, axis, [((i + 1) % count, i) for i in range(ends)]),
            ],
            axis=dim,
        )
    return cells


def take_rows(sample_data, example_rows):
    return sample_data[example_rows]


def local_geometry(images, heights, groups):
    slot_count, band_len, col_count = (images.shape[0], images.shape[1], images.shape[2])
    slot_ids = lax.axis_index("batch") * slot_count + jnp.arange(slot_count, dtype=jnp.int32)
    band_rows = heights[slot_ids] // lax.axis_size("rows")
    local_row = jnp.arange(band_len, dtype=jnp.int32)
    is_valid = local_row[None, :] < band_rows[:, None]
    is_last = local_row[None, :] == band_rows[:, None] - 1
    is_first = local_row[None, :] == 0
    col_ids = jnp.arange(col_count, dtype=jnp.int32)
    halves = groups[slot_ids][:, None] == 1
    left_ok = (col_ids[None, :] > 0) & ~(halves & (col_ids[None, :] == col_count // 2))
    right_ok = (col_ids[None, :] < col_count - 1) & ~(
        halves & (col_ids[None, :] == col_count // 2 - 1)
    )
    valid_mask = is_valid.astype(jnp.float32)[None, :, :, None, None]
    valid_low = valid_mask.astype(jnp.bfloat16)
    last_hot = is_last.astype(jnp.bfloat16)[None, :, :, None, None]
    first_hot = is_first.astype(jnp.float32)[None, :, :, None, None]
    left_low = left_ok.astype(jnp.bfloat16)[None, :, None, :, None]
    right_low = right_ok.astype(jnp.bfloat16)[None, :, None, :, None]
    pixel_count = jnp.sum(heights).astype(jnp.float32) * col_count
    return (
        valid_mask,
        valid_low,
        last_hot,
        first_hot,
        left_low,
        right_low,
        band_rows - 1,
        pixel_count,
    )


def shift_columns(middle_value, left_ok, right_ok):
    zero_col = jnp.zeros_like(middle_value[..., :1, :])
    left_cols = jnp.concatenate([zero_col, middle_value[..., :-1, :]], axis=-2) * left_ok
    right_cols = jnp.concatenate([middle_value[..., 1:, :], zero_col], axis=-2) * right_ok
    return (left_cols, middle_value, right_cols)


def row_versions(inputs, upper_rim, lower_rim, last_hot):
    zero_row = jnp.zeros_like(inputs[:, :, :1])
    up_rows = jnp.concatenate([upper_rim[:, :, None], inputs[:, :, :-1]], axis=2)
    down_rows = (
        jnp.concatenate([inputs[:, :, 1:], zero_row], axis=2) + last_hot * lower_rim[:, :, None]
    )
    return (up_rows, inputs, down_rows)


def build_patches(inputs, upper_rim, lower_rim, geometry_set):
    pieces = []
    for middle_value in row_versions(inputs, upper_rim, lower_rim, geometry_set[2]):
        pieces.extend(shift_columns(middle_value, geometry_set[4], geometry_set[5]))
    return jnp.concatenate(pieces, axis=-1)


def convolve_forward(inputs, kernel, geometry_set):
    task_count, slot_count = (inputs.shape[0], inputs.shape[1])
    flat_in = inputs.reshape((task_count * slot_count,) + inputs.shape[2:])
    last_rows = jax.vmap(take_rows)(flat_in, jnp.tile(geometry_set[6], task_count))
    edge_rows = jnp.stack([flat_in[:, 0], last_rows], axis=1)
    rim_rows = with_halo(edge_rows, (("rows", 1),), 1)
    upper_rim = rim_rows[:, 0].reshape((task_count, slot_count) + inputs.shape[3:])
    lower_rim = rim_rows[:, 3].reshape((task_count, slot_count) + inputs.shape[3:])
    patches = build_patches(inputs, upper_rim, lower_rim, geometry_set)
    summed = jnp.einsum("tshwk,tkd->tshwd", patches, kernel, preferred_element_type=jnp.float32)
    return (summed, upper_rim, lower_rim)


def convolve_backward(inputs, upper_rim, lower_rim, grad_low, kernel, geometry_set):
    valid_mask, valid_low, last_hot, first_hot, left_ok, right_ok, last_index, pixel_count = (
        geometry_set
    )
    task_count, slot_count = (inputs.shape[0], inputs.shape[1])
    channels = inputs.shape[-1]
    patches = build_patches(inputs, upper_rim, lower_rim, geometry_set)
    kernel_grad = jnp.einsum(
        "tshwk,tshwd->tkd", patches, grad_low, preferred_element_type=jnp.float32
    )
    tap_grads = jnp.einsum("tshwd,tkd->tshwk", grad_low, kernel, preferred_element_type=jnp.float32)
    tap_grads = tap_grads.reshape(tap_grads.shape[:-1] + (9, channels))
    row_grads = []
    for row_shift in range(3):
        row_accum = None
        for col_shift in range(3):
            shifted_grad = tap_grads[..., 3 * row_shift + col_shift, :]
            zero_col = jnp.zeros_like(shifted_grad[..., :1, :])
            if col_shift == 0:
                masked = shifted_grad * left_ok
                returned_rows = jnp.concatenate([masked[..., 1:, :], zero_col], axis=-2)
            elif col_shift == 2:
                masked = shifted_grad * right_ok
                returned_rows = jnp.concatenate([zero_col, masked[..., :-1, :]], axis=-2)
            else:
                returned_rows = shifted_grad
            row_accum = returned_rows if row_accum is None else row_accum + returned_rows
        row_grads.append(row_accum)
    up_grad, mid_grad, down_grad = row_grads
    zero_row = jnp.zeros_like(mid_grad[:, :, :1])
    input_grad = mid_grad + jnp.concatenate([up_grad[:, :, 1:], zero_row], axis=2)
    input_grad = input_grad + jnp.concatenate([zero_row, down_grad[:, :, :-1]], axis=2)
    flat_down = down_grad.reshape((task_count * slot_count,) + down_grad.shape[2:])
    lower_grad = jax.vmap(take_rows)(flat_down, jnp.tile(last_index, task_count))
    upper_grad = up_grad[:, :, 0].reshape((task_count * slot_count,) + up_grad.shape[3:])
    outgoing = jnp.stack([upper_grad, lower_grad], axis=1)
    returned = with_halo(outgoing.astype(jnp.bfloat16), (("rows", 1),), 1).astype(outgoing.dtype)
    from_above = returned[:, 0].reshape((task_count, slot_count) + inputs.shape[3:])
    from_below = returned[:, 3].reshape((task_count, slot_count) + inputs.shape[3:])
    input_grad = input_grad + first_hot * from_above[:, :, None] + last_hot * from_below[:, :, None]
    return (input_grad * valid_mask, kernel_grad)


def norm_forward(values, gain_row, bias_row, geometry_set):
    valid_mask, pixel_count = (geometry_set[0], geometry_set[7])
    masked = values * valid_mask
    totals = lax.psum(
        (jnp.sum(masked, axis=(1, 2, 3)), jnp.sum(masked * values, axis=(1, 2, 3))),
        ("batch", "rows"),
    )
    average = totals[0] / pixel_count
    spread = totals[1] / pixel_count - average * average
    inverse = lax.rsqrt(spread + NORM_EPS)
    normed = (values - average[:, None, None, None]) * inverse[:, None, None, None]
    return (normed * gain_row[:, None, None, None] + bias_row[:, None, None, None], normed, inverse)


def norm_backward(out_grad, normed, inverse, gain_row, geometry_set):
    valid_mask, pixel_count = (geometry_set[0], geometry_set[7])
    masked = out_grad * valid_mask
    totals = lax.psum(
        (jnp.sum(masked * normed, axis=(1, 2, 3)), jnp.sum(masked, axis=(1, 2, 3))),
        ("batch", "rows"),
    )
    gain_grad, bias_grad = totals
    scale_row = (gain_row * inverse)[:, None, None, None]
    centered = (
        masked
        - (bias_grad[:, None, None, None] + normed * gain_grad[:, None, None, None]) / pixel_count
    )
    return (scale_row * centered * valid_mask, gain_grad, bias_grad)


def gelu_grad(pre_act, out_grad):
    return jax.vjp(jax.nn.gelu, pre_act)[1](out_grad)[0]


def adamw(weights_in, grad_in, moment_old, square_old, step_rate):
    moment_new = BETA_ONE * moment_old + (1.0 - BETA_ONE) * grad_in
    square_new = BETA_TWO * square_old + (1.0 - BETA_TWO) * grad_in * grad_in
    moment_hat = moment_new / (1.0 - BETA_ONE**ADAM_STEP)
    square_hat = square_new / (1.0 - BETA_TWO**ADAM_STEP)
    updated = weights_in - step_rate * (
        moment_hat / (jnp.sqrt(square_hat) + ADAM_EPS) + DECAY * weights_in
    )
    return (updated, moment_new, square_new)


def whole_rows(pieces):
    return jnp.transpose(pieces, (1, 0, 2)).reshape(pieces.shape[1], -1)


def owner_pieces(flat_rows, device_count):
    row_count, row_len = flat_rows.shape
    return jnp.transpose(
        flat_rows.reshape(row_count, device_count, row_len // device_count), (1, 0, 2)
    )


def unpack_weights(gathered):
    kernel_all = whole_rows(gathered[0]).reshape(2 + TASK_COUNT, 9 * C, C)
    attend_all = whole_rows(gathered[1])
    return (
        kernel_all,
        attend_all[0].reshape(TASK_COUNT, C, B),
        attend_all[1].reshape(TASK_COUNT, B, C),
    )


def local(
    images,
    heights,
    groups,
    ratios,
    task_cotangent,
    kernels,
    moment_kernels,
    square_kernels,
    attention,
    moment_attention,
    square_attention,
    affine,
    moment_affine,
    square_affine,
):
    geometry_set = local_geometry(images, heights, groups)
    valid_mask = geometry_set[0]
    device_count = lax.axis_size("batch") * lax.axis_size("rows")
    slot_count, band_len, col_count = (images.shape[0], images.shape[1], images.shape[2])
    gathered = (
        lax.all_gather(kernels.astype(jnp.bfloat16), ("batch", "rows"), axis=0, tiled=True),
        lax.all_gather(attention.astype(jnp.bfloat16), ("batch", "rows"), axis=0, tiled=True),
    )
    kernel_all, down_all, up_all = unpack_weights(gathered)
    gain_all, bias_all = (affine[0], affine[1])
    down_start = 2 * C
    up_start = down_start + TASK_COUNT * B
    conv_start = up_start + TASK_COUNT * C
    down_gain = gain_all[down_start:up_start].reshape(TASK_COUNT, B)
    up_gain = gain_all[up_start:conv_start].reshape(TASK_COUNT, C)
    task_gain = gain_all[conv_start:].reshape(TASK_COUNT, C)
    start_rows = images[None] * geometry_set[1]
    first_out, first_upper, first_lower = convolve_forward(
        start_rows, kernel_all[0:1], geometry_set
    )
    first_pre, first_normed, first_inverse = norm_forward(
        first_out, gain_all[None, 0:C], bias_all[None, 0:C], geometry_set
    )
    first_act = (jax.nn.gelu(first_pre) * valid_mask).astype(jnp.bfloat16)
    second_output, second_upper, second_lower = convolve_forward(
        first_act, kernel_all[1:2], geometry_set
    )
    second_pre, second_normed, second_inverse = norm_forward(
        second_output, gain_all[None, C : 2 * C], bias_all[None, C : 2 * C], geometry_set
    )
    second_act = jax.nn.gelu(second_pre) * valid_mask
    hidden = jnp.einsum(
        "shwc,tcb->tshwb", first_act[0], down_all, preferred_element_type=jnp.float32
    )
    hidden_pre, hidden_normed, hidden_inverse = norm_forward(
        hidden, down_gain, bias_all[down_start:up_start].reshape(TASK_COUNT, B), geometry_set
    )
    squeezed = (jax.nn.gelu(hidden_pre) * valid_mask).astype(jnp.bfloat16)
    expanded = jnp.einsum("tshwb,tbc->tshwc", squeezed, up_all, preferred_element_type=jnp.float32)
    expand_pre, expand_normed, expand_inverse = norm_forward(
        expanded, up_gain, bias_all[up_start:conv_start].reshape(TASK_COUNT, C), geometry_set
    )
    attend_mask = jax.nn.sigmoid(expand_pre)
    selected = (attend_mask * second_act).astype(jnp.bfloat16)
    task_out, task_upper_rim, task_lower = convolve_forward(selected, kernel_all[2:], geometry_set)
    task_pre, task_normed, task_inverse = norm_forward(
        task_out, task_gain, bias_all[conv_start:].reshape(TASK_COUNT, C), geometry_set
    )
    activated = jax.nn.gelu(task_pre) * valid_mask
    pooled = jnp.mean(
        activated.reshape(TASK_COUNT, slot_count, band_len // 2, 2, col_count // 2, 2, C),
        axis=(3, 5),
    )
    regathered = (
        lax.all_gather(kernels.astype(jnp.bfloat16), ("batch", "rows"), axis=0, tiled=True),
        lax.all_gather(attention.astype(jnp.bfloat16), ("batch", "rows"), axis=0, tiled=True),
    )
    kernel_back, down_back, up_back = unpack_weights(regathered)
    task_weight_stack = TASK_COUNT * jax.nn.softmax(ratios / SOFTMAX_TEMP)
    pooled_grad = task_weight_stack[:, None, None, None, None] * task_cotangent.astype(jnp.float32)
    act_grad = jnp.repeat(jnp.repeat(pooled_grad, 2, axis=2), 2, axis=3) * 0.25
    task_pre_grad = gelu_grad(task_pre, act_grad * valid_mask)
    task_out_grad, task_gain_grad, task_bias_grad = norm_backward(
        task_pre_grad, task_normed, task_inverse, task_gain, geometry_set
    )
    selected_grad, task_kernel_grad = convolve_backward(
        selected,
        task_upper_rim,
        task_lower,
        task_out_grad.astype(jnp.bfloat16),
        kernel_back[2:],
        geometry_set,
    )
    mask_grad = selected_grad * second_act
    second_from_tasks = jnp.sum(selected_grad * attend_mask, axis=0, keepdims=True)
    expand_pre_grad = mask_grad * attend_mask * (1.0 - attend_mask)
    expand_grad, up_gain_grad, up_bias_grad = norm_backward(
        expand_pre_grad, expand_normed, expand_inverse, up_gain, geometry_set
    )
    expand_low = expand_grad.astype(jnp.bfloat16)
    up_kernel_grad = jnp.einsum(
        "tshwb,tshwc->tbc", squeezed, expand_low, preferred_element_type=jnp.float32
    )
    squeezed_grad = jnp.einsum(
        "tshwc,tbc->tshwb", expand_low, up_back, preferred_element_type=jnp.float32
    )
    hidden_pre_grad = gelu_grad(hidden_pre, squeezed_grad * valid_mask)
    hidden_grad, down_gain_grad, down_bias_grad = norm_backward(
        hidden_pre_grad, hidden_normed, hidden_inverse, down_gain, geometry_set
    )
    hidden_low = hidden_grad.astype(jnp.bfloat16)
    down_kernel_grad = jnp.einsum(
        "shwc,tshwb->tcb", first_act[0], hidden_low, preferred_element_type=jnp.float32
    )
    first_from_attend = jnp.einsum(
        "tshwb,tcb->shwc", hidden_low, down_back, preferred_element_type=jnp.float32
    )[None]
    attend_grads = jnp.stack([down_kernel_grad.reshape(-1), up_kernel_grad.reshape(-1)])
    second_pre_grad = gelu_grad(second_pre, second_from_tasks * valid_mask)
    second_out_grad, second_gain_grad, second_bias_grad = norm_backward(
        second_pre_grad, second_normed, second_inverse, gain_all[None, C : 2 * C], geometry_set
    )
    first_act_grad, second_kernel_grad = convolve_backward(
        first_act,
        second_upper,
        second_lower,
        second_out_grad.astype(jnp.bfloat16),
        kernel_back[1:2],
        geometry_set,
    )
    first_pre_grad = gelu_grad(first_pre, (first_act_grad + first_from_attend) * valid_mask)
    first_out_grad, first_gain_grad, first_bias_grad = norm_backward(
        first_pre_grad, first_normed, first_inverse, gain_all[None, 0:C], geometry_set
    )
    start_grad, first_kernel_grad = convolve_backward(
        start_rows,
        first_upper,
        first_lower,
        first_out_grad.astype(jnp.bfloat16),
        kernel_back[0:1],
        geometry_set,
    )
    image_grad = start_grad[0]
    kernel_grads = jnp.concatenate(
        [
            first_kernel_grad.reshape(1, -1),
            second_kernel_grad.reshape(1, -1),
            task_kernel_grad.reshape(TASK_COUNT, -1),
        ],
        axis=0,
    )
    kernel_shard, attend_shard = (
        lax.psum_scatter(
            owner_pieces(kernel_grads, device_count),
            ("batch", "rows"),
            scatter_dimension=0,
            tiled=True,
        ),
        lax.psum_scatter(
            owner_pieces(attend_grads, device_count),
            ("batch", "rows"),
            scatter_dimension=0,
            tiled=True,
        ),
    )
    gain_grads = jnp.concatenate(
        [
            first_gain_grad.reshape(-1),
            second_gain_grad.reshape(-1),
            down_gain_grad.reshape(-1),
            up_gain_grad.reshape(-1),
            task_gain_grad.reshape(-1),
        ]
    )
    bias_grads = jnp.concatenate(
        [
            first_bias_grad.reshape(-1),
            second_bias_grad.reshape(-1),
            down_bias_grad.reshape(-1),
            up_bias_grad.reshape(-1),
            task_bias_grad.reshape(-1),
        ]
    )
    affine_grad = jnp.stack([gain_grads, bias_grads])
    kernels_new, kernels_moment, kernels_square = adamw(
        kernels, kernel_shard, moment_kernels, square_kernels, RATE_KERNEL
    )
    attention_new, attention_moment, attention_square = adamw(
        attention, attend_shard, moment_attention, square_attention, RATE_ATTEND
    )
    affine_new, affine_moment, affine_square = adamw(
        affine, affine_grad, moment_affine, square_affine, RATE_AFFINE
    )
    return (
        pooled,
        image_grad,
        kernels_new,
        kernels_moment,
        kernels_square,
        attention_new,
        attention_moment,
        attention_square,
        affine_new,
        affine_moment,
        affine_square,
    )


def solution(mesh):
    return jax.shard_map(
        local,
        mesh=mesh,
        in_specs=(
            P("batch", "rows", None, None),
            P(),
            P(),
            P(),
            P(None, "batch", "rows", None, None),
            P(("batch", "rows"), None, None),
            P(("batch", "rows"), None, None),
            P(("batch", "rows"), None, None),
            P(("batch", "rows"), None, None),
            P(("batch", "rows"), None, None),
            P(("batch", "rows"), None, None),
            P(),
            P(),
            P(),
        ),
        out_specs=(
            P(None, "batch", "rows", None, None),
            P("batch", "rows", None, None),
            P(("batch", "rows"), None, None),
            P(("batch", "rows"), None, None),
            P(("batch", "rows"), None, None),
            P(("batch", "rows"), None, None),
            P(("batch", "rows"), None, None),
            P(("batch", "rows"), None, None),
            P(),
            P(),
            P(),
        ),
        check_vma=False,
    )
```

profile of v0, /device:TPU:0, one launch (start us, length us, event | category | flops | bytes accessed | tf_op | source)
XLA Modules:
  0.0 1667.3 jit_solution(1773007564756836504)
XLA Ops:
  7.3 3.3 copy.187
  15.3 3.0 collective-permute-start
  25.5 48.6 %all_gather.9 = bf16[32,2,6144]{2,1,0:T(2,128)(2,1)S(1)} all-gather(bf16[1,2,6144]{2,1,0:T(2,128)(2,1)S(1)} %convert_element_type.224), channel_id=1, replica_groups=mesh['batch'=8,'rows'=4] {'batch','rows'}, dimensions={0}, use_global_device_ids=true | all-gather | bytes 811008 | tf_op jit(solution)/shard_map/all_gather | solution.py:244
  74.1 3.4 slice_reduce_fusion.3
  84.1 148.7 %all-gather.2.cloned.1.call-done = bf16[32,5,73728]{2,1,0:T(8,128)(2,1)} async-done(((bf16[1,5,73728]{2,1,0:T(8,128)(2,1)}), bf16[32,5,73728]{2,1,0:T(8,128)(2,1)}) %all-gather.2.cloned.1.call-update) | async-done | bytes 23592976 | tf_op jit(solution)/shard_map/all_gather | solution.py:243
  232.8 47.3 %slice_reduce_fusion.1 = (bf16[32,73728]{1,0:T(8,128)(2,1)}, bf16[32,73728]{1,0:T(8,128)(2,1)}) fusion(bf16[5,32,73728]{2,0,1:T(8,128)(2,1)} %bitcast.428), kind=kLoop, calls=%fused_computation.9 | loop fusion | bytes 18874368 | tf_op jit(solution)/shard_map/slice | solution.py:256
  280.1 6.0 reshape.1276
  286.1 3.1 fusion.63
  289.3 38.8 %all-reduce.55 = (f32[1,512]{1,0:T(1,128)S(1)}, f32[1,512]{1,0:T(1,128)S(1)}) all-reduce(f32[1,512]{1,0:T(1,128)S(1)} %bitcast.495, f32[1,512]{1,0:T(1,128)S(1)} %bitcast.494), channel_id=1, replica_groups=mesh['batch'=8,'rows'=4] {'batch','rows'}, use_global_device_ids=true, to_apply=%region_1.2 | all-reduce | flops 1024 | bytes 8192 | tf_op jit(solution)/shard_map/psum | solution.py:159
  330.8 41.4 %all-reduce.54 = (f32[3,128]{1,0:T(4,128)S(1)}, f32[3,128]{1,0:T(4,128)S(1)}) all-reduce(f32[3,128]{1,0:T(4,128)S(1)} %get-tuple-element.132, f32[3,128]{1,0:T(4,128)S(1)} %get-tuple-element.131), channel_id=1, replica_groups=mesh['batch'=8,'rows'=4] {'batch','rows'}, use_global_device_ids=true, to_apply=%region_8.9 | all-reduce | flops 768 | bytes 6144 | tf_op jit(solution)/shard_map/psum | solution.py:159
  373.2 19.9 %slice.632 = bf16[3,32,73728]{2,0,1:T(4,128)(2,1)} slice(bf16[5,32,73728]{2,0,1:T(8,128)(2,1)} %bitcast.429), slice={[2:5], [0:32], [0:73728]} | slice | bytes 28311552 | tf_op jit(solution)/shard_map/slice | solution.py:282
  393.1 6.0 reshape.1283
  399.1 6.1 reshape.1280
  405.2 15.6 copy.88
  420.8 16.7 %reshape.1281 = bf16[3,4608,512,1]{2,1,0,3:T(8,128)(2,1)} reshape(bf16[3,32,73728]{2,1,0:T(8,128)(2,1)} %copy.88) | data formatting | bytes 28311552 | tf_op jit(solution)/shard_map/slice | solution.py:282
  440.6 3.6 fusion.72
  444.2 42.6 %all-reduce.53 = (f32[1,512]{1,0:T(1,128)S(1)}, f32[1,512]{1,0:T(1,128)S(1)}, f32[3,512]{1,0:T(4,128)S(1)}, f32[3,512]{1,0:T(4,128)S(1)}) all-reduce(f32[1,512]{1,0:T(1,128)S(1)} %bitcast.493, f32[1,512]{1,0:T(1,128)S(1)} %bitcast.492, f32[3,512]{1,0:T(4,128)S(1)} %get-tuple-element.117, ...), channel_id=1, replica_groups=mesh['batch'=8,'rows'=4] {'batch','rows'}, use_global_device_ids=true, to_apply=%region_14.15 | all-reduce | flops 4096 | bytes 32768 | tf_op jit(solution)/shard_map/psum | solution.py:159
  491.8 3.0 collective-permute-start.4
  499.1 8.5 multiply_reduce_fusion
  507.7 43.2 %all-reduce.52 = (f32[3,512]{1,0:T(4,128)}, f32[3,512]{1,0:T(4,128)}) all-reduce(f32[3,512]{1,0:T(4,128)} %get-tuple-element.115, f32[3,512]{1,0:T(4,128)} %get-tuple-element.114), channel_id=1, replica_groups=mesh['batch'=8,'rows'=4] {'batch','rows'}, use_global_device_ids=true, to_apply=%region_20.21 | all-reduce | flops 3072 | bytes 24576 | tf_op jit(solution)/shard_map/psum | solution.py:159
  552.8 4.0 fusion.150
  556.8 40.4 %all-reduce.51 = (f32[3,512]{1,0:T(4,128)}, f32[3,512]{1,0:T(4,128)}) all-reduce(f32[3,512]{1,0:T(4,128)} %get-tuple-element.120, f32[3,512]{1,0:T(4,128)} %get-tuple-element.119), channel_id=1, replica_groups=mesh['batch'=8,'rows'=4] {'batch','rows'}, use_global_device_ids=true, to_apply=%region_27.28 | all-reduce | flops 3072 | bytes 24576 | tf_op jit(solution)/shard_map/psum | solution.py:173
  599.6 12.6 fusion
  612.2 9.5 reshape.1083
  621.6 22.6 %fusion.163 = (f32[3,1,8,16,1,512]{5,4,3,2,0,1:T(1,128)S(1)}, f32[3,1,8,16,1,512]{5,4,3,2,0,1:T(1,128)S(1)}, f32[3,1,8,16,1,512]{5,4,3,2,0,1:T(1,128)S(1)}, f32[...) fusion(f32[3,1,8,16,9,512]{5,4,3,2,0,1:T(8,128)} %reshape.1083), kind=kLoop, calls=%fused_computation.380 | loop fusion | bytes 14155776 | tf_op jit(solution)/shard_map/slice | solution.py:129
  649.5 2.4 gather_fusion.1
  655.9 4.0 collective-permute-start.6
  659.9 11.2 convolution_bitcast_fusion
  671.1 23.5 %concatenate.334 = f32[3,32,73728]{2,1,0:T(8,128)} reshape(f32[3,4608,512]{2,1,0:T(8,128)} %convolution_bitcast_fusion) | data formatting | bytes 56623104 | tf_op jit(solution)/shard_map/concatenate | solution.py:361
  694.7 37.6 %copy.104 = f32[3,32,73728]{2,0,1:T(4,128)} copy(f32[3,32,73728]{2,1,0:T(8,128)} %concatenate.334) | data formatting | bytes 56623104 | tf_op jit(solution)/shard_map/concatenate | solution.py:361
  734.9 41.4 %all-reduce.50 = (f32[3,512]{1,0:T(4,128)S(1)}, f32[3,512]{1,0:T(4,128)S(1)}) all-reduce(f32[3,512]{1,0:T(4,128)S(1)} %get-tuple-element.112, f32[3,512]{1,0:T(4,128)S(1)} %get-tuple-element.118), channel_id=1, replica_groups=mesh['batch'=8,'rows'=4] {'batch','rows'}, use_global_device_ids=true, to_apply=%region_36.37 | all-reduce | flops 3072 | bytes 24576 | tf_op jit(solution)/shard_map/psum | solution.py:173
  778.4 39.7 %all-reduce.49 = (f32[512]{0:T(512)S(1)}, f32[512]{0:T(512)S(1)}, f32[3,128]{1,0:T(4,128)S(1)}, f32[3,128]{1,0:T(4,128)S(1)}) all-reduce(f32[512]{0:T(512)S(1)} %get-tuple-element.130, f32[512]{0:T(512)S(1)} %get-tuple-element.129, f32[3,128]{1,0:T(4,128)S(1)} %get-tuple-element.134, ...), channel_id=1, replica_groups=mesh['batch'=8,'rows'=4] {'batch','rows'}, use_global_device_ids=true, to_apply=%region_32.33 | all-reduce | flops 1792 | bytes 14336 | tf_op jit(solution)/shard_map/psum | solution.py:173
  818.2 4.0 fusion.14
  827.5 5.1 convolution_bitcast_fusion.1
  844.4 3.0 collective-permute-start.8
  847.5 24.4 %concatenate.355 = f32[1,32,73728]{2,0,1:T(1,128)} reshape(f32[4608,512]{1,0:T(8,128)} %convolution_bitcast_fusion.1) | data formatting | bytes 18874368 | tf_op jit(solution)/shard_map/concatenate | solution.py:361
  873.8 41.2 %all-reduce.48 = (f32[512]{0:T(512)S(1)}, f32[512]{0:T(512)S(1)}) all-reduce(f32[512]{0:T(512)S(1)} %get-tuple-element.128, f32[512]{0:T(512)S(1)} %get-tuple-element.127), channel_id=1, replica_groups=mesh['batch'=8,'rows'=4] {'batch','rows'}, use_global_device_ids=true, to_apply=%region_44.45 | all-reduce | flops 1024 | bytes 8192 | tf_op jit(solution)/shard_map/psum | solution.py:173
  915.1 6.3 convolution_bitcast_fusion.2
  921.5 24.4 %concatenate.354 = f32[1,32,73728]{2,0,1:T(1,128)} reshape(f32[4608,512]{1,0:T(8,128)} %convolution_bitcast_fusion.2) | data formatting | bytes 18874368 | tf_op jit(solution)/shard_map/concatenate | solution.py:361
  945.9 43.9 %maximum_bitcast_fusion = f32[32,5,73728]{2,1,0:T(8,128)} fusion(f32[3,32,73728]{2,0,1:T(4,128)} %copy.104, f32[1,32,73728]{2,0,1:T(1,128)} %concatenate.355, f32[1,32,73728]{2,0,1:T(1,128)} %concatenate.354), kind=kLoop, calls=%fused_computation.2 | loop fusion | flops 23592960 | bytes 94371840 | tf_op jit(solution)/shard_map/transpose | solution.py:207
  989.9 6.1 reshape.1286
  998.0 4.8 fusion.17
  1008.3 3.0 collective-permute-done.11
  1013.8 632.6 %reduce-scatter.2.cloned.1.call-done = f32[1,5,73728]{2,1,0:T(8,128)} async-done(((f32[32,5,73728]{2,1,0:T(8,128)}), f32[1,5,73728]{2,1,0:T(8,128)}) %reduce-scatter.2.cloned.1.call-update) | async-done | bytes 1474576 | tf_op jit(solution)/shard_map/reduce_scatter | solution.py:370
  1646.4 6.3 copy_subtract_fusion
  1652.7 2.6 copy.111
  1655.4 2.6 copy.112
  1658.0 2.6 copy.113
  (438 shorter events, 76.3 us)
Async XLA Ops:
  7.3 225.5 %all-gather.2.cloned.1.call-start = ((), (), s32[]{:S(2)}) async-start(), calls=%async_computation.1 | async-start | bytes 38928384 | tf_op jit(solution)/shard_map/all_gather | solution.py:243
  10.6 1001.5 %all-reduce.58.cloned.1.call-start = ((), (), s32[]{:S(2)}) async-start(), calls=%async_computation.3 | async-start | bytes 3145728
  13.9 474.1 %copy-start.45 = (f32[8]{0:T(128)}, f32[8]{0:T(128)S(1)}, u32[]{:S(2)}) copy-start(f32[8]{0:T(128)S(1)} %get-tuple-element.283) | copy-start | bytes 100
  14.0 69.7 %collective-permute-start.1 = (bf16[1,1,16,512]{3,2,1,0:T(8,128)(2,1)S(1)}, bf16[1,1,16,512]{3,2,1,0:T(8,128)(2,1)S(1)}, u32[]{:S(2)}, u32[]{:S(2)}) collective-permute-start(bf16[1,1,16,512]{3,2,1,0:T(8,128)(2,1)S(1)} %get-tuple-element.239), channel_id=1, source_target_pairs={{1,0},{2,1},{3,2},{5,4},{6,5},{7,6},{9,8},{10,9},{11,10},{13,12},{... | collective-permute-start | bytes 49160 | tf_op jit(solution)/shard_map/ppermute | solution.py:33
  15.3 67.8 %collective-permute-start = (bf16[1,1,16,512]{3,2,1,0:T(8,128)(2,1)S(1)}, bf16[1,1,16,512]{3,2,1,0:T(8,128)(2,1)S(1)}, u32[]{:S(2)}, u32[]{:S(2)}) collective-permute-start(bf16[1,1,16,512]{3,2,1,0:T(8,128)(2,1)S(1)} %get-tuple-element.240), channel_id=1, source_target_pairs={{0,1},{1,2},{2,3},{4,5},{5,6},{6,7},{8,9},{9,10},{10,11},{12,13},{... | collective-permute-start | bytes 49160 | tf_op jit(solution)/shard_map/ppermute | solution.py:31
  19.7 420.8 %copy-start.71 = (bf16[16]{0:T(256)(128)(2,1)}, bf16[16]{0:T(256)(128)(2,1)S(1)}, u32[]{:S(2)}) copy-start(bf16[16]{0:T(256)(128)(2,1)S(1)} %and_convert_fusion) | copy-start | bytes 100
  19.7 420.6 %copy-start.73 = (bf16[16]{0:T(256)(128)(2,1)}, bf16[16]{0:T(256)(128)(2,1)S(1)}, u32[]{:S(2)}) copy-start(bf16[16]{0:T(256)(128)(2,1)S(1)} %and_convert_fusion.1) | copy-start | bytes 100
  19.7 475.1 %copy-start.101 = (bf16[8]{0:T(256)(128)(2,1)}, bf16[8]{0:T(256)(128)(2,1)S(1)}, u32[]{:S(2)}) copy-start(bf16[8]{0:T(256)(128)(2,1)S(1)} %compare_convert_fusion.1) | copy-start | bytes 52
  23.9 348.9 %copy-start.99 = (f32[384]{0:T(512)}, f32[384]{0:T(512)S(1)}, u32[]{:S(2)}) copy-start(f32[384]{0:T(512)S(1)} %get-tuple-element.139) | copy-start | bytes 4612
  23.9 348.9 %copy-start.104 = (f32[384]{0:T(512)}, f32[384]{0:T(512)S(1)}, u32[]{:S(2)}) copy-start(f32[384]{0:T(512)S(1)} %get-tuple-element.140) | copy-start | bytes 4612
  77.5 413.7 %copy-start.88 = (s32[3]{0:T(128)}, s32[3]{0:T(128)S(1)}, u32[]{:S(2)}) copy-start(s32[3]{0:T(128)S(1)} %or_bitcast_fusion) | copy-start | bytes 40
  80.0 408.3 %copy-start.42 = (f32[3,512]{1,0:T(4,128)}, f32[3,512]{1,0:T(4,128)S(1)}, u32[]{:S(2)}) copy-start(f32[3,512]{1,0:T(4,128)S(1)} %mul.1582) | copy-start | bytes 18436
  80.1 408.3 %copy-start.49 = (f32[3,512]{1,0:T(4,128)}, f32[3,512]{1,0:T(4,128)S(1)}, u32[]{:S(2)}) copy-start(f32[3,512]{1,0:T(4,128)S(1)} %add.498) | copy-start | bytes 18436
  82.6 247.9 %copy-start.27 = (bf16[3,512,128,1]{2,1,0,3:T(8,128)(2,1)}, bf16[3,512,128,1]{2,1,0,3:T(8,128)(2,1)S(1)}, u32[]{:S(2)}) copy-start(bf16[3,512,128,1]{2,1,0,3:T(8,128)(2,1)S(1)} %reshape.1278) | copy-start | bytes 1179652
  83.1 289.7 %copy-start.38 = (bf16[3,128,512,1]{2,1,0,3:T(8,128)(2,1)}, bf16[3,128,512,1]{2,1,0,3:T(8,128)(2,1)S(1)}, u32[]{:S(2)}) copy-start(bf16[3,128,512,1]{2,1,0,3:T(8,128)(2,1)S(1)} %reshape.1279) | copy-start | bytes 1179652
  84.1 202.0 %copy-start.24 = (bf16[1,1,8,16,4608]{4,3,2,1,0:T(8,128)(2,1)}, bf16[1,1,8,16,4608]{4,3,2,1,0:T(8,128)(2,1)S(1)}, u32[]{:S(2)}) copy-start(bf16[1,1,8,16,4608]{4,3,2,1,0:T(8,128)(2,1)S(1)} %multiply_dynamic-update-slice_fusion.12) | copy-start | bytes 3538948
  289.3 150.7 %copy-start.3 = (f32[8,16,512]{2,1,0:T(8,128)}, f32[8,16,512]{2,1,0:T(8,128)S(1)}, u32[]{:S(2)}) copy-start(f32[8,16,512]{2,1,0:T(8,128)S(1)} %get-tuple-element.276) | copy-start | bytes 786436
  328.7 111.3 %copy-start.59 = (f32[1,512]{1,0:T(1,128)}, f32[1,512]{1,0:T(1,128)S(1)}, u32[]{:S(2)}) copy-start(f32[1,512]{1,0:T(1,128)S(1)} %get-tuple-element.171) | copy-start | bytes 6148
  328.7 111.3 %copy-start.61 = (f32[1,512]{1,0:T(1,128)}, f32[1,512]{1,0:T(1,128)S(1)}, u32[]{:S(2)}) copy-start(f32[1,512]{1,0:T(1,128)S(1)} %get-tuple-element.172) | copy-start | bytes 6148
  328.7 111.3 %copy-start.65 = (f32[1,512]{1,0:T(1,128)}, f32[1,512]{1,0:T(1,128)S(1)}, u32[]{:S(2)}) copy-start(f32[1,512]{1,0:T(1,128)S(1)} %get-tuple-element.253) | copy-start | bytes 6148
  328.7 111.4 %copy-start.67 = (f32[1,512]{1,0:T(1,128)}, f32[1,512]{1,0:T(1,128)S(1)}, u32[]{:S(2)}) copy-start(f32[1,512]{1,0:T(1,128)S(1)} %get-tuple-element.254) | copy-start | bytes 6148
  328.8 64.2 %copy-start.34 = (bf16[8,16,512]{2,1,0:T(8,128)(2,1)}, bf16[8,16,512]{2,1,0:T(8,128)(2,1)S(1)}, u32[]{:S(2)}) copy-start(bf16[8,16,512]{2,1,0:T(8,128)(2,1)S(1)} %multiply_convert_fusion.3) | copy-start | bytes 393220
  329.2 109.6 %collective-permute-start.3 = (bf16[1,1,16,512]{3,2,1,0:T(8,128)(2,1)S(1)}, bf16[1,1,16,512]{3,2,1,0:T(8,128)(2,1)S(1)}, u32[]{:S(2)}, u32[]{:S(2)}) collective-permute-start(bf16[1,1,16,512]{3,2,1,0:T(8,128)(2,1)S(1)} %slice.617), channel_id=1, source_target_pairs={{1,0},{2,1},{3,2},{5,4},{6,5},{7,6},{9,8},{10,9},{11,10},{13,12},{... | collective-permute-start | bytes 49160 | tf_op jit(solution)/shard_map/ppermute | solution.py:33
  330.8 62.3 %copy-start.20 = (f32[3,1,8,16,128]{4,3,0,2,1:T(8,128)}, f32[3,1,8,16,128]{4,3,0,2,1:T(8,128)S(1)}, u32[]{:S(2)}) copy-start(f32[3,1,8,16,128]{4,3,0,2,1:T(8,128)S(1)} %get-tuple-element.278) | copy-start | bytes 589828
  373.2 115.3 %copy-start = (f32[3,8,16,512]{3,2,1,0:T(8,128)}, f32[3,8,16,512]{3,2,1,0:T(8,128)S(1)}, u32[]{:S(2)}) copy-start(f32[3,8,16,512]{3,2,1,0:T(8,128)S(1)} %get-tuple-element.279) | copy-start | bytes 2359300
  437.5 2.1 collective-permute-start.2
  444.2 46.9 %copy-start.9 = (f32[8,16,512]{2,1,0:T(8,128)}, f32[8,16,512]{2,1,0:T(8,128)S(1)}, u32[]{:S(2)}) copy-start(f32[8,16,512]{2,1,0:T(8,128)S(1)} %get-tuple-element.277) | copy-start | bytes 786436
  488.8 6.0 collective-permute-start.5
  491.8 3.9 collective-permute-start.4
  654.6 77.7 %collective-permute-start.7 = (bf16[3,1,16,512]{3,2,0,1:T(8,128)(2,1)}, bf16[3,1,16,512]{3,2,0,1:T(8,128)(2,1)}, u32[]{:S(2)}, u32[]{:S(2)}) collective-permute-start(bf16[3,1,16,512]{3,2,0,1:T(8,128)(2,1)} %fusion.135), channel_id=1, source_target_pairs={{1,0},{2,1},{3,2},{5,4},{6,5},{7,6},{9,8},{10,9},{11,10},{13,12},{... | collective-permute-start | bytes 147464 | tf_op jit(solution)/shard_map/ppermute | solution.py:33
  655.9 76.4 %collective-permute-start.6 = (bf16[3,1,16,512]{3,2,0,1:T(8,128)(2,1)}, bf16[3,1,16,512]{3,2,0,1:T(8,128)(2,1)}, u32[]{:S(2)}, u32[]{:S(2)}) collective-permute-start(bf16[3,1,16,512]{3,2,0,1:T(8,128)(2,1)} %bitcast.385), channel_id=1, source_target_pairs={{0,1},{1,2},{2,3},{4,5},{5,6},{6,7},{8,9},{9,10},{10,11},{12,13},{... | collective-permute-start | bytes 147464 | tf_op jit(solution)/shard_map/ppermute | solution.py:31
  733.3 43.0 %copy-start.81 = (f32[3,512]{1,0:T(4,128)S(1)}, f32[3,512]{1,0:T(4,128)}, u32[]{:S(2)}) copy-start(f32[3,512]{1,0:T(4,128)} %get-tuple-element.178) | copy-start | bytes 18436
  733.3 43.3 %copy-start.21 = (f32[3,1,8,16,128]{4,3,0,2,1:T(8,128)S(1)}, f32[3,1,8,16,128]{4,3,0,2,1:T(8,128)}, u32[]{:S(2)}) copy-start(f32[3,1,8,16,128]{4,3,0,2,1:T(8,128)} %copy-done.20) | copy-start | bytes 589828
  733.3 43.3 %copy-start.39 = (bf16[3,128,512,1]{2,1,0,3:T(8,128)(2,1)S(1)}, bf16[3,128,512,1]{2,1,0,3:T(8,128)(2,1)}, u32[]{:S(2)}) copy-start(bf16[3,128,512,1]{2,1,0,3:T(8,128)(2,1)} %copy-done.38) | copy-start | bytes 1179652
  733.3 43.3 %copy-start.90 = (f32[3,128]{1,0:T(4,128)S(1)}, f32[3,128]{1,0:T(4,128)}, u32[]{:S(2)}) copy-start(f32[3,128]{1,0:T(4,128)} %copy-done.89) | copy-start | bytes 4612
  733.3 43.3 %copy-start.93 = (f32[3,128]{1,0:T(4,128)S(1)}, f32[3,128]{1,0:T(4,128)}, u32[]{:S(2)}) copy-start(f32[3,128]{1,0:T(4,128)} %copy-done.92) | copy-start | bytes 4612
  733.3 43.3 %copy-start.100 = (f32[384]{0:T(512)S(1)}, f32[384]{0:T(512)}, u32[]{:S(2)}) copy-start(f32[384]{0:T(512)} %copy-done.99) | copy-start | bytes 4612
  733.3 43.3 %copy-start.105 = (f32[384]{0:T(512)S(1)}, f32[384]{0:T(512)}, u32[]{:S(2)}) copy-start(f32[384]{0:T(512)} %copy-done.104) | copy-start | bytes 4612
  734.9 42.8 %copy-start.22 = (f32[3,1,8,16,128]{4,3,0,2,1:T(8,128)S(1)}, f32[3,1,8,16,128]{4,3,0,2,1:T(8,128)}, u32[]{:S(2)}) copy-start(f32[3,1,8,16,128]{4,3,0,2,1:T(8,128)} %copy-done.20) | copy-start | bytes 589828
  776.7 41.5 %copy-start.107 = (f32[1,512]{1,0:T(1,128)S(1)}, f32[1,512]{1,0:T(1,128)}, u32[]{:S(2)}) copy-start(f32[1,512]{1,0:T(1,128)} %get-tuple-element.175) | copy-start | bytes 6148
  843.0 803.4 %reduce-scatter.2.cloned.1.call-start = ((), (), s32[]{:S(2)}) async-start(), calls=%async_computation.2 | async-start | bytes 77856768 | tf_op jit(solution)/shard_map/reduce_scatter | solution.py:370
  843.1 28.9 %collective-permute-start.9 = (bf16[1,1,16,512]{3,2,1,0:T(8,128)(2,1)}, bf16[1,1,16,512]{3,2,1,0:T(8,128)(2,1)S(1)}, u32[]{:S(2)}, u32[]{:S(2)}) collective-permute-start(bf16[1,1,16,512]{3,2,1,0:T(8,128)(2,1)} %get-tuple-element.226), channel_id=1, source_target_pairs={{1,0},{2,1},{3,2},{5,4},{6,5},{7,6},{9,8},{10,9},{11,10},{13,12},{... | collective-permute-start | bytes 49160 | tf_op jit(solution)/shard_map/ppermute | solution.py:33
  844.4 27.6 %collective-permute-start.8 = (bf16[1,1,16,512]{3,2,1,0:T(8,128)(2,1)}, bf16[1,1,16,512]{3,2,1,0:T(8,128)(2,1)S(1)}, u32[]{:S(2)}, u32[]{:S(2)}) collective-permute-start(bf16[1,1,16,512]{3,2,1,0:T(8,128)(2,1)} %get-tuple-element.223), channel_id=1, source_target_pairs={{0,1},{1,2},{2,3},{4,5},{5,6},{6,7},{8,9},{9,10},{10,11},{12,13},{... | collective-permute-start | bytes 49160 | tf_op jit(solution)/shard_map/ppermute | solution.py:31
  871.9 43.1 %copy-start.103 = (f32[1,512]{1,0:T(1,128)S(1)}, f32[1,512]{1,0:T(1,128)}, u32[]{:S(2)}) copy-start(f32[1,512]{1,0:T(1,128)} %get-tuple-element.170) | copy-start | bytes 6148
  1003.8 642.6 %copy-start.8 = (f32[1,5,73728]{2,0,1:T(1,128)S(1)}, f32[1,5,73728]{2,0,1:T(1,128)}, u32[]{:S(2)}) copy-start(f32[1,5,73728]{2,0,1:T(1,128)} %param.19) | copy-start | bytes 4423684
  1003.8 642.6 %copy-start.33 = (f32[1,5,73728]{2,0,1:T(1,128)S(1)}, f32[1,5,73728]{2,0,1:T(1,128)}, u32[]{:S(2)}) copy-start(f32[1,5,73728]{2,0,1:T(1,128)} %param.20) | copy-start | bytes 4423684
  1004.0 4.2 collective-permute-start.10
  1005.9 5.4 collective-permute-start.11
  (91 other events, 1000.8 us)
Sparse Core Ops, SparseCore 0:
  11.6 221.1 all-gather.1
  843.1 132.8 all-reduce.57
  990.0 656.3 reduce-scatter.1
where the time goes:
time: 1690 us; the launch traced here: 1670 us
  waiting for transfers between devices  786 us (47%)
  blocking collectives  377 us (22%)
  local copies, waits for them, and re-layouts  305 us (18%)
  other arithmetic  91 us (5%)
  matrix products  64.1 us (4%)
  starting transfers between devices  24.2 us (1%)
  between operations  20.3 us (1%)
    reduce_scatter x1, waiting for transfers between devices, local(): lax.psum_scatter(owner_pieces(kernel_grads, device_count), ('batch', 'row...  633 us
    psum x4, blocking collectives, norm_forward(): lax.psum((jnp.sum(masked, axis=(1, 2, 3)), jnp.sum(masked * values, axis=...  166 us
    psum x4, blocking collectives, norm_backward(): lax.psum((jnp.sum(masked * normed, axis=(1, 2, 3)), jnp.sum(masked, axis=...  163 us
    all_gather x1, waiting for transfers between devices, local(): lax.all_gather(kernels.astype(jnp.bfloat16), ('batch', 'rows'), axis=0, t...  149 us
    concatenate x4, local copies, waits for them, and re-layouts, local(): jnp.concatenate([first_kernel_grad.reshape(1, -1), second_kernel_grad.res...  110 us
    slice x3, local copies, waits for them, and re-layouts, local(): kernel_all[2:]  52.2 us
    all_gather x1, blocking collectives, local(): lax.all_gather(attention.astype(jnp.bfloat16), ('batch', 'rows'), axis=0,...  48.6 us
    slice x1, local copies, waits for them, and re-layouts, local(): kernel_all[0:1]  47.3 us
  transfers between devices with their start and end apart: 15, of which 5 were waited for; matrix products, arithmetic and copies ran while one was open for 16% of the time, Pallas kernels for 0%

commit v1 on v0

--- a/solution.py
+++ b/solution.py
@@ -1,6 +1,10 @@
+import functools
+
 import jax
 import jax.numpy as jnp
 from jax import lax
+from jax.experimental import pallas as pl
+from jax.experimental.pallas import tpu as pltpu
 from jax.sharding import PartitionSpec as P
 
 C = 512
@@ -423,9 +427,856 @@
     )
 
 
+AXES = ("batch", "rows")
+BF = jnp.bfloat16
+F32 = jnp.float32
+BAND = 8
+WID = 16
+PIX = BAND * WID
+EXT = PIX + 2 * WID
+PAIR = 2
+TOP = 16
+VMEM_LIMIT = 56 * 1024 * 1024
+GELU_A = 0.7978845608028654
+GELU_B = 0.044715
+DOWN_AT = 2 * C
+UP_AT = DOWN_AT + TASK_COUNT * B
+CONV_AT = UP_AT + TASK_COUNT * C
+HIDDEN = TASK_COUNT * B
+M_ROWS, M_GROUP, M_BAND, M_TOP, M_TOTAL, M_DEV = 0, 2, 4, 5, 6, 7
+
+
+def swap(value, mask):
+    count = lax.axis_size("batch") * lax.axis_size("rows")
+    return lax.ppermute(value, AXES, [(i, i ^ mask) for i in range(count)])
+
+
+def kernel_call(body, out_shapes, args, places, scratch=(), flops=0, name=None):
+    moved = sum(a.size * a.dtype.itemsize for a in args) + sum(
+        o.size * o.dtype.itemsize for o in out_shapes
+    )
+    space = {"s": pltpu.SMEM, "v": pltpu.VMEM, "a": pl.ANY}
+    return pl.pallas_call(
+        body,
+        out_shape=out_shapes,
+        in_specs=[pl.BlockSpec(memory_space=space[p]) for p in places],
+        out_specs=[pl.BlockSpec(memory_space=pltpu.VMEM) for _ in out_shapes],
+        scratch_shapes=list(scratch),
+        compiler_params=pltpu.CompilerParams(vmem_limit_bytes=VMEM_LIMIT),
+        cost_estimate=pl.CostEstimate(flops=flops, bytes_accessed=moved, transcendentals=0),
+        name=name,
+    )(*args)
+
+
+def sds(shape, dtype=F32):
+    return jax.ShapeDtypeStruct(shape, dtype)
+
+
+def gelu(x):
+    t = jnp.tanh(GELU_A * (x + GELU_B * x * x * x))
+    return 0.5 * x * (1.0 + t)
+
+
+def gelu_slope(x):
+    square = x * x
+    t = jnp.tanh(GELU_A * (x + GELU_B * x * square))
+    return 0.5 * (1.0 + t) + 0.5 * x * (1.0 - t * t) * (GELU_A * (1.0 + 3.0 * GELU_B * square))
+
+
+def total_of(meta):
+    return meta[M_TOTAL].astype(F32) * float(WID)
+
+
+def pixel_ids(count, width=C):
+    return lax.broadcasted_iota(jnp.int32, (count, width), 0)
+
+
+def own_mask(meta, slot, width=C):
+    return (pixel_ids(PIX, width) < meta[M_ROWS + slot] * WID).astype(F32)
+
+
+def inner_mask(meta, slot, width=C):
+    ids = pixel_ids(EXT, width)
+    return ((ids >= WID) & (ids < WID + meta[M_ROWS + slot] * WID)).astype(F32)
+
+
+def outer_mask(meta, slot, width=C):
+    ids = pixel_ids(EXT, width)
+    low = jnp.where(meta[M_BAND] > 0, 0, WID)
+    high = WID * (meta[M_ROWS + slot] + jnp.where(meta[M_BAND] < 3, 2, 1))
+    return ((ids >= low) & (ids < high)).astype(F32)
+
+
+def norm_terms(stats, row, start, width, affine, at, total):
+    mean = stats[row : row + 1, start : start + width] / total
+    spread = stats[row + 1 : row + 2, start : start + width] / total - mean * mean
+    inverse = lax.rsqrt(spread + NORM_EPS)
+    gain = affine[0:1, at : at + width]
+    bias = affine[1:2, at : at + width]
+    return mean, inverse, gain, bias
+
+
+def rims(meta, first, second):
+    band = meta[M_BAND]
+    odd = (band % 2) == 1
+    up = jnp.where(odd, first, second)
+    down = jnp.where(odd, second, first)
+    return (
+        jnp.where(band > 0, up, jnp.zeros_like(up)),
+        jnp.where(band < 3, down, jnp.zeros_like(down)),
+    )
+
+
+def put_ext(meta, ext, slot, own, up, down):
+    base = slot * EXT
+    ext[base : base + WID] = up[slot * WID : (slot + 1) * WID]
+    ext[base + WID : base + WID + PIX] = own
+    ext[base + WID + PIX : base + EXT] = jnp.zeros_like(ext[0:WID])
+    at = pl.multiple_of(base + WID + meta[M_ROWS + slot] * WID, WID)
+    ext[pl.ds(at, WID)] = down[slot * WID : (slot + 1) * WID]
+
+
+def put_edges(meta, ref, first, second):
+    odd = (meta[M_BAND] % 2) == 1
+    for slot in range(PAIR):
+        last = PIX * slot + WID * (meta[M_ROWS + slot] - 1)
+        head = PIX * slot
+        at = pl.multiple_of(jnp.where(odd, head, last), WID)
+        first[slot * WID : (slot + 1) * WID] = ref[pl.ds(at, WID)]
+        at = pl.multiple_of(jnp.where(odd, last, head), WID)
+        second[slot * WID : (slot + 1) * WID] = ref[pl.ds(at, WID)]
+
+
+def column_versions(meta, slot, value):
+    column = pixel_ids(EXT) & (WID - 1)
+    halves = meta[M_GROUP + slot] == 1
+    cut = jnp.where(halves, WID // 2, 0)
+    left = jnp.where((column == 0) | (column == cut), 0.0, pltpu.roll(value, 1, 0))
+    cut = jnp.where(halves, WID // 2 - 1, WID - 1)
+    right = jnp.where(
+        (column == WID - 1) | (column == cut), 0.0, pltpu.roll(value, EXT - 1, 0)
+    )
+    return left.astype(BF), value.astype(BF), right.astype(BF)
+
+
+def weights_wait(kernel, sem):
+    pltpu.make_async_copy(kernel, kernel, sem).wait()
+
+
+def weights_start(meta, pieces, kernel, sem, block):
+    half = C // 2
+    masks = {
+        "A": [x * 4 + a * 8 + b * 16 for x in range(2) for a in range(2) for b in range(2)],
+        "B": [y * 2 + a * 8 + b * 16 for y in range(2) for a in range(2) for b in range(2)],
+    }
+    plan = [("A", 0), ("A", 2), ("A", 1), ("A", 3), ("B", 0), ("B", 4), ("B", 1), ("B", 5)]
+    for ref, (part, extra) in zip(pieces, plan):
+        for i, mask in enumerate(masks[part]):
+            row = pl.multiple_of((meta[M_DEV] ^ (mask ^ extra)) * block, 16)
+            lane = 0 if part == "A" else half
+            pltpu.make_async_copy(
+                ref.at[i, pl.ds(0, block)],
+                kernel.at[pl.ds(row, block), pl.ds(lane, half)],
+                sem,
+            ).start()
+
+
+def conv_body(block, meta, ext, *rest):
+    pieces, (out, stats, edge1, edge2), (kernel, patch, sem) = rest[:8], rest[8:12], rest[12:]
+    weights_start(meta, pieces, kernel, sem, block)
+    for slot in range(PAIR):
+        value = ext[slot * EXT : (slot + 1) * EXT].astype(F32)
+        versions = column_versions(meta, slot, value)
+        for tap in range(9):
+            start = WID * (tap // 3)
+            patch[slot * PIX : (slot + 1) * PIX, tap * C : (tap + 1) * C] = versions[tap % 3][
+                start : start + PIX
+            ]
+    weights_wait(kernel, sem)
+    out[...] = jnp.dot(patch[...], kernel[...], preferred_element_type=F32)
+    first, second = 0.0, 0.0
+    for slot in range(PAIR):
+        value = out[slot * PIX : (slot + 1) * PIX]
+        masked = value * own_mask(meta, slot)
+        first = first + jnp.sum(masked, axis=0, keepdims=True)
+        second = second + jnp.sum(masked * value, axis=0, keepdims=True)
+    stats[...] = jnp.zeros_like(stats)
+    stats[0:1] = first
+    stats[1:2] = second
+    put_edges(meta, out, edge1, edge2)
+
+
+def dgrad_body(block, meta, ext, *rest):
+    pieces, out, (kernel, sem) = rest[:8], rest[8], rest[9:]
+    weights_start(meta, pieces, kernel, sem, block)
+    versions = []
+    for slot in range(PAIR):
+        value = ext[slot * EXT : (slot + 1) * EXT].astype(F32)
+        versions.append(column_versions(meta, slot, value))
+    weights_wait(kernel, sem)
+    for tap in range(9):
+        start = WID * (2 - tap // 3)
+        piece = jnp.concatenate(
+            [versions[slot][2 - tap % 3][start : start + PIX] for slot in range(PAIR)], axis=0
+        )
+        part = lax.dot_general(
+            piece,
+            kernel[tap * C : (tap + 1) * C],
+            (((1,), (1,)), ((), ())),
+            preferred_element_type=F32,
+        )
+        if tap == 0:
+            out[...] = part
+        else:
+            out[...] += part
+
+
+def wgrad_body(block, meta, ext, grad, keep, send, patch, result):
+    core = meta[M_DEV] % 2
+    low = jnp.concatenate(
+        [
+            grad[slot * EXT + WID : slot * EXT + WID + PIX] * own_mask(meta, slot).astype(BF)
+            for slot in range(PAIR)
+        ],
+        axis=0,
+    )
+    rows = 16 * block
+
+    def half(top):
+        first_tap = (top * rows) // C
+        for slot in range(PAIR):
+            value = ext[slot * EXT : (slot + 1) * EXT].astype(F32)
+            versions = column_versions(meta, slot, value)
+            for i in range(5):
+                tap = first_tap + i
+                start = WID * (tap // 3)
+                patch[slot * PIX : (slot + 1) * PIX, i * C : (i + 1) * C] = versions[tap % 3][
+                    start : start + PIX
+                ]
+        lane = top * rows - first_tap * C
+        result[...] = lax.dot_general(
+            patch[:, lane : lane + rows], low, (((0,), (0,)), ((), ())), preferred_element_type=F32
+        )
+
+    for top in range(2):
+        pl.when(meta[M_TOP] == top)(functools.partial(half, top))
+    for j in range(8):
+        y, x, a = j & 1, (j >> 1) & 1, (j >> 2) & 1
+        place = x * 4 + y * 2 + a
+        at = pl.multiple_of((2 * j + core) * block, 16)
+        keep[place] = result[pl.ds(at, block)]
+        at = pl.multiple_of((2 * j + 1 - core) * block, 16)
+        send[place] = result[pl.ds(at, block)]
+
+
+def squeeze_body(meta, z1, s1, rec1, rec2, affine, down, a1, hidden, stats, ext):
+    total = total_of(meta)
+    mean, inverse, gain, bias = norm_terms(s1, 0, 0, C, affine, 0, total)
+
+    def act(z):
+        return gelu((z - mean) * inverse * gain + bias)
+
+    up, dn = rims(meta, rec1[...], rec2[...])
+    up, dn = act(up), act(dn)
+    for slot in range(PAIR):
+        own = act(z1[slot * PIX : (slot + 1) * PIX])
+        put_ext(meta, ext, slot, own, up, dn)
+        at = slice(slot * EXT, (slot + 1) * EXT)
+        a1[at] = (ext[at] * outer_mask(meta, slot)).astype(BF)
+    hidden[...] = jnp.dot(a1[...], down[...], preferred_element_type=F32)
+    first, second = 0.0, 0.0
+    for slot in range(PAIR):
+        value = hidden[slot * EXT : (slot + 1) * EXT]
+        masked = value * inner_mask(meta, slot, HIDDEN)
+        first = first + jnp.sum(masked, axis=0, keepdims=True)
+        second = second + jnp.sum(masked * value, axis=0, keepdims=True)
+    stats[...] = jnp.zeros_like(stats)
+    stats[0:1, 0:HIDDEN] = first
+    stats[1:2, 0:HIDDEN] = second
+
+
+def expand_body(meta, hidden, hstats, affine, up_w, squeezed, expanded, stats):
+    total = total_of(meta)
+    mean, inverse, gain, bias = norm_terms(hstats, 0, 0, HIDDEN, affine, DOWN_AT, total)
+    for slot in range(PAIR):
+        at = slice(slot * EXT, (slot + 1) * EXT)
+        value = gelu((hidden[at] - mean) * inverse * gain + bias)
+        squeezed[at] = (value * outer_mask(meta, slot, HIDDEN)).astype(BF)
+    stats[...] = jnp.zeros_like(stats)
+    for task in range(TASK_COUNT):
+        part = jnp.dot(
+            squeezed[:, task * B : (task + 1) * B], up_w[task], preferred_element_type=F32
+        )
+        expanded[task] = part
+        first, second = 0.0, 0.0
+        for slot in range(PAIR):
+            value = expanded[task, slot * EXT : (slot + 1) * EXT]
+            masked = value * inner_mask(meta, slot)
+            first = first + jnp.sum(masked, axis=0, keepdims=True)
+            second = second + jnp.sum(masked * value, axis=0, keepdims=True)
+        stats[2 + 2 * task : 3 + 2 * task] = first
+        stats[3 + 2 * task : 4 + 2 * task] = second
+
+
+def select_body(meta, z2, rec1, rec2, stats, expanded, affine, sel0, sel1, sel2, ext):
+    total = total_of(meta)
+    mean, inverse, gain, bias = norm_terms(stats, 0, 0, C, affine, C, total)
+
+    def act(z):
+        return gelu((z - mean) * inverse * gain + bias)
+
+    up, dn = rims(meta, rec1[...], rec2[...])
+    up, dn = act(up), act(dn)
+    for slot in range(PAIR):
+        put_ext(meta, ext, slot, act(z2[slot * PIX : (slot + 1) * PIX]), up, dn)
+    for task, sel in enumerate((sel0, sel1, sel2)):
+        terms = norm_terms(stats, 2 + 2 * task, 0, C, affine, UP_AT + task * C, total)
+        mean_u, inverse_u, gain_u, bias_u = terms
+        for slot in range(PAIR):
+            at = slice(slot * EXT, (slot + 1) * EXT)
+            pre = (expanded[task, at] - mean_u) * inverse_u * gain_u + bias_u
+            gate = jax.nn.sigmoid(pre)
+            sel[at] = (gate * (ext[at] * outer_mask(meta, slot))).astype(BF)
+
+
+def spread_matrix(rows_out, first_row, cells):
+    pixel = lax.broadcasted_iota(jnp.int32, (rows_out, cells), 0)
+    cell = lax.broadcasted_iota(jnp.int32, (rows_out, cells), 1)
+    row = (pixel >> 4) + first_row
+    column = pixel & (WID - 1)
+    want = ((row + 1) >> 1) * (WID // 2) + (column >> 1)
+    return (cell == want).astype(BF)
+
+
+def pool_body(meta, lam, z30, z31, z32, stats, cot, affine, pooled, back):
+    total = total_of(meta)
+    cells = cot.shape[2]
+    spread = spread_matrix(PIX, 1, cells)
+    pixel = lax.broadcasted_iota(jnp.int32, (BAND * WID // 4, PIX), 1)
+    cell = lax.broadcasted_iota(jnp.int32, (BAND * WID // 4, PIX), 0)
+    owner = (pixel >> 5) * (WID // 2) + ((pixel & (WID - 1)) >> 1)
+    gather = jnp.where(owner == cell, 0.25, 0.0).astype(F32)
+    back[...] = jnp.zeros_like(back)
+    for task, z3 in enumerate((z30, z31, z32)):
+        mean, inverse, gain, bias = norm_terms(
+            stats, 2 * task, 0, C, affine, CONV_AT + task * C, total
+        )
+        first, second = 0.0, 0.0
+        for slot in range(PAIR):
+            normed = (z3[slot * PIX : (slot + 1) * PIX] - mean) * inverse
+            pre = normed * gain + bias
+            mask = own_mask(meta, slot)
+            square = pre * pre
+            t = jnp.tanh(GELU_A * (pre + GELU_B * pre * square))
+            slope = 0.5 * (1.0 + t) + 0.5 * pre * (1.0 - t * t) * (
+                GELU_A * (1.0 + 3.0 * GELU_B * square)
+            )
+            active = 0.5 * pre * (1.0 + t) * mask
+
+            def store(active=active, task=task):
+                pooled[task] = jnp.dot(
+                    gather, active, preferred_element_type=F32, precision=lax.Precision.HIGHEST
+                )
+
+            pl.when(meta[M_TOP] == slot)(store)
+            seed = jnp.dot(spread, cot[task, slot], preferred_element_type=F32)
+            grad = slope * (seed * (lam[task] * 0.25)) * mask
+            first = first + jnp.sum(grad * normed, axis=0, keepdims=True)
+            second = second + jnp.sum(grad, axis=0, keepdims=True)
+        back[2 * task : 2 * task + 1] = first
+        back[2 * task + 1 : 2 * task + 2] = second
+
+
+def task_grad_body(
+    meta, lam, z30, z31, z32, rec1, rec2, stats, back, cot, affine, out0, out1, out2, ext
+):
+    total = total_of(meta)
+    spread = spread_matrix(EXT, 0, cot.shape[2])
+    for task, (z3, out) in enumerate(((z30, out0), (z31, out1), (z32, out2))):
+        mean, inverse, gain, bias = norm_terms(
+            stats, 2 * task, 0, C, affine, CONV_AT + task * C, total
+        )
+        dgain, dbias = back[2 * task : 2 * task + 1], back[2 * task + 1 : 2 * task + 2]
+        at = slice(task * PAIR * WID, (task + 1) * PAIR * WID)
+        up, dn = rims(meta, rec1[at], rec2[at])
+        for slot in range(PAIR):
+            put_ext(meta, ext, slot, z3[slot * PIX : (slot + 1) * PIX], up, dn)
+            at = slice(slot * EXT, (slot + 1) * EXT)
+            normed = (ext[at] - mean) * inverse
+            slope = gelu_slope(normed * gain + bias)
+            seed = jnp.dot(spread, cot[task, slot], preferred_element_type=F32)
+            grad = slope * (seed * (lam[task] * 0.25))
+            value = (gain * inverse) * (grad - (dbias + normed * dgain) / total)
+            out[at] = jnp.where(outer_mask(meta, slot) > 0, value, 0.0).astype(BF)
+
+
+def branch_grad_body(
+    meta, ds0, ds1, ds2, expanded, z2, stats, affine, dpu, dp2, back, edge1, edge2
+):
+    total = total_of(meta)
+    mean, inverse, gain, bias = norm_terms(stats, 0, 0, C, affine, C, total)
+    terms = [
+        norm_terms(stats, 2 + 2 * task, 0, C, affine, UP_AT + task * C, total)
+        for task in range(TASK_COUNT)
+    ]
+    sums = [0.0] * 8
+    for slot in range(PAIR):
+        own = slice(slot * PIX, (slot + 1) * PIX)
+        inner = slice(slot * EXT + WID, slot * EXT + WID + PIX)
+        mask = own_mask(meta, slot)
+        normed2 = (z2[own] - mean) * inverse
+        pre2 = normed2 * gain + bias
+        feature = gelu(pre2) * mask
+        dfeature = 0.0
+        for task, ds in enumerate((ds0, ds1, ds2)):
+            mean_u, inverse_u, gain_u, bias_u = terms[task]
+            normed = (expanded[task, inner] - mean_u) * inverse_u
+            gate = jax.nn.sigmoid(normed * gain_u + bias_u)
+            grad = ds[own] * mask
+            dfeature = dfeature + grad * gate
+            value = grad * feature * gate * (1.0 - gate)
+            dpu[task, own] = value
+            sums[2 + 2 * task] += jnp.sum(value * normed, axis=0, keepdims=True)
+            sums[3 + 2 * task] += jnp.sum(value, axis=0, keepdims=True)
+        value = gelu_slope(pre2) * dfeature
+        dp2[own] = value
+        sums[0] += jnp.sum(value * normed2, axis=0, keepdims=True)
+        sums[1] += jnp.sum(value, axis=0, keepdims=True)
+    for i in range(8):
+        back[i : i + 1] = sums[i]
+    put_edges(meta, dp2, edge1, edge2)
+
+
+def expand_grad_body(
+    meta, dpu, expanded, stats, back, squeezed, hidden, hstats, up_w, affine, dup, dph, hback
+):
+    total = total_of(meta)
+    hback[...] = jnp.zeros_like(hback)
+    for task in range(TASK_COUNT):
+        mean, inverse, gain, _ = norm_terms(
+            stats, 2 + 2 * task, 0, C, affine, UP_AT + task * C, total
+        )
+        dgain, dbias = back[2 + 2 * task : 3 + 2 * task], back[3 + 2 * task : 4 + 2 * task]
+        grads, acts = [], []
+        for slot in range(PAIR):
+            own = slice(slot * PIX, (slot + 1) * PIX)
+            inner = slice(slot * EXT + WID, slot * EXT + WID + PIX)
+            normed = (expanded[task, inner] - mean) * inverse
+            value = (gain * inverse) * (dpu[task, own] - (dbias + normed * dgain) / total)
+            grads.append((value * own_mask(meta, slot)).astype(BF))
+            acts.append(squeezed[inner, task * B : (task + 1) * B])
+        grad = jnp.concatenate(grads, axis=0)
+        dup[task] = lax.dot_general(
+            jnp.concatenate(acts, axis=0),
+            grad,
+            (((0,), (0,)), ((), ())),
+            preferred_element_type=F32,
+        )
+        dsq = lax.dot_general(
+            grad, up_w[task], (((1,), (1,)), ((), ())), preferred_element_type=F32
+        )
+        mean, inverse, gain, bias = norm_terms(
+            hstats, 0, task * B, B, affine, DOWN_AT + task * B, total
+        )
+        first, second = 0.0, 0.0
+        for slot in range(PAIR):
+            own = slice(slot * PIX, (slot + 1) * PIX)
+            inner = slice(slot * EXT + WID, slot * EXT + WID + PIX)
+            normed = (hidden[inner, task * B : (task + 1) * B] - mean) * inverse
+            value = gelu_slope(normed * gain + bias) * dsq[own] * own_mask(meta, slot, B)
+            dph[own, task * B : (task + 1) * B] = value
+            first = first + jnp.sum(value * normed, axis=0, keepdims=True)
+            second = second + jnp.sum(value, axis=0, keepdims=True)
+        hback[0:1, task * B : (task + 1) * B] = first
+        hback[1:2, task * B : (task + 1) * B] = second
+
+
+def norm_grad_body(
+    at_channel, meta, grad, grec1, grec2, z, zrec1, zrec2, stats, back, affine, out, gext, zext
+):
+    total = total_of(meta)
+    mean, inverse, gain, _ = norm_terms(stats, 0, 0, C, affine, at_channel, total)
+    dgain, dbias = back[0:1], back[1:2]
+    gup, gdn = rims(meta, grec1[...], grec2[...])
+    zup, zdn = rims(meta, zrec1[...], zrec2[...])
+    for slot in range(PAIR):
+        own = slice(slot * PIX, (slot + 1) * PIX)
+        put_ext(meta, gext, slot, grad[own], gup, gdn)
+        put_ext(meta, zext, slot, z[own], zup, zdn)
+        at = slice(slot * EXT, (slot + 1) * EXT)
+        normed = (zext[at] - mean) * inverse
+        value = (gain * inverse) * (gext[at] - (dbias + normed * dgain) / total)
+        out[at] = jnp.where(outer_mask(meta, slot) > 0, value, 0.0).astype(BF)
+
+
+def squeeze_grad_body(
+    meta, dph, hidden, hstats, hback, down, a1, da1, z1, s1, affine, dp1, back, edge1, edge2, ddown
+):
+    total = total_of(meta)
+    mean, inverse, gain, _ = norm_terms(hstats, 0, 0, HIDDEN, affine, DOWN_AT, total)
+    dgain, dbias = hback[0:1, 0:HIDDEN], hback[1:2, 0:HIDDEN]
+    grads, acts = [], []
+    for slot in range(PAIR):
+        own = slice(slot * PIX, (slot + 1) * PIX)
+        inner = slice(slot * EXT + WID, slot * EXT + WID + PIX)
+        normed = (hidden[inner] - mean) * inverse
+        value = (gain * inverse) * (dph[own] - (dbias + normed * dgain) / total)
+        grads.append((value * own_mask(meta, slot, HIDDEN)).astype(BF))
+        acts.append(a1[inner])
+    grad = jnp.concatenate(grads, axis=0)
+    act = jnp.concatenate(acts, axis=0)
+    ddown[...] = lax.dot_general(
+        act, grad, (((0,), (0,)), ((), ())), preferred_element_type=F32
+    )
+    extra = lax.dot_general(grad, down[...], (((1,), (1,)), ((), ())), preferred_element_type=F32)
+    mean, inverse, gain, bias = norm_terms(s1, 0, 0, C, affine, 0, total)
+    first, second = 0.0, 0.0
+    for slot in range(PAIR):
+        own = slice(slot * PIX, (slot + 1) * PIX)
+        normed = (z1[own] - mean) * inverse
+        value = gelu_slope(normed * gain + bias) * (da1[own] + extra[own]) * own_mask(meta, slot)
+        dp1[own] = value
+        first = first + jnp.sum(value * normed, axis=0, keepdims=True)
+        second = second + jnp.sum(value, axis=0, keepdims=True)
+    back[...] = jnp.zeros_like(back)
+    back[0:1] = first
+    back[1:2] = second
+    put_edges(meta, dp1, edge1, edge2)
+
+
+CONV_FLOPS = 2 * PAIR * PIX * 9 * C * C
+
+
+def conv_call(meta, ext, pieces, block):
+    shapes = [sds((PAIR * PIX, C)), sds((8, C)), sds((PAIR * WID, C)), sds((PAIR * WID, C))]
+    scratch = [
+        pltpu.VMEM((9 * C, C), BF),
+        pltpu.VMEM((PAIR * PIX, 9 * C), BF),
+        pltpu.SemaphoreType.DMA,
+    ]
+    return kernel_call(
+        functools.partial(conv_body, block), shapes, (meta, ext) + tuple(pieces),
+        "sv" + "a" * 8, scratch, CONV_FLOPS, "conv",
+    )
+
+
+def dgrad_call(meta, ext, pieces, block):
+    scratch = [pltpu.VMEM((9 * C, C), BF), pltpu.SemaphoreType.DMA]
+    return kernel_call(
+        functools.partial(dgrad_body, block), [sds((PAIR * PIX, C))],
+        (meta, ext) + tuple(pieces), "sv" + "a" * 8, scratch, CONV_FLOPS, "dgrad",
+    )[0]
+
+
+def wgrad_call(meta, ext, grad, block):
+    scratch = [pltpu.VMEM((PAIR * PIX, 5 * C), BF), pltpu.VMEM((16 * block, C), F32)]
+    return kernel_call(
+        functools.partial(wgrad_body, block), [sds((8, block, C)), sds((8, block, C))],
+        (meta, ext, grad), "svv", scratch, CONV_FLOPS // 2, "wgrad",
+    )
+
+
+def sync(stats, edge1=None, edge2=None):
+    rows = stats.shape[0]
+    if edge1 is None:
+        stats = stats + swap(stats, 1)
+        stats = stats + swap(stats, 3)
+        first = second = None
+    else:
+        got = swap(jnp.concatenate([stats, edge1], axis=0), 1)
+        stats, first = stats + got[:rows], got[rows:]
+        got = swap(jnp.concatenate([stats, edge2], axis=0), 3)
+        stats, second = stats + got[:rows], got[rows:]
+    stats = stats + swap(stats, 4)
+    stats = stats + swap(stats, 8)
+    return stats, first, second
+
+
+def gather_pieces(shard):
+    half = C // 2
+    two = jnp.stack([shard, swap(shard, 16)])
+    four = jnp.concatenate([two, swap(two, 8)])
+    left, right = four[:, :, :half], four[:, :, half:]
+    left8 = jnp.concatenate([left, swap(left, 4)])
+    right8 = jnp.concatenate([right, swap(right, 2)])
+    left_far, right_far = swap(left8, 2), swap(right8, 4)
+    return (
+        left8, left_far, swap(left8, 1), swap(left_far, 1),
+        right8, right_far, swap(right8, 1), swap(right_far, 1),
+    )
+
+
+def attention_rows(pieces, block, me):
+    tails = [p[:, block:] for p in pieces]
+    left = jnp.concatenate(tails[:4])
+    right = jnp.concatenate(tails[4:])
+    base_a = [x * 4 + a * 8 + b * 16 for x in range(2) for a in range(2) for b in range(2)]
+    base_b = [y * 2 + a * 8 + b * 16 for y in range(2) for a in range(2) for b in range(2)]
+    order_a = [m ^ e for e in (0, 2, 1, 3) for m in base_a]
+    order_b = [m ^ e for e in (0, 4, 1, 5) for m in base_b]
+    spot_a = [order_a.index(m) for m in range(32)]
+    spot_b = [order_b.index(m) for m in range(32)]
+    owners = me ^ jnp.arange(32)
+    left = jnp.take(left, jnp.array(spot_a)[owners], axis=0)
+    right = jnp.take(right, jnp.array(spot_b)[owners], axis=0)
+    return jnp.concatenate([left, right], axis=-1)
+
+
+def pick(value, index):
+    return lax.dynamic_index_in_dim(value, index, 0, keepdims=False)
+
+
+def scatter_sum(keep, send, bits, x_first):
+    total = keep + swap(send, 1)
+    x, y, a = bits
+    rows = total.shape[1:]
+    if x_first:
+        total = total.reshape((2, 4) + rows)
+        total = pick(total, x) + swap(pick(total, 1 - x).astype(BF), 4).astype(F32)
+        total = total.reshape((2, 2) + rows)
+        total = pick(total, y) + swap(pick(total, 1 - y).astype(BF), 2).astype(F32)
+    else:
+        total = total.reshape((2, 2, 2) + rows)
+        total = lax.dynamic_index_in_dim(total, y, 1, keepdims=False) + swap(
+            lax.dynamic_index_in_dim(total, 1 - y, 1, keepdims=False).astype(BF), 2
+        ).astype(F32)
+        total = pick(total, x) + swap(pick(total, 1 - x).astype(BF), 4).astype(F32)
+    return pick(total, a) + swap(pick(total, 1 - a).astype(BF), 8).astype(F32)
+
+
+def order_pair(own, other, top):
+    return jnp.where(
+        top == 0, jnp.concatenate([own, other]), jnp.concatenate([other, own])
+    )
+
+
+def image_ext(images, rows, band):
+    valid = (jnp.arange(BAND) < rows).astype(BF)[:, None, None]
+    own = images[0] * valid
+    last = lax.dynamic_index_in_dim(own, rows - 1, 0, keepdims=False)
+    odd = band % 2 == 1
+    first = swap(jnp.where(odd, own[0], last), 1)
+    second = swap(jnp.where(odd, last, own[0]), 3)
+    up = jnp.where(band > 0, jnp.where(odd, first, second), 0)
+    down = jnp.where(band < 3, jnp.where(odd, second, first), 0)
+    ext = jnp.concatenate([up[None], own, jnp.zeros_like(up)[None]])
+    ext = lax.dynamic_update_index_in_dim(ext, down, rows + 1, 0)
+    return ext.reshape(EXT, C)
+
+
+def cotangent_ext(cotangent, rows, band):
+    own = cotangent[:, 0]
+    last = lax.dynamic_index_in_dim(own, rows // 2 - 1, 1, keepdims=False)
+    odd = band % 2 == 1
+    first = swap(jnp.where(odd, own[:, 0], last), 1)
+    second = swap(jnp.where(odd, last, own[:, 0]), 3)
+    up = jnp.where(odd, first, second)
+    down = jnp.where(odd, second, first)
+    ext = jnp.concatenate([up[:, None], own, jnp.zeros_like(up)[:, None]], axis=1)
+    ext = lax.dynamic_update_index_in_dim(ext, down, rows // 2 + 1, 1)
+    return ext.reshape(TASK_COUNT, -1, C)
+
+
+def local_pairs(
+    images,
+    heights,
+    groups,
+    ratios,
+    task_cotangent,
+    kernels,
+    moment_kernels,
+    square_kernels,
+    attention,
+    moment_attention,
+    square_attention,
+    affine,
+    moment_affine,
+    square_affine,
+):
+    slot = lax.axis_index("batch")
+    band = lax.axis_index("rows")
+    me = slot * 4 + band
+    top = slot // 4
+    low_slot = slot % 4
+    block = kernels.shape[2] // C
+    kernel_low = kernels[0].astype(BF).reshape(2 + TASK_COUNT, block, C)
+    attend_low = attention[0].astype(BF)
+    extra = attend_low.size // C
+    rows_pair = jnp.stack([heights[low_slot], heights[low_slot + 4]]) // 4
+    group_pair = jnp.stack([groups[low_slot], groups[low_slot + 4]])
+    meta = jnp.concatenate(
+        [rows_pair, group_pair, jnp.stack([band, top, jnp.sum(heights), me])]
+    ).astype(jnp.int32)
+    lam = TASK_COUNT * jax.nn.softmax(ratios / SOFTMAX_TEMP)
+    own_rows = heights[slot] // 4
+
+    own_ext = image_ext(images, own_rows, band)
+    x0 = order_pair(own_ext, swap(own_ext, TOP), top)
+    pieces = [gather_pieces(kernel_low[0])]
+    pieces.append(
+        gather_pieces(jnp.concatenate([kernel_low[1], attend_low.reshape(extra, C)], axis=0))
+    )
+    for k in range(2, 2 + TASK_COUNT):
+        pieces.append(gather_pieces(kernel_low[k]))
+    own_cot = cotangent_ext(task_cotangent, own_rows, band)
+    cot = jnp.moveaxis(order_pair(own_cot[None], swap(own_cot, TOP)[None], top), 0, 1)
+
+    z1, st, e1, e2 = conv_call(meta, x0, pieces[0], block)
+    s1, z1r1, z1r2 = sync(st, e1, e2)
+    tails = attention_rows(pieces[1], block, me)
+    kind_rows = extra // 2
+    down = tails[:, :kind_rows].reshape(TASK_COUNT, C, B).transpose(1, 0, 2).reshape(C, HIDDEN)
+    up_w = tails[:, kind_rows:].reshape(TASK_COUNT, B, C)
+    a1, hidden, hst = kernel_call(
+        squeeze_body,
+        [sds((PAIR * EXT, C), BF), sds((PAIR * EXT, HIDDEN)), sds((8, C))],
+        (meta, z1, s1, z1r1, z1r2, affine, down),
+        "svvvvvv",
+        [pltpu.VMEM((PAIR * EXT, C), F32)],
+        2 * PAIR * EXT * C * HIDDEN,
+        "squeeze",
+    )
+    hstats, _, _ = sync(hst)
+    z2, st2, e1, e2 = conv_call(meta, a1, pieces[1], block)
+    squeezed, expanded, ust = kernel_call(
+        expand_body,
+        [sds((PAIR * EXT, HIDDEN), BF), sds((TASK_COUNT, PAIR * EXT, C)), sds((8, C))],
+        (meta, hidden, hstats, affine, up_w),
+        "svvvv",
+        flops=2 * PAIR * EXT * C * HIDDEN,
+        name="expand",
+    )
+    s2, z2r1, z2r2 = sync(st2 + ust, e1, e2)
+    selected = kernel_call(
+        select_body,
+        [sds((PAIR * EXT, C), BF)] * TASK_COUNT,
+        (meta, z2, z2r1, z2r2, s2, expanded, affine),
+        "svvvvvv",
+        [pltpu.VMEM((PAIR * EXT, C), F32)],
+        name="select",
+    )
+    z3, st3, e31, e32 = zip(
+        *[conv_call(meta, selected[t], pieces[2 + t], block) for t in range(TASK_COUNT)]
+    )
+    s3, _, _ = sync(jnp.concatenate([s[:2] for s in st3] + [jnp.zeros((2, C), F32)]))
+    z3r1 = swap(jnp.concatenate(e31), 1)
+    z3r2 = swap(jnp.concatenate(e32), 3)
+    pooled, bst = kernel_call(
+        pool_body,
+        [sds((TASK_COUNT, PIX // 4, C)), sds((8, C))],
+        (meta, lam) + z3 + (s3, cot, affine),
+        "ssvvvvvv",
+        name="pool",
+    )
+    b3, _, _ = sync(bst)
+    dz3 = kernel_call(
+        task_grad_body,
+        [sds((PAIR * EXT, C), BF)] * TASK_COUNT,
+        (meta, lam) + z3 + (z3r1, z3r2, s3, b3, cot, affine),
+        "ssvvvvvvvvv",
+        [pltpu.VMEM((PAIR * EXT, C), F32)],
+        name="task_grad",
+    )
+    ds = [dgrad_call(meta, dz3[t], pieces[2 + t], block) for t in range(TASK_COUNT)]
+    dpu, dp2, bst, e1, e2 = kernel_call(
+        branch_grad_body,
+        [
+            sds((TASK_COUNT, PAIR * PIX, C)),
+            sds((PAIR * PIX, C)),
+            sds((8, C)),
+            sds((PAIR * WID, C)),
+            sds((PAIR * WID, C)),
+        ],
+        (meta,) + tuple(ds) + (expanded, z2, s2, affine),
+        "svvvvvvv",
+        name="branch_grad",
+    )
+    b2, dp2r1, dp2r2 = sync(bst, e1, e2)
+    dup, dph, hbst = kernel_call(
+        expand_grad_body,
+        [sds((TASK_COUNT, B, C)), sds((PAIR * PIX, HIDDEN)), sds((8, C))],
+        (meta, dpu, expanded, s2, b2, squeezed, hidden, hstats, up_w, affine),
+        "svvvvvvvvv",
+        flops=4 * PAIR * PIX * C * HIDDEN,
+        name="expand_grad",
+    )
+    hback, _, _ = sync(hbst)
+    ext_scratch = [pltpu.VMEM((PAIR * EXT, C), F32), pltpu.VMEM((PAIR * EXT, C), F32)]
+    dz2 = kernel_call(
+        functools.partial(norm_grad_body, C),
+        [sds((PAIR * EXT, C), BF)],
+        (meta, dp2, dp2r1, dp2r2, z2, z2r1, z2r2, s2, b2, affine),
+        "svvvvvvvvv",
+        ext_scratch,
+        name="norm_grad",
+    )[0]
+    da1 = dgrad_call(meta, dz2, pieces[1], block)
+    dp1, bst, e1, e2, ddown = kernel_call(
+        squeeze_grad_body,
+        [
+            sds((PAIR * PIX, C)),
+            sds((8, C)),
+            sds((PAIR * WID, C)),
+            sds((PAIR * WID, C)),
+            sds((C, HIDDEN)),
+        ],
+        (meta, dph, hidden, hstats, hback, down, a1, da1, z1, s1, affine),
+        "svvvvvvvvvv",
+        flops=4 * PAIR * PIX * C * HIDDEN,
+        name="squeeze_grad",
+    )
+    b1, dp1r1, dp1r2 = sync(bst, e1, e2)
+    dz1 = kernel_call(
+        functools.partial(norm_grad_body, 0),
+        [sds((PAIR * EXT, C), BF)],
+        (meta, dp1, dp1r1, dp1r2, z1, z1r1, z1r2, s1, b1, affine),
+        "svvvvvvvvv",
+        ext_scratch,
+        name="norm_grad",
+    )[0]
+    dx = dgrad_call(meta, dz1, pieces[0], block)
+    image_grad = lax.dynamic_slice_in_dim(dx, top * PIX, PIX, 0).reshape(1, BAND, WID, C)
+    valid = (jnp.arange(BAND) < own_rows).astype(F32)[None, :, None, None]
+    image_grad = image_grad * valid
+
+    bits = ((me >> 2) & 1, (me >> 1) & 1, (me >> 3) & 1)
+    inputs = (x0, a1) + tuple(selected)
+    grads = (dz1, dz2) + tuple(dz3)
+    shards = [None] * (2 + TASK_COUNT)
+    for k in (2, 3, 4, 1, 0):
+        keep, send = wgrad_call(meta, inputs[k], grads[k], block)
+        shards[k] = scatter_sum(keep, send, bits, k % 2 == 0)
+
+    ddown = ddown.reshape(C, TASK_COUNT, B).transpose(1, 0, 2)
+    attend = jnp.stack([ddown.reshape(-1), dup.reshape(-1)]).reshape(2, 2, 2, 2, 2, 2, -1)
+    attend = lax.dynamic_index_in_dim(attend, top, 1, keepdims=False)
+    attend = attend.transpose(2, 3, 1, 4, 0, 5).reshape(2, 2, 2, 2, -1, C)
+    attend = attend.reshape(8, 2, -1, C)
+    core = me & 1
+    keep = lax.dynamic_index_in_dim(attend, core, 1, keepdims=False)
+    send = lax.dynamic_index_in_dim(attend, 1 - core, 1, keepdims=False)
+    attend_shard = scatter_sum(keep, send, bits, True).reshape(1, 2, -1)
+
+    kernel_shard = jnp.stack(shards).reshape(1, 2 + TASK_COUNT, -1)
+    gain_grads = jnp.concatenate(
+        [b1[0], b2[0], hback[0, :HIDDEN], b2[2], b2[4], b2[6], b3[0], b3[2], b3[4]]
+    )
+    bias_grads = jnp.concatenate(
+        [b1[1], b2[1], hback[1, :HIDDEN], b2[3], b2[5], b2[7], b3[1], b3[3], b3[5]]
+    )
+    affine_grad = jnp.stack([gain_grads, bias_grads])
+    return (
+        (pooled.reshape(TASK_COUNT, 1, BAND // 2, WID // 2, C), image_grad)
+        + adamw(kernels, kernel_shard, moment_kernels, square_kernels, RATE_KERNEL)
+        + adamw(attention, attend_shard, moment_attention, square_attention, RATE_ATTEND)
+        + adamw(affine, affine_grad, moment_affine, square_affine, RATE_AFFINE)
+    )
+
+
 def solution(mesh):
+    paired = mesh.shape["batch"] == 8 and mesh.shape["rows"] == 4
     return jax.shard_map(
-        local,
+        local_pairs if paired else local,
         mesh=mesh,
         in_specs=(
             P("batch", "rows", None, None),

time: 1690 us -> 535 us (0.32); the launches traced: 1670 us -> 529 us
  waiting for transfers between devices: 786 us -> 179 us
  blocking collectives: 377 us -> 0 us
  local copies, waits for them, and re-layouts: 305 us -> 54.2 us
  Pallas kernels: 0 us -> 131 us
  matrix products: 64.1 us -> 0 us
  starting transfers between devices: 24.2 us -> 83.9 us
    reduce_scatter x1 -> x0, waiting for transfers between devices: 633 us -> none  [local(): lax.psum_scatter(owner_pieces(kernel_grads, device_count), ('batch', 'row...]
    psum x8 -> x0, blocking collectives: 329 us -> none  [the longest x4 166 us: norm_forward(): lax.psum((jnp.sum(masked, axis=(1, 2, 3)), jnp.sum(masked * values, axis=...]
    ppermute x12 -> x114, waiting for transfers between devices: 4.24 us -> 179 us  [swap(): return lax.ppermute(value, AXES, [(i, i ^ mask) for i in range(count)])]
    all_gather x1 -> x0, waiting for transfers between devices: 149 us -> none  [local(): lax.all_gather(kernels.astype(jnp.bfloat16), ('batch', 'rows'), axis=0, t...]
    pallas_call x0 -> x25, Pallas kernels: none -> 131 us  [kernel_call(): pl.pallas_call(body, out_shape=out_shapes, in_specs=[pl.BlockSpec(memory_...]
    slice x30 -> x31, local copies, waits for them, and re-layouts: 130 us -> 17 us  [the longest x4 4.38 us: local_pairs(): pieces.append(gather_pieces(kernel_low[k]))]
    concatenate x6 -> x7, local copies, waits for them, and re-layouts: 110 us -> 3.94 us  [the longest x1 2.6 us: local_pairs(): jnp.concatenate([rows_pair, group_pair, jnp.stack([band, top, jnp.sum(hei...]
    dot_general x15 -> x0, matrix products: 64.1 us -> none  [the longest x3 22.6 us: convolve_backward(): jnp.einsum('tshwk,tshwd->tkd', patches, grad_low, preferred_element_type=...]
  transfers between devices with their start and end apart: 15 -> 114, of which waited for: 5 -> 43; matrix products, arithmetic and copies ran while one was open for 16% -> 19% of each run, Pallas kernels for 0% -> 19%
where the time goes in v1:
time: 535 us; the launch traced here: 529 us
  waiting for transfers between devices  179 us (33%)
  Pallas kernels  131 us (24%)
  starting transfers between devices  83.9 us (16%)
  other arithmetic  75.8 us (14%)
  local copies, waits for them, and re-layouts  54.2 us (10%)
  between operations  5.63 us (1%)
    ppermute x114, waiting for transfers between devices, swap(): return lax.ppermute(value, AXES, [(i, i ^ mask) for i in range(count)])  179 us
    pallas_call x25, Pallas kernels, kernel_call(): pl.pallas_call(body, out_shape=out_shapes, in_specs=[pl.BlockSpec(memory_...  131 us
    ppermute x114, starting transfers between devices, swap(): return lax.ppermute(value, AXES, [(i, i ^ mask) for i in range(count)])  83.9 us
    sub x3, other arithmetic, adamw(): weights_in - step_rate * (moment_hat / (jnp.sqrt(square_hat) + ADAM_EPS)...  13.6 us
    add x6, other arithmetic, scatter_sum(): total = keep + swap(send, 1)  11.7 us
  transfers between devices with their start and end apart: 114, of which 43 were waited for; matrix products, arithmetic and copies ran while one was open for 19% of the time, Pallas kernels for 19%

profile of v1, /device:TPU:0, one launch (start us, length us, event | category | flops | bytes accessed | tf_op | source)
XLA Modules:
  0.0 529.3 jit_solution(17601291389947876933)
XLA Ops:
  11.3 4.1 slice_reduce_fusion
  32.1 7.4 %collective-permute-done.3 = bf16[144,512]{1,0:T(8,128)(2,1)S(1)} collective-permute-done((bf16[144,512]{1,0:T(8,128)(2,1)S(1)}, bf16[144,512]{1,0:T(8,128)(2,1)S(1)}, u32[]{:S(2)}, u32[]{:S(2)}) %collective-permute-start.3) | collective-permute-done | bytes 147488 | tf_op jit(solution)/shard_map/ppermute | solution.py:451
  39.5 10.3 %collective-permute-done.35 = bf16[144,512]{1,0:T(8,128)(2,1)S(1)} collective-permute-done((bf16[144,512]{1,0:T(8,128)(2,1)S(1)}, bf16[144,512]{1,0:T(8,128)(2,1)S(1)}, u32[]{:S(2)}, u32[]{:S(2)}) %collective-permute-start.35) | collective-permute-done | bytes 147488 | tf_op jit(solution)/shard_map/ppermute | solution.py:451
  49.9 3.2 collective-permute-done.45
  55.3 9.9 %collective-permute-done.4 = bf16[2,144,512]{2,1,0:T(8,128)(2,1)S(1)} collective-permute-done((bf16[2,144,512]{2,1,0:T(8,128)(2,1)S(1)}, bf16[2,144,512]{2,1,0:T(8,128)(2,1)S(1)}, u32[]{:S(2)}, u32[]{:S(2)}) %collective-permute-start.4) | collective-permute-done | bytes 294944 | tf_op jit(solution)/shard_map/ppermute | solution.py:451
  69.0 16.1 %collective-permute-done.18 = bf16[2,168,512]{2,1,0:T(8,128)(2,1)S(1)} collective-permute-done((bf16[2,168,512]{2,1,0:T(8,128)(2,1)S(1)}, bf16[2,168,512]{2,1,0:T(8,128)(2,1)S(1)}, u32[]{:S(2)}, u32[]{:S(2)}) %collective-permute-start.18) | collective-permute-done | bytes 344096 | tf_op jit(solution)/shard_map/ppermute | solution.py:451
  90.7 17.3 %collective-permute-done.23 = bf16[4,168,256]{2,1,0:T(8,128)(2,1)S(1)} collective-permute-done((bf16[4,168,256]{2,1,0:T(8,128)(2,1)S(1)}, bf16[4,168,256]{2,1,0:T(8,128)(2,1)S(1)}, u32[]{:S(2)}, u32[]{:S(2)}) %collective-permute-start.23) | collective-permute-done | bytes 344096 | tf_op jit(solution)/shard_map/ppermute | solution.py:451
  114.2 5.6 %conv.5 = (f32[256,512]{1,0:T(8,128)}, f32[8,512]{1,0:T(8,128)}, f32[32,512]{1,0:T(8,128)}, f32[32,512]{1,0:T(8,128)}) custom-call(s32[8]{0:T(128)} %concatenate.147.meta, bf16[320,512]{1,0:T(8,128)(2,1)} %maximum_select_fusion.ext, bf16[8,144,256]{2,1,0:T(8,128)(2,1)} %copy-done.5, bf16[8,144,256]{2,1,0:T(8,128)(2,1)} %copy-done.25, ...), custom_call_target="tpu_custom_call" | custom-call | flops 1207959552 | bytes 5718048 | tf_op jit(solution)/shard_map/conv/pallas_call | solution.py:459
  122.6 4.0 collective-permute-done.24.rest_5_
  168.2 5.7 %conv.6 = (f32[256,512]{1,0:T(8,128)}, f32[8,512]{1,0:T(8,128)}, f32[32,512]{1,0:T(8,128)}, f32[32,512]{1,0:T(8,128)}) custom-call(s32[8]{0:T(128)} %concatenate.147.meta, bf16[320,512]{1,0:T(8,128)(2,1)} %get-tuple-element.73.ext.a1, bf16[8,168,256]{2,1,0:T(8,128)(2,1)} %copy-done.3, bf16[8,168,256]{2,1,0:T(8,128)(2,1)} %copy-done.15, ...), custom_call_target="tpu_custom_call" | custom-call | flops 1207959552 | bytes 6504480 | tf_op jit(solution)/shard_map/conv/pallas_call | solution.py:459
  177.1 14.4 %collective-permute-done.70 = bf16[3,8,512]{2,1,0:T(8,128)(2,1)} collective-permute-done((bf16[3,8,512]{2,1,0:T(8,128)(2,1)}, bf16[3,8,512]{2,1,0:T(8,128)(2,1)}, u32[]{:S(2)}, u32[]{:S(2)}) %collective-permute-start.70) | collective-permute-done | bytes 24608 | tf_op jit(solution)/shard_map/ppermute | solution.py:451
  191.9 3.2 expand.1
  202.6 9.5 %collective-permute-done.52.rest_5_ = bf16[8,144,256]{2,1,0:T(8,128)(2,1)S(1)} collective-permute-done((bf16[8,144,256]{2,1,0:T(8,128)(2,1)S(1)}, bf16[8,144,256]{2,1,0:T(8,128)(2,1)S(1)}, u32[]{:S(2)}, u32[]{:S(2)}) %collective-permute-start.52) | collective-permute-done | bytes 589856 | tf_op jit(solution)/shard_map/ppermute | solution.py:451
  212.1 4.7 collective-permute-done.32
  218.7 5.4 %collective-permute-done.62.rest_5_ = bf16[8,144,256]{2,1,0:T(8,128)(2,1)} collective-permute-done((bf16[8,144,256]{2,1,0:T(8,128)(2,1)S(1)}, bf16[8,144,256]{2,1,0:T(8,128)(2,1)}, u32[]{:S(2)}, u32[]{:S(2)}) %collective-permute-start.62) | collective-permute-done | bytes 589856 | tf_op jit(solution)/shard_map/ppermute | solution.py:451
  239.5 3.9 select.21
  243.4 5.7 %conv.9 = (f32[256,512]{1,0:T(8,128)}, f32[8,512]{1,0:T(8,128)}, f32[32,512]{1,0:T(8,128)}, f32[32,512]{1,0:T(8,128)}) custom-call(s32[8]{0:T(128)} %concatenate.147.meta, bf16[320,512]{1,0:T(8,128)(2,1)} %get-tuple-element.86.ext, bf16[8,144,256]{2,1,0:T(8,128)(2,1)} %copy-done.11, bf16[8,144,256]{2,1,0:T(8,128)(2,1)} %collective-permute-done.58.rest_1_, ...), custom_call_target="tpu_custom_call" | custom-call | flops 1207959552 | bytes 5718048 | tf_op jit(solution)/shard_map/conv/pallas_call | solution.py:459
  249.8 3.1 collective-permute-start.71
  253.0 18.3 %conv.8 = (f32[256,512]{1,0:T(8,128)}, f32[8,512]{1,0:T(8,128)}, f32[32,512]{1,0:T(8,128)}, f32[32,512]{1,0:T(8,128)}) custom-call(s32[8]{0:T(128)} %concatenate.147.meta, bf16[320,512]{1,0:T(8,128)(2,1)} %get-tuple-element.84.ext, bf16[8,144,256]{2,1,0:T(8,128)(2,1)} %copy-done.9, bf16[8,144,256]{2,1,0:T(8,128)(2,1)} %collective-permute-done.48.rest_1_, ...), custom_call_target="tpu_custom_call" | custom-call | flops 1207959552 | bytes 5718048 | tf_op jit(solution)/shard_map/conv/pallas_call | solution.py:459
  273.4 5.7 %conv.7 = (f32[256,512]{1,0:T(8,128)}, f32[8,512]{1,0:T(8,128)}, f32[32,512]{1,0:T(8,128)}, f32[32,512]{1,0:T(8,128)}) custom-call(s32[8]{0:T(128)} %concatenate.147.meta, bf16[320,512]{1,0:T(8,128)(2,1)} %get-tuple-element.82.ext, bf16[8,144,256]{2,1,0:T(8,128)(2,1)} %copy-done.7, bf16[8,144,256]{2,1,0:T(8,128)(2,1)} %copy-done.31, ...), custom_call_target="tpu_custom_call" | custom-call | flops 1207959552 | bytes 5718048 | tf_op jit(solution)/shard_map/conv/pallas_call | solution.py:459
  292.7 5.7 %pool.1 = (f32[3,32,512]{2,1,0:T(8,128)}, f32[8,512]{1,0:T(8,128)}) custom-call(s32[8]{0:T(128)} %concatenate.147.meta, f32[3]{0:T(128)} %divide_multiply_fusion.lam, f32[256,512]{1,0:T(8,128)} %get-tuple-element.83.z30, f32[256,512]{1,0:T(8,128)} %get-tuple-element.85.z31, f32[256,512]{1,0:T(8,128)} %get-tuple-element.87.z32, f32[8,512]{1,0:T(8,128)} %add.397.stats, ...), custom_call_target="tpu_custom_call" | custom-call | bytes 2133036 | tf_op jit(solution)/shard_map/pool/pallas_call | solution.py:459
  300.9 2.9 collective-permute-done.75
  304.5 3.0 collective-permute-done.76
  308.4 2.8 collective-permute-done.77
  313.2 4.5 task_grad.1
  317.7 5.7 %dgrad.5.ds0 = f32[256,512]{1,0:T(8,128)} custom-call(s32[8]{0:T(128)} %concatenate.147.meta, bf16[320,512]{1,0:T(8,128)(2,1)} %get-tuple-element.99.ext.grad, bf16[8,144,256]{2,1,0:T(8,128)(2,1)} %copy-done.7, bf16[8,144,256]{2,1,0:T(8,128)(2,1)} %copy-done.31, bf16[8,144,256]{2,1,0:T(8,128)(2,1)} %copy-done.38, bf16[8,144,256]{2,1,0:T(8,128)(2,1)} %copy-done.40, ...), custom_call_target="tpu_custom_call" | custom-call | flops 1207959552 | bytes 5570592 | tf_op jit(solution)/shard_map/dgrad/pallas_call | solution.py:459
  323.4 5.6 %dgrad.6.ds1 = f32[256,512]{1,0:T(8,128)} custom-call(s32[8]{0:T(128)} %concatenate.147.meta, bf16[320,512]{1,0:T(8,128)(2,1)} %get-tuple-element.100.ext.grad, bf16[8,144,256]{2,1,0:T(8,128)(2,1)} %copy-done.9, bf16[8,144,256]{2,1,0:T(8,128)(2,1)} %collective-permute-done.48.rest_1_, bf16[8,144,256]{2,1,0:T(8,128)(2,1)} %copy-done.32, ...), custom_call_target="tpu_custom_call" | custom-call | flops 1207959552 | bytes 5570592 | tf_op jit(solution)/shard_map/dgrad/pallas_call | solution.py:459
  329.0 5.6 %dgrad.7.ds2 = f32[256,512]{1,0:T(8,128)} custom-call(s32[8]{0:T(128)} %concatenate.147.meta, bf16[320,512]{1,0:T(8,128)(2,1)} %get-tuple-element.101.ext.grad, bf16[8,144,256]{2,1,0:T(8,128)(2,1)} %copy-done.11, bf16[8,144,256]{2,1,0:T(8,128)(2,1)} %collective-permute-done.58.rest_1_, bf16[8,144,256]{2,1,0:T(8,128)(2,1)} %copy-done.35, ...), custom_call_target="tpu_custom_call" | custom-call | flops 1207959552 | bytes 5570592 | tf_op jit(solution)/shard_map/dgrad/pallas_call | solution.py:459
  334.7 5.6 %branch_grad.1 = (f32[3,256,512]{2,1,0:T(8,128)}, f32[256,512]{1,0:T(8,128)}, f32[8,512]{1,0:T(8,128)}, f32[32,512]{1,0:T(8,128)}, f32[32,512]{1,0:T(8,128)}) custom-call(s32[8]{0:T(128)} %concatenate.147.meta, f32[256,512]{1,0:T(8,128)} %dgrad.5.ds0, f32[256,512]{1,0:T(8,128)} %dgrad.6.ds1, f32[256,512]{1,0:T(8,128)} %dgrad.7.ds2, ...), custom_call_target="tpu_custom_call" | custom-call | bytes 6360096 | tf_op jit(solution)/shard_map/branch_grad/pallas_call | solution.py:459
  344.3 4.2 collective-permute-done.79
  349.2 3.0 collective-permute-done.80
  356.5 4.0 expand_grad.1
  360.6 4.8 wgrad.7
  366.1 4.4 wgrad.8
  371.4 4.4 wgrad.9
  381.5 5.6 %dgrad.8.da1 = f32[256,512]{1,0:T(8,128)} custom-call(s32[8]{0:T(128)} %concatenate.147.meta, bf16[320,512]{1,0:T(8,128)(2,1)} %norm_grad.2.ext.grad, bf16[8,168,256]{2,1,0:T(8,128)(2,1)} %copy-done.3, bf16[8,168,256]{2,1,0:T(8,128)(2,1)} %copy-done.15, bf16[8,168,256]{2,1,0:T(8,128)(2,1)} %copy-done.17, bf16[8,168,256]{2,1,0:T(8,128)(2,1)} %copy-done.19, ...), custom_call_target="tpu_custom_call" | custom-call | flops 1207959552 | bytes 6357024 | tf_op jit(solution)/shard_map/dgrad/pallas_call | solution.py:459
  387.8 3.7 squeeze_grad.1
  392.7 4.7 wgrad.6
  404.7 2.9 collective-permute-done.88
  419.8 5.6 %dgrad.9 = f32[256,512]{1,0:T(8,128)} custom-call(s32[8]{0:T(128)} %concatenate.147.meta, bf16[320,512]{1,0:T(8,128)(2,1)} %norm_grad.3.ext.grad, bf16[8,144,256]{2,1,0:T(8,128)(2,1)} %copy-done.5, bf16[8,144,256]{2,1,0:T(8,128)(2,1)} %copy-done.25, bf16[8,144,256]{2,1,0:T(8,128)(2,1)} %copy-done.27, bf16[8,144,256]{2,1,0:T(8,128)(2,1)} %copy-done.29, ...), custom_call_target="tpu_custom_call" | custom-call | flops 1207959552 | bytes 5570592 | tf_op jit(solution)/shard_map/dgrad/pallas_call | solution.py:459
  426.1 4.8 wgrad.5
  452.0 3.1 collective-permute-done.103
  456.3 6.9 %collective-permute-done.107 = bf16[4,144,512]{2,1,0:T(8,128)(2,1)S(1)} collective-permute-done((bf16[4,144,512]{2,1,0:T(8,128)(2,1)S(1)}, bf16[4,144,512]{2,1,0:T(8,128)(2,1)S(1)}, u32[]{:S(2)}, u32[]{:S(2)}) %collective-permute-start.107) | collective-permute-done | bytes 589856 | tf_op jit(solution)/shard_map/ppermute | solution.py:451
  464.0 3.8 collective-permute-done.95
  469.6 4.5 collective-permute-done.100
  475.2 7.0 %collective-permute-done.104 = bf16[2,144,512]{2,1,0:T(8,128)(2,1)S(1)} collective-permute-done((bf16[2,144,512]{2,1,0:T(8,128)(2,1)S(1)}, bf16[2,144,512]{2,1,0:T(8,128)(2,1)S(1)}, u32[]{:S(2)}, u32[]{:S(2)}) %collective-permute-start.104) | collective-permute-done | bytes 294944 | tf_op jit(solution)/shard_map/ppermute | solution.py:451
  502.0 3.6 collective-permute-done.92
  517.0 12.0 %multiply_subtract_fusion = (f32[1,5,73728]{2,0,1:T(1,128)}, f32[1,5,73728]{2,0,1:T(1,128)}, f32[1,5,73728]{2,0,1:T(1,128)}) fusion(f32[1,5,73728]{2,0,1:T(1,128)S(1)} %copy-done.4, f32[1,5,73728]{2,0,1:T(1,128)S(1)} %constant_dynamic-update-slice_fusion.2, f32[1,5,73728]{2,0,1:T(1,128)S(1)} %copy-done.44, f32[1,5,73728]{2,0,1:T(1,128)S(1)} %copy-done.45), kind=kLoop, calls=%fused_computation.8 | loop fusion | flops 5529600 | bytes 10321920 | tf_op jit(solution)/shard_map/sub | solution.py:199
  (612 shorter events, 231.4 us)
Async XLA Ops:
  5.7 23.4 %collective-permute-start = (bf16[16,512]{1,0:T(8,128)(2,1)S(1)}, bf16[16,512]{1,0:T(8,128)(2,1)S(1)}, u32[]{:S(2)}, u32[]{:S(2)}) collective-permute-start(bf16[16,512]{1,0:T(8,128)(2,1)S(1)} %get-tuple-element.190), channel_id=1, source_target_pairs={{0,1},{1,0},{2,3},{3,2},{4,5},{5,4},{6,7},{7,6},{8,9},{9,8},{10,11... | collective-permute-start | bytes 49160 | tf_op jit(solution)/shard_map/ppermute | solution.py:451
  6.2 23.2 %collective-permute-start.1 = (bf16[16,512]{1,0:T(8,128)(2,1)S(1)}, bf16[16,512]{1,0:T(8,128)(2,1)S(1)}, u32[]{:S(2)}, u32[]{:S(2)}) collective-permute-start(bf16[16,512]{1,0:T(8,128)(2,1)S(1)} %get-tuple-element.189), channel_id=1, source_target_pairs={{0,3},{1,2},{2,1},{3,0},{4,7},{5,6},{6,5},{7,4},{8,11},{9,10},{10,... | collective-permute-start | bytes 49160 | tf_op jit(solution)/shard_map/ppermute | solution.py:451
  15.5 24.0 %collective-permute-start.3 = (bf16[144,512]{1,0:T(8,128)(2,1)S(1)}, bf16[144,512]{1,0:T(8,128)(2,1)S(1)}, u32[]{:S(2)}, u32[]{:S(2)}) collective-permute-start(bf16[144,512]{1,0:T(8,128)(2,1)S(1)} %squeeze.185), channel_id=1, source_target_pairs={{0,16},{1,17},{2,18},{3,19},{4,20},{5,21},{6,22},{7,23},{8,24},{9,... | collective-permute-start | bytes 442376 | tf_op jit(solution)/shard_map/ppermute | solution.py:451
  18.4 34.8 %collective-permute-start.17 = (bf16[168,512]{1,0:T(8,128)(2,1)S(1)}, bf16[168,512]{1,0:T(8,128)(2,1)S(1)}, u32[]{:S(2)}, u32[]{:S(2)}) collective-permute-start(bf16[168,512]{1,0:T(8,128)(2,1)S(1)} %constant_dynamic-update-slice_fusion), channel_id=1, source_target_pairs={{0,16},{1,17},{2,18},{3,19},{4,20},{5,21},{6,22},{7,23},{8,24},{9,... | collective-permute-start | bytes 516104 | tf_op jit(solution)/shard_map/ppermute | solution.py:451
  18.9 31.0 %collective-permute-start.35 = (bf16[144,512]{1,0:T(8,128)(2,1)S(1)}, bf16[144,512]{1,0:T(8,128)(2,1)S(1)}, u32[]{:S(2)}, u32[]{:S(2)}) collective-permute-start(bf16[144,512]{1,0:T(8,128)(2,1)S(1)} %squeeze.187), channel_id=1, source_target_pairs={{0,16},{1,17},{2,18},{3,19},{4,20},{5,21},{6,22},{7,23},{8,24},{9,... | collective-permute-start | bytes 442376 | tf_op jit(solution)/shard_map/ppermute | solution.py:451
  29.1 24.1 %collective-permute-start.45 = (bf16[144,512]{1,0:T(8,128)(2,1)S(1)}, bf16[144,512]{1,0:T(8,128)(2,1)S(1)}, u32[]{:S(2)}, u32[]{:S(2)}) collective-permute-start(bf16[144,512]{1,0:T(8,128)(2,1)S(1)} %squeeze.188), channel_id=1, source_target_pairs={{0,16},{1,17},{2,18},{3,19},{4,20},{5,21},{6,22},{7,23},{8,24},{9,... | collective-permute-start | bytes 442376 | tf_op jit(solution)/shard_map/ppermute | solution.py:451
  29.4 36.0 %collective-permute-start.55 = (bf16[144,512]{1,0:T(8,128)(2,1)S(1)}, bf16[144,512]{1,0:T(8,128)(2,1)S(1)}, u32[]{:S(2)}, u32[]{:S(2)}) collective-permute-start(bf16[144,512]{1,0:T(8,128)(2,1)S(1)} %squeeze.189), channel_id=1, source_target_pairs={{0,16},{1,17},{2,18},{3,19},{4,20},{5,21},{6,22},{7,23},{8,24},{9,... | collective-permute-start | bytes 442376 | tf_op jit(solution)/shard_map/ppermute | solution.py:451
  39.5 28.1 %collective-permute-start.2 = (bf16[160,512]{1,0:T(8,128)(2,1)S(1)}, bf16[160,512]{1,0:T(8,128)(2,1)S(1)}, u32[]{:S(2)}, u32[]{:S(2)}) collective-permute-start(bf16[160,512]{1,0:T(8,128)(2,1)S(1)} %bitcast.190), channel_id=1, source_target_pairs={{0,16},{1,17},{2,18},{3,19},{4,20},{5,21},{6,22},{7,23},{8,24},{9,... | collective-permute-start | bytes 491528 | tf_op jit(solution)/shard_map/ppermute | solution.py:451
  53.1 36.0 %collective-permute-start.36 = (bf16[2,144,512]{2,1,0:T(8,128)(2,1)S(1)}, bf16[2,144,512]{2,1,0:T(8,128)(2,1)S(1)}, u32[]{:S(2)}, u32[]{:S(2)}) collective-permute-start(bf16[2,144,512]{2,1,0:T(8,128)(2,1)S(1)} %pad_maximum_fusion.20), channel_id=1, source_target_pairs={{0,8},{1,9},{2,10},{3,11},{4,12},{5,13},{6,14},{7,15},{8,0},{9,1},... | collective-permute-start | bytes 884744 | tf_op jit(solution)/shard_map/ppermute | solution.py:451
  53.2 36.6 %collective-permute-start.46 = (bf16[2,144,512]{2,1,0:T(8,128)(2,1)S(1)}, bf16[2,144,512]{2,1,0:T(8,128)(2,1)S(1)}, u32[]{:S(2)}, u32[]{:S(2)}) collective-permute-start(bf16[2,144,512]{2,1,0:T(8,128)(2,1)S(1)} %pad_maximum_fusion.21), channel_id=1, source_target_pairs={{0,8},{1,9},{2,10},{3,11},{4,12},{5,13},{6,14},{7,15},{8,0},{9,1},... | collective-permute-start | bytes 884744 | tf_op jit(solution)/shard_map/ppermute | solution.py:451
  65.2 19.9 %collective-permute-start.18 = (bf16[2,168,512]{2,1,0:T(8,128)(2,1)S(1)}, bf16[2,168,512]{2,1,0:T(8,128)(2,1)S(1)}, u32[]{:S(2)}, u32[]{:S(2)}) collective-permute-start(bf16[2,168,512]{2,1,0:T(8,128)(2,1)S(1)} %pad_maximum_fusion.18), channel_id=1, source_target_pairs={{0,8},{1,9},{2,10},{3,11},{4,12},{5,13},{6,14},{7,15},{8,0},{9,1},... | collective-permute-start | bytes 1032200 | tf_op jit(solution)/shard_map/ppermute | solution.py:451
  65.3 19.9 %collective-permute-start.5 = (bf16[4,144,256]{2,1,0:T(8,128)(2,1)S(1)}, bf16[4,144,256]{2,1,0:T(8,128)(2,1)S(1)}, u32[]{:S(2)}, u32[]{:S(2)}) collective-permute-start(bf16[4,144,256]{2,1,0:T(8,128)(2,1)S(1)} %get-tuple-element.186), channel_id=1, source_target_pairs={{0,4},{1,5},{2,6},{3,7},{4,0},{5,1},{6,2},{7,3},{8,12},{9,13},{10,... | collective-permute-start | bytes 884744 | tf_op jit(solution)/shard_map/ppermute | solution.py:451
  67.6 18.2 %collective-permute-start.9 = (bf16[4,144,256]{2,1,0:T(8,128)(2,1)S(1)}, bf16[4,144,256]{2,1,0:T(8,128)(2,1)S(1)}, u32[]{:S(2)}, u32[]{:S(2)}) collective-permute-start(bf16[4,144,256]{2,1,0:T(8,128)(2,1)S(1)} %get-tuple-element.185), channel_id=1, source_target_pairs={{0,2},{1,3},{2,0},{3,1},{4,6},{5,7},{6,4},{7,5},{8,10},{9,11},{10,... | collective-permute-start | bytes 884744 | tf_op jit(solution)/shard_map/ppermute | solution.py:451
  85.3 22.7 %collective-permute-start.6 = (bf16[8,144,256]{2,1,0:T(8,128)(2,1)S(1)}, bf16[8,144,256]{2,1,0:T(8,128)(2,1)S(1)}, u32[]{:S(2)}, u32[]{:S(2)}) collective-permute-start(bf16[8,144,256]{2,1,0:T(8,128)(2,1)S(1)} %pad_maximum_fusion.4.rest_0_), channel_id=1, source_target_pairs={{0,2},{1,3},{2,0},{3,1},{4,6},{5,7},{6,4},{7,5},{8,10},{9,11},{10,... | collective-permute-start | bytes 1769480 | tf_op jit(solution)/shard_map/ppermute | solution.py:451
  85.9 22.6 %collective-permute-start.10 = (bf16[8,144,256]{2,1,0:T(8,128)(2,1)S(1)}, bf16[8,144,256]{2,1,0:T(8,128)(2,1)S(1)}, u32[]{:S(2)}, u32[]{:S(2)}) collective-permute-start(bf16[8,144,256]{2,1,0:T(8,128)(2,1)S(1)} %pad_maximum_fusion.5.rest_4_), channel_id=1, source_target_pairs={{0,4},{1,5},{2,6},{3,7},{4,0},{5,1},{6,2},{7,3},{8,12},{9,13},{10,... | collective-permute-start | bytes 1769480 | tf_op jit(solution)/shard_map/ppermute | solution.py:451
  87.5 20.4 %collective-permute-start.23 = (bf16[4,168,256]{2,1,0:T(8,128)(2,1)S(1)}, bf16[4,168,256]{2,1,0:T(8,128)(2,1)S(1)}, u32[]{:S(2)}, u32[]{:S(2)}) collective-permute-start(bf16[4,168,256]{2,1,0:T(8,128)(2,1)S(1)} %get-tuple-element.177), channel_id=1, source_target_pairs={{0,2},{1,3},{2,0},{3,1},{4,6},{5,7},{6,4},{7,5},{8,10},{9,11},{10,... | collective-permute-start | bytes 1032200 | tf_op jit(solution)/shard_map/ppermute | solution.py:451
  89.2 19.5 %collective-permute-start.19 = (bf16[4,168,256]{2,1,0:T(8,128)(2,1)S(1)}, bf16[4,168,256]{2,1,0:T(8,128)(2,1)S(1)}, u32[]{:S(2)}, u32[]{:S(2)}) collective-permute-start(bf16[4,168,256]{2,1,0:T(8,128)(2,1)S(1)} %get-tuple-element.178), channel_id=1, source_target_pairs={{0,4},{1,5},{2,6},{3,7},{4,0},{5,1},{6,2},{7,3},{8,12},{9,13},{10,... | collective-permute-start | bytes 1032200 | tf_op jit(solution)/shard_map/ppermute | solution.py:451
  89.8 21.4 %collective-permute-start.7 = (bf16[8,144,256]{2,1,0:T(8,128)(2,1)S(1)}, bf16[8,144,256]{2,1,0:T(8,128)(2,1)S(1)}, u32[]{:S(2)}, u32[]{:S(2)}) collective-permute-start(bf16[8,144,256]{2,1,0:T(8,128)(2,1)S(1)} %pad_maximum_fusion.4.rest_0_), channel_id=1, source_target_pairs={{0,1},{1,0},{2,3},{3,2},{4,5},{5,4},{6,7},{7,6},{8,9},{9,8},{10,11... | collective-permute-start | bytes 1769480 | tf_op jit(solution)/shard_map/ppermute | solution.py:451
  111.4 18.2 %collective-permute-start.20 = (bf16[8,168,256]{2,1,0:T(8,128)(2,1)S(1)}, bf16[8,168,256]{2,1,0:T(8,128)(2,1)S(1)}, u32[]{:S(2)}, u32[]{:S(2)}) collective-permute-start(bf16[8,168,256]{2,1,0:T(8,128)(2,1)S(1)} %pad_maximum_fusion.rest_0_), channel_id=1, source_target_pairs={{0,2},{1,3},{2,0},{3,1},{4,6},{5,7},{6,4},{7,5},{8,10},{9,11},{10,... | collective-permute-start | bytes 2064392 | tf_op jit(solution)/shard_map/ppermute | solution.py:451
  136.2 23.6 %collective-permute-start.69 = (bf16[3,8,512]{2,1,0:T(8,128)(2,1)}, bf16[3,8,512]{2,1,0:T(8,128)(2,1)}, u32[]{:S(2)}, u32[]{:S(2)}) collective-permute-start(bf16[3,8,512]{2,1,0:T(8,128)(2,1)} %get-tuple-element.188), channel_id=1, source_target_pairs={{0,1},{1,0},{2,3},{3,2},{4,5},{5,4},{6,7},{7,6},{8,9},{9,8},{10,11... | collective-permute-start | bytes 73736 | tf_op jit(solution)/shard_map/ppermute | solution.py:451
  143.3 18.1 %collective-permute-start.51 = (bf16[4,144,256]{2,1,0:T(8,128)(2,1)S(1)}, bf16[4,144,256]{2,1,0:T(8,128)(2,1)}, u32[]{:S(2)}, u32[]{:S(2)}) collective-permute-start(bf16[4,144,256]{2,1,0:T(8,128)(2,1)S(1)} %copy-done.49), channel_id=1, source_target_pairs={{0,2},{1,3},{2,0},{3,1},{4,6},{5,7},{6,4},{7,5},{8,10},{9,11},{10,... | collective-permute-start | bytes 884744 | tf_op jit(solution)/shard_map/ppermute | solution.py:451
  156.9 41.1 %collective-permute-start.38 = (bf16[8,144,256]{2,1,0:T(8,128)(2,1)S(1)}, bf16[8,144,256]{2,1,0:T(8,128)(2,1)S(1)}, u32[]{:S(2)}, u32[]{:S(2)}) collective-permute-start(bf16[8,144,256]{2,1,0:T(8,128)(2,1)S(1)} %pad_maximum_fusion.7.rest_0_), channel_id=1, source_target_pairs={{0,2},{1,3},{2,0},{3,1},{4,6},{5,7},{6,4},{7,5},{8,10},{9,11},{10,... | collective-permute-start | bytes 1769480 | tf_op jit(solution)/shard_map/ppermute | solution.py:451
  159.8 36.1 %collective-permute-start.61 = (bf16[4,144,256]{2,1,0:T(8,128)(2,1)}, bf16[4,144,256]{2,1,0:T(8,128)(2,1)}, u32[]{:S(2)}, u32[]{:S(2)}) collective-permute-start(bf16[4,144,256]{2,1,0:T(8,128)(2,1)} %get-tuple-element.179), channel_id=1, source_target_pairs={{0,2},{1,3},{2,0},{3,1},{4,6},{5,7},{6,4},{7,5},{8,10},{9,11},{10,... | collective-permute-start | bytes 884744 | tf_op jit(solution)/shard_map/ppermute | solution.py:451
  161.4 38.6 %collective-permute-start.42 = (bf16[8,144,256]{2,1,0:T(8,128)(2,1)S(1)}, bf16[8,144,256]{2,1,0:T(8,128)(2,1)}, u32[]{:S(2)}, u32[]{:S(2)}) collective-permute-start(bf16[8,144,256]{2,1,0:T(8,128)(2,1)S(1)} %pad_maximum_fusion.8.rest_4_), channel_id=1, source_target_pairs={{0,4},{1,5},{2,6},{3,7},{4,0},{5,1},{6,2},{7,3},{8,12},{9,13},{10,... | collective-permute-start | bytes 1769480 | tf_op jit(solution)/shard_map/ppermute | solution.py:451
  162.1 38.4 %collective-permute-start.48 = (bf16[8,144,256]{2,1,0:T(8,128)(2,1)S(1)}, bf16[8,144,256]{2,1,0:T(8,128)(2,1)}, u32[]{:S(2)}, u32[]{:S(2)}) collective-permute-start(bf16[8,144,256]{2,1,0:T(8,128)(2,1)S(1)} %pad_maximum_fusion.10.rest_0_), channel_id=1, source_target_pairs={{0,2},{1,3},{2,0},{3,1},{4,6},{5,7},{6,4},{7,5},{8,10},{9,11},{10,... | collective-permute-start | bytes 1769480 | tf_op jit(solution)/shard_map/ppermute | solution.py:451
  168.2 23.3 %collective-permute-start.70 = (bf16[3,8,512]{2,1,0:T(8,128)(2,1)}, bf16[3,8,512]{2,1,0:T(8,128)(2,1)}, u32[]{:S(2)}, u32[]{:S(2)}) collective-permute-start(bf16[3,8,512]{2,1,0:T(8,128)(2,1)} %get-tuple-element.187), channel_id=1, source_target_pairs={{0,3},{1,2},{2,1},{3,0},{4,7},{5,6},{6,5},{7,4},{8,11},{9,10},{10,... | collective-permute-start | bytes 73736 | tf_op jit(solution)/shard_map/ppermute | solution.py:451
  200.0 17.9 %collective-permute-start.53 = (bf16[8,144,256]{2,1,0:T(8,128)(2,1)S(1)}, bf16[8,144,256]{2,1,0:T(8,128)(2,1)S(1)}, u32[]{:S(2)}, u32[]{:S(2)}) collective-permute-start(bf16[8,144,256]{2,1,0:T(8,128)(2,1)S(1)} %pad_maximum_fusion.11.rest_4_), channel_id=1, source_target_pairs={{0,1},{1,0},{2,3},{3,2},{4,5},{5,4},{6,7},{7,6},{8,9},{9,8},{10,11... | collective-permute-start | bytes 1769480 | tf_op jit(solution)/shard_map/ppermute | solution.py:451
  200.6 18.1 %collective-permute-start.58 = (bf16[8,144,256]{2,1,0:T(8,128)(2,1)S(1)}, bf16[8,144,256]{2,1,0:T(8,128)(2,1)}, u32[]{:S(2)}, u32[]{:S(2)}) collective-permute-start(bf16[8,144,256]{2,1,0:T(8,128)(2,1)S(1)} %pad_maximum_fusion.13.rest_0_), channel_id=1, source_target_pairs={{0,2},{1,3},{2,0},{3,1},{4,6},{5,7},{6,4},{7,5},{8,10},{9,11},{10,... | collective-permute-start | bytes 1769480 | tf_op jit(solution)/shard_map/ppermute | solution.py:451
  201.0 23.1 %collective-permute-start.62 = (bf16[8,144,256]{2,1,0:T(8,128)(2,1)S(1)}, bf16[8,144,256]{2,1,0:T(8,128)(2,1)}, u32[]{:S(2)}, u32[]{:S(2)}) collective-permute-start(bf16[8,144,256]{2,1,0:T(8,128)(2,1)S(1)} %pad_maximum_fusion.14.rest_4_), channel_id=1, source_target_pairs={{0,4},{1,5},{2,6},{3,7},{4,0},{5,1},{6,2},{7,3},{8,12},{9,13},{10,... | collective-permute-start | bytes 1769480 | tf_op jit(solution)/shard_map/ppermute | solution.py:451
  230.0 19.9 %collective-permute-start.54 = (bf16[8,144,256]{2,1,0:T(8,128)(2,1)}, bf16[8,144,256]{2,1,0:T(8,128)(2,1)S(1)}, u32[]{:S(2)}, u32[]{:S(2)}) collective-permute-start(bf16[8,144,256]{2,1,0:T(8,128)(2,1)} %copy-done.33), channel_id=1, source_target_pairs={{0,1},{1,0},{2,3},{3,2},{4,5},{5,4},{6,7},{7,6},{8,9},{9,8},{10,11... | collective-permute-start | bytes 1769480 | tf_op jit(solution)/shard_map/ppermute | solution.py:451
  232.3 39.7 %collective-permute-start.39 = (bf16[8,144,256]{2,1,0:T(8,128)(2,1)S(1)}, bf16[8,144,256]{2,1,0:T(8,128)(2,1)S(1)}, u32[]{:S(2)}, u32[]{:S(2)}) collective-permute-start(bf16[8,144,256]{2,1,0:T(8,128)(2,1)S(1)} %pad_maximum_fusion.7.rest_0_), channel_id=1, source_target_pairs={{0,1},{1,0},{2,3},{3,2},{4,5},{5,4},{6,7},{7,6},{8,9},{9,8},{10,11... | collective-permute-start | bytes 1769480 | tf_op jit(solution)/shard_map/ppermute | solution.py:451
  232.4 39.6 %collective-permute-start.43 = (bf16[8,144,256]{2,1,0:T(8,128)(2,1)S(1)}, bf16[8,144,256]{2,1,0:T(8,128)(2,1)S(1)}, u32[]{:S(2)}, u32[]{:S(2)}) collective-permute-start(bf16[8,144,256]{2,1,0:T(8,128)(2,1)S(1)} %pad_maximum_fusion.8.rest_4_), channel_id=1, source_target_pairs={{0,1},{1,0},{2,3},{3,2},{4,5},{5,4},{6,7},{7,6},{8,9},{9,8},{10,11... | collective-permute-start | bytes 1769480 | tf_op jit(solution)/shard_map/ppermute | solution.py:451
  233.0 39.0 %collective-permute-start.40 = (bf16[8,144,256]{2,1,0:T(8,128)(2,1)}, bf16[8,144,256]{2,1,0:T(8,128)(2,1)S(1)}, u32[]{:S(2)}, u32[]{:S(2)}) collective-permute-start(bf16[8,144,256]{2,1,0:T(8,128)(2,1)} %copy-done.31), channel_id=1, source_target_pairs={{0,1},{1,0},{2,3},{3,2},{4,5},{5,4},{6,7},{7,6},{8,9},{9,8},{10,11... | collective-permute-start | bytes 1769480 | tf_op jit(solution)/shard_map/ppermute | solution.py:451
  234.2 37.8 %collective-permute-start.44 = (bf16[8,144,256]{2,1,0:T(8,128)(2,1)}, bf16[8,144,256]{2,1,0:T(8,128)(2,1)S(1)}, u32[]{:S(2)}, u32[]{:S(2)}) collective-permute-start(bf16[8,144,256]{2,1,0:T(8,128)(2,1)} %collective-permute-done.42.rest_5_), channel_id=1, source_target_pairs={{0,1},{1,0},{2,3},{3,2},{4,5},{5,4},{6,7},{7,6},{8,9},{9,8},{10,11... | collective-permute-start | bytes 1769480 | tf_op jit(solution)/shard_map/ppermute | solution.py:451
  249.8 39.5 %collective-permute-start.71 = (bf16[3,48,512]{2,1,0:T(8,128)(2,1)S(1)}, bf16[3,48,512]{2,1,0:T(8,128)(2,1)S(1)}, u32[]{:S(2)}, u32[]{:S(2)}) collective-permute-start(bf16[3,48,512]{2,1,0:T(8,128)(2,1)S(1)} %bitcast.202), channel_id=1, source_target_pairs={{0,16},{1,17},{2,18},{3,19},{4,20},{5,21},{6,22},{7,23},{8,24},{9,... | collective-permute-start | bytes 442376 | tf_op jit(solution)/shard_map/ppermute | solution.py:451
  281.0 30.8 %collective-permute-start.72 = (f32[96,512]{1,0:T(8,128)S(1)}, f32[96,512]{1,0:T(8,128)S(1)}, u32[]{:S(2)}, u32[]{:S(2)}) collective-permute-start(f32[96,512]{1,0:T(8,128)S(1)} %pad_maximum_fusion.23), channel_id=1, source_target_pairs={{0,1},{1,0},{2,3},{3,2},{4,5},{5,4},{6,7},{7,6},{8,9},{9,8},{10,11... | collective-permute-start | bytes 589832 | tf_op jit(solution)/shard_map/ppermute | solution.py:451
  282.7 29.2 %collective-permute-start.73 = (f32[96,512]{1,0:T(8,128)S(1)}, f32[96,512]{1,0:T(8,128)S(1)}, u32[]{:S(2)}, u32[]{:S(2)}) collective-permute-start(f32[96,512]{1,0:T(8,128)S(1)} %pad_maximum_fusion.24), channel_id=1, source_target_pairs={{0,3},{1,2},{2,1},{3,0},{4,7},{5,6},{6,5},{7,4},{8,11},{9,10},{10,... | collective-permute-start | bytes 589832 | tf_op jit(solution)/shard_map/ppermute | solution.py:451
  375.8 56.1 %collective-permute-start.98 = (f32[8,144,512]{2,1,0:T(8,128)}, f32[8,144,512]{2,1,0:T(8,128)}, u32[]{:S(2)}, u32[]{:S(2)}) collective-permute-start(f32[8,144,512]{2,1,0:T(8,128)} %get-tuple-element.119), channel_id=1, source_target_pairs={{0,1},{1,0},{2,3},{3,2},{4,5},{5,4},{6,7},{7,6},{8,9},{9,8},{10,11... | collective-permute-start | bytes 7077896 | tf_op jit(solution)/shard_map/ppermute | solution.py:451
  375.8 60.7 %collective-permute-start.102 = (f32[8,144,512]{2,1,0:T(8,128)}, f32[8,144,512]{2,1,0:T(8,128)}, u32[]{:S(2)}, u32[]{:S(2)}) collective-permute-start(f32[8,144,512]{2,1,0:T(8,128)} %get-tuple-element.121), channel_id=1, source_target_pairs={{0,1},{1,0},{2,3},{3,2},{4,5},{5,4},{6,7},{7,6},{8,9},{9,8},{10,11... | collective-permute-start | bytes 7077896 | tf_op jit(solution)/shard_map/ppermute | solution.py:451
  376.3 63.2 %collective-permute-start.106 = (f32[8,144,512]{2,1,0:T(8,128)}, f32[8,144,512]{2,1,0:T(8,128)}, u32[]{:S(2)}, u32[]{:S(2)}) collective-permute-start(f32[8,144,512]{2,1,0:T(8,128)} %get-tuple-element.123), channel_id=1, source_target_pairs={{0,1},{1,0},{2,3},{3,2},{4,5},{5,4},{6,7},{7,6},{8,9},{9,8},{10,11... | collective-permute-start | bytes 7077896 | tf_op jit(solution)/shard_map/ppermute | solution.py:451
  397.4 45.5 %collective-permute-start.94 = (f32[8,144,512]{2,1,0:T(8,128)}, f32[8,144,512]{2,1,0:T(8,128)}, u32[]{:S(2)}, u32[]{:S(2)}) collective-permute-start(f32[8,144,512]{2,1,0:T(8,128)} %get-tuple-element.117), channel_id=1, source_target_pairs={{0,1},{1,0},{2,3},{3,2},{4,5},{5,4},{6,7},{7,6},{8,9},{9,8},{10,11... | collective-permute-start | bytes 7077896 | tf_op jit(solution)/shard_map/ppermute | solution.py:451
  441.9 21.3 %collective-permute-start.107 = (bf16[4,144,512]{2,1,0:T(8,128)(2,1)S(1)}, bf16[4,144,512]{2,1,0:T(8,128)(2,1)S(1)}, u32[]{:S(2)}, u32[]{:S(2)}) collective-permute-start(bf16[4,144,512]{2,1,0:T(8,128)(2,1)S(1)} %fusion.7), channel_id=1, source_target_pairs={{0,4},{1,5},{2,6},{3,7},{4,0},{5,1},{6,2},{7,3},{8,12},{9,13},{10,... | collective-permute-start | bytes 1769480 | tf_op jit(solution)/shard_map/ppermute | solution.py:451
  445.3 22.5 %collective-permute-start.95 = (bf16[2,2,144,512]{3,2,1,0:T(8,128)(2,1)S(1)}, bf16[2,2,144,512]{3,2,1,0:T(8,128)(2,1)S(1)}, u32[]{:S(2)}, u32[]{:S(2)}) collective-permute-start(bf16[2,2,144,512]{3,2,1,0:T(8,128)(2,1)S(1)} %fusion.4), channel_id=1, source_target_pairs={{0,2},{1,3},{2,0},{3,1},{4,6},{5,7},{6,4},{7,5},{8,10},{9,11},{10,... | collective-permute-start | bytes 1769480 | tf_op jit(solution)/shard_map/ppermute | solution.py:451
  450.0 47.4 %collective-permute-start.91 = (bf16[4,144,512]{2,1,0:T(8,128)(2,1)}, bf16[4,144,512]{2,1,0:T(8,128)(2,1)}, u32[]{:S(2)}, u32[]{:S(2)}) collective-permute-start(bf16[4,144,512]{2,1,0:T(8,128)(2,1)} %fusion.3), channel_id=1, source_target_pairs={{0,4},{1,5},{2,6},{3,7},{4,0},{5,1},{6,2},{7,3},{8,12},{9,13},{10,... | collective-permute-start | bytes 1769480 | tf_op jit(solution)/shard_map/ppermute | solution.py:451
  451.4 22.6 %collective-permute-start.100 = (bf16[2,144,512]{2,1,0:T(8,128)(2,1)S(1)}, bf16[2,144,512]{2,1,0:T(8,128)(2,1)S(1)}, u32[]{:S(2)}, u32[]{:S(2)}) collective-permute-start(bf16[2,144,512]{2,1,0:T(8,128)(2,1)S(1)} %fusion.11), channel_id=1, source_target_pairs={{0,2},{1,3},{2,0},{3,1},{4,6},{5,7},{6,4},{7,5},{8,10},{9,11},{10,... | collective-permute-start | bytes 884744 | tf_op jit(solution)/shard_map/ppermute | solution.py:451
  455.4 26.8 %collective-permute-start.104 = (bf16[2,144,512]{2,1,0:T(8,128)(2,1)S(1)}, bf16[2,144,512]{2,1,0:T(8,128)(2,1)S(1)}, u32[]{:S(2)}, u32[]{:S(2)}) collective-permute-start(bf16[2,144,512]{2,1,0:T(8,128)(2,1)S(1)} %fusion.12), channel_id=1, source_target_pairs={{0,4},{1,5},{2,6},{3,7},{4,0},{5,1},{6,2},{7,3},{8,12},{9,13},{10,... | collective-permute-start | bytes 884744 | tf_op jit(solution)/shard_map/ppermute | solution.py:451
  463.5 20.9 %collective-permute-start.108 = (bf16[2,144,512]{2,1,0:T(8,128)(2,1)S(1)}, bf16[2,144,512]{2,1,0:T(8,128)(2,1)S(1)}, u32[]{:S(2)}, u32[]{:S(2)}) collective-permute-start(bf16[2,144,512]{2,1,0:T(8,128)(2,1)S(1)} %fusion.13), channel_id=1, source_target_pairs={{0,2},{1,3},{2,0},{3,1},{4,6},{5,7},{6,4},{7,5},{8,10},{9,11},{10,... | collective-permute-start | bytes 884744 | tf_op jit(solution)/shard_map/ppermute | solution.py:451
  468.7 30.6 %collective-permute-start.96 = (bf16[2,144,512]{2,1,0:T(8,128)(2,1)}, bf16[2,144,512]{2,1,0:T(8,128)(2,1)}, u32[]{:S(2)}, u32[]{:S(2)}) collective-permute-start(bf16[2,144,512]{2,1,0:T(8,128)(2,1)} %fusion.10), channel_id=1, source_target_pairs={{0,4},{1,5},{2,6},{3,7},{4,0},{5,1},{6,2},{7,3},{8,12},{9,13},{10,... | collective-permute-start | bytes 884744 | tf_op jit(solution)/shard_map/ppermute | solution.py:451
  (150 other events, 1358.9 us)

commit v2 on v1

--- a/solution.py
+++ b/solution.py
@@ -446,26 +446,47 @@
 M_ROWS, M_GROUP, M_BAND, M_TOP, M_TOTAL, M_DEV = 0, 2, 4, 5, 6, 7
 
 
-def swap(value, mask):
+def swap(value, even, odd=None):
+    odd = even if odd is None else odd
     count = lax.axis_size("batch") * lax.axis_size("rows")
-    return lax.ppermute(value, AXES, [(i, i ^ mask) for i in range(count)])
-
-
-def kernel_call(body, out_shapes, args, places, scratch=(), flops=0, name=None):
+    pairs = [(i, i ^ (odd if i % 2 else even)) for i in range(count)]
+    return lax.ppermute(value, AXES, pairs)
+
+
+def kernel_call(
+    body, out_shapes, args, places, scratch=(), flops=0, name=None, deps=(), outs=None, alias=None
+):
     moved = sum(a.size * a.dtype.itemsize for a in args) + sum(
         o.size * o.dtype.itemsize for o in out_shapes
     )
     space = {"s": pltpu.SMEM, "v": pltpu.VMEM, "a": pl.ANY}
+    count, waits = len(args), len(deps)
+
+    def spec(place, value):
+        if isinstance(place, int):
+            shape = (None,) + value.shape[1:]
+            return pl.BlockSpec(shape, lambda i: (place,) + (0,) * (value.ndim - 1))
+        return pl.BlockSpec(memory_space=space[place])
+
+    def run(*refs):
+        body(*refs[:count], *refs[count + waits :])
+
+    grid = (1,) if any(isinstance(p, int) for p in places) else ()
     return pl.pallas_call(
-        body,
+        run,
         out_shape=out_shapes,
-        in_specs=[pl.BlockSpec(memory_space=space[p]) for p in places],
-        out_specs=[pl.BlockSpec(memory_space=pltpu.VMEM) for _ in out_shapes],
+        grid=grid,
+        in_specs=[spec(p, a) for p, a in zip(places, args)]
+        + [pl.BlockSpec(memory_space=pl.ANY)] * waits,
+        out_specs=[
+            pl.BlockSpec(memory_space=space[p]) for p in (outs or "v" * len(out_shapes))
+        ],
         scratch_shapes=list(scratch),
+        input_output_aliases=alias or {},
         compiler_params=pltpu.CompilerParams(vmem_limit_bytes=VMEM_LIMIT),
         cost_estimate=pl.CostEstimate(flops=flops, bytes_accessed=moved, transcendentals=0),
         name=name,
-    )(*args)
+    )(*args, *deps)
 
 
 def sds(shape, dtype=F32):
@@ -565,15 +586,17 @@
 
 def weights_start(meta, pieces, kernel, sem, block):
     half = C // 2
-    masks = {
-        "A": [x * 4 + a * 8 + b * 16 for x in range(2) for a in range(2) for b in range(2)],
-        "B": [y * 2 + a * 8 + b * 16 for y in range(2) for a in range(2) for b in range(2)],
-    }
-    plan = [("A", 0), ("A", 2), ("A", 1), ("A", 3), ("B", 0), ("B", 4), ("B", 1), ("B", 5)]
-    for ref, (part, extra) in zip(pieces, plan):
-        for i, mask in enumerate(masks[part]):
-            row = pl.multiple_of((meta[M_DEV] ^ (mask ^ extra)) * block, 16)
-            lane = 0 if part == "A" else half
+    for index, ref in enumerate(pieces):
+        other = index // 2
+        device = meta[M_DEV] ^ other
+        core = device & 1
+        near = jnp.where(core == 0, 4, 2)
+        far = 6 - near
+        lane = pl.multiple_of(core * half, half)
+        for i in range(16):
+            mask = (i & 1) + 16 * ((i >> 1) & 1) + 8 * ((i >> 2) & 1)
+            owner = device ^ (mask + near * (i >> 3) + far * (index % 2))
+            row = pl.multiple_of(owner * block, 16)
             pltpu.make_async_copy(
                 ref.at[i, pl.ds(0, block)],
                 kernel.at[pl.ds(row, block), pl.ds(lane, half)],
@@ -581,8 +604,25 @@
             ).start()
 
 
+def merge_body(spans, *refs):
+    out, sem = refs[-2], refs[-1]
+    copies = []
+    for i, (operand, first, count, place) in enumerate(spans):
+        source = refs[operand]
+        if first is None:
+            target = out.at[pl.ds(place, count)]
+        else:
+            source = source.at[pl.ds(first, count)]
+            target = out.at[place]
+        copies.append(pltpu.make_async_copy(source, target, sem.at[i]))
+    for copy in copies:
+        copy.start()
+    for copy in copies:
+        copy.wait()
+
+
 def conv_body(block, meta, ext, *rest):
-    pieces, (out, stats, edge1, edge2), (kernel, patch, sem) = rest[:8], rest[8:12], rest[12:]
+    pieces, (out, stats, edge1, edge2), (kernel, patch, sem) = rest[:4], rest[4:8], rest[8:]
     weights_start(meta, pieces, kernel, sem, block)
     for slot in range(PAIR):
         value = ext[slot * EXT : (slot + 1) * EXT].astype(F32)
@@ -607,7 +647,7 @@
 
 
 def dgrad_body(block, meta, ext, *rest):
-    pieces, out, (kernel, sem) = rest[:8], rest[8], rest[9:]
+    pieces, out, (kernel, sem) = rest[:4], rest[4], rest[5:]
     weights_start(meta, pieces, kernel, sem, block)
     versions = []
     for slot in range(PAIR):
@@ -631,45 +671,65 @@
             out[...] += part
 
 
-def wgrad_body(block, meta, ext, grad, keep, send, patch, result):
-    core = meta[M_DEV] % 2
-    low = jnp.concatenate(
-        [
-            grad[slot * EXT + WID : slot * EXT + WID + PIX] * own_mask(meta, slot).astype(BF)
-            for slot in range(PAIR)
-        ],
-        axis=0,
-    )
+def wgrad_body(block, task, meta, ext, ext_far, grad, grad_far, *rest):
+    keep_out, send_out, patch, result, keep, send, sems = rest[-7:]
+    device = meta[M_DEV]
+    core = device & 1
+    half = C // 2
+    lows = []
+    for ref in (grad, grad_far):
+        for slot in range(PAIR):
+            value = ref[slot * EXT + WID : slot * EXT + WID + PIX]
+            value = jnp.where(core == 0, value[:, :half], value[:, half:])
+            lows.append(value * own_mask(meta, slot, half).astype(BF))
+    low = jnp.concatenate(lows, axis=0)
     rows = 16 * block
 
-    def half(top):
+    def work(top):
         first_tap = (top * rows) // C
-        for slot in range(PAIR):
-            value = ext[slot * EXT : (slot + 1) * EXT].astype(F32)
-            versions = column_versions(meta, slot, value)
-            for i in range(5):
-                tap = first_tap + i
-                start = WID * (tap // 3)
-                patch[slot * PIX : (slot + 1) * PIX, i * C : (i + 1) * C] = versions[tap % 3][
-                    start : start + PIX
-                ]
+        for source, ref in enumerate((ext, ext_far)):
+            for slot in range(PAIR):
+                value = ref[slot * EXT : (slot + 1) * EXT].astype(F32)
+                versions = column_versions(meta, slot, value)
+                base = (source * PAIR + slot) * PIX
+                for i in range(5):
+                    tap = first_tap + i
+                    start = WID * (tap // 3)
+                    patch[base : base + PIX, i * C : (i + 1) * C] = versions[tap % 3][
+                        start : start + PIX
+                    ]
         lane = top * rows - first_tap * C
         result[...] = lax.dot_general(
             patch[:, lane : lane + rows], low, (((0,), (0,)), ((), ())), preferred_element_type=F32
         )
 
     for top in range(2):
-        pl.when(meta[M_TOP] == top)(functools.partial(half, top))
-    for j in range(8):
-        y, x, a = j & 1, (j >> 1) & 1, (j >> 2) & 1
-        place = x * 4 + y * 2 + a
-        at = pl.multiple_of((2 * j + core) * block, 16)
+        pl.when(meta[M_TOP] == top)(functools.partial(work, top))
+    weight_one = jnp.where(core == 0, 4, 2)
+    weight_two = 6 - weight_one
+    bit_one = jnp.where((device & weight_one) > 0, 1, 0)
+    bit_two = jnp.where((device & weight_two) > 0, 1, 0)
+    bit_low = (device >> 3) & 1
+    for place in range(8):
+        two = bit_two ^ (place >> 2)
+        low_z = bit_low ^ ((place >> 1) & 1)
+        base = (core ^ (place & 1)) + 8 * low_z + weight_two * two
+        at = pl.multiple_of((base + weight_one * bit_one) * block, 16)
         keep[place] = result[pl.ds(at, block)]
-        at = pl.multiple_of((2 * j + 1 - core) * block, 16)
-        send[place] = result[pl.ds(at, block)]
-
-
-def squeeze_body(meta, z1, s1, rec1, rec2, affine, down, a1, hidden, stats, ext):
+        at = pl.multiple_of((base + weight_one * (1 - bit_one)) * block, 16)
+        send[place] = result[pl.ds(at, block)].astype(BF)
+    copies = (
+        pltpu.make_async_copy(keep, keep_out.at[task], sems.at[0]),
+        pltpu.make_async_copy(send, send_out.at[task], sems.at[1]),
+    )
+    for copy in copies:
+        copy.start()
+    for copy in copies:
+        copy.wait()
+
+
+def squeeze_body(meta, z1, s1, rec1, rec2, affine, down, a1_out, hidden, stats, ext):
+    a1 = a1_out.at[0]
     total = total_of(meta)
     mean, inverse, gain, bias = norm_terms(s1, 0, 0, C, affine, 0, total)
 
@@ -718,7 +778,7 @@
         stats[3 + 2 * task : 4 + 2 * task] = second
 
 
-def select_body(meta, z2, rec1, rec2, stats, expanded, affine, sel0, sel1, sel2, ext):
+def select_body(meta, z2, rec1, rec2, stats, expanded, affine, selected, ext):
     total = total_of(meta)
     mean, inverse, gain, bias = norm_terms(stats, 0, 0, C, affine, C, total)
 
@@ -729,14 +789,14 @@
     up, dn = act(up), act(dn)
     for slot in range(PAIR):
         put_ext(meta, ext, slot, act(z2[slot * PIX : (slot + 1) * PIX]), up, dn)
-    for task, sel in enumerate((sel0, sel1, sel2)):
+    for task in range(TASK_COUNT):
         terms = norm_terms(stats, 2 + 2 * task, 0, C, affine, UP_AT + task * C, total)
         mean_u, inverse_u, gain_u, bias_u = terms
         for slot in range(PAIR):
             at = slice(slot * EXT, (slot + 1) * EXT)
             pre = (expanded[task, at] - mean_u) * inverse_u * gain_u + bias_u
             gate = jax.nn.sigmoid(pre)
-            sel[at] = (gate * (ext[at] * outer_mask(meta, slot))).astype(BF)
+            selected[task, at] = (gate * (ext[at] * outer_mask(meta, slot))).astype(BF)
 
 
 def spread_matrix(rows_out, first_row, cells):
@@ -788,11 +848,11 @@
 
 
 def task_grad_body(
-    meta, lam, z30, z31, z32, rec1, rec2, stats, back, cot, affine, out0, out1, out2, ext
+    meta, lam, z30, z31, z32, rec1, rec2, stats, back, cot, affine, out, ext
 ):
     total = total_of(meta)
     spread = spread_matrix(EXT, 0, cot.shape[2])
-    for task, (z3, out) in enumerate(((z30, out0), (z31, out1), (z32, out2))):
+    for task, z3 in enumerate((z30, z31, z32)):
         mean, inverse, gain, bias = norm_terms(
             stats, 2 * task, 0, C, affine, CONV_AT + task * C, total
         )
@@ -807,7 +867,7 @@
             seed = jnp.dot(spread, cot[task, slot], preferred_element_type=F32)
             grad = slope * (seed * (lam[task] * 0.25))
             value = (gain * inverse) * (grad - (dbias + normed * dgain) / total)
-            out[at] = jnp.where(outer_mask(meta, slot) > 0, value, 0.0).astype(BF)
+            out[task, at] = jnp.where(outer_mask(meta, slot) > 0, value, 0.0).astype(BF)
 
 
 def branch_grad_body(
@@ -906,7 +966,7 @@
         at = slice(slot * EXT, (slot + 1) * EXT)
         normed = (zext[at] - mean) * inverse
         value = (gain * inverse) * (gext[at] - (dbias + normed * dgain) / total)
-        out[at] = jnp.where(outer_mask(meta, slot) > 0, value, 0.0).astype(BF)
+        out[0, at] = jnp.where(outer_mask(meta, slot) > 0, value, 0.0).astype(BF)
 
 
 def squeeze_grad_body(
@@ -947,7 +1007,7 @@
 CONV_FLOPS = 2 * PAIR * PIX * 9 * C * C
 
 
-def conv_call(meta, ext, pieces, block):
+def conv_call(meta, ext, entry, pieces, block, deps=()):
     shapes = [sds((PAIR * PIX, C)), sds((8, C)), sds((PAIR * WID, C)), sds((PAIR * WID, C))]
     scratch = [
         pltpu.VMEM((9 * C, C), BF),
@@ -956,24 +1016,58 @@
     ]
     return kernel_call(
         functools.partial(conv_body, block), shapes, (meta, ext) + tuple(pieces),
-        "sv" + "a" * 8, scratch, CONV_FLOPS, "conv",
-    )
-
-
-def dgrad_call(meta, ext, pieces, block):
+        ("s", entry) + ("a",) * 4, scratch, CONV_FLOPS, "conv", deps,
+    )
+
+
+def dgrad_call(meta, ext, entry, pieces, block, deps=()):
     scratch = [pltpu.VMEM((9 * C, C), BF), pltpu.SemaphoreType.DMA]
     return kernel_call(
         functools.partial(dgrad_body, block), [sds((PAIR * PIX, C))],
-        (meta, ext) + tuple(pieces), "sv" + "a" * 8, scratch, CONV_FLOPS, "dgrad",
+        (meta, ext) + tuple(pieces), ("s", entry) + ("a",) * 4, scratch, CONV_FLOPS, "dgrad", deps,
     )[0]
 
 
-def wgrad_call(meta, ext, grad, block):
-    scratch = [pltpu.VMEM((PAIR * PIX, 5 * C), BF), pltpu.VMEM((16 * block, C), F32)]
+def wgrad_call(meta, ext, ext_far, grad, grad_far, block, count=1, task=0, into=None, deps=()):
+    half = C // 2
+    shapes = [sds((count, 8, block, half)), sds((count, 8, block, half), BF)]
+    scratch = [
+        pltpu.VMEM((2 * PAIR * PIX, 5 * C), BF),
+        pltpu.VMEM((16 * block, half), F32),
+        pltpu.VMEM((8, block, half), F32),
+        pltpu.VMEM((8, block, half), BF),
+        pltpu.SemaphoreType.DMA((2,)),
+    ]
+    args, places, alias = (meta, ext, ext_far, grad, grad_far), ("s",) + (task,) * 4, {}
+    if into is not None:
+        args, places, alias = args + tuple(into), places + ("a", "a"), {5: 0, 6: 1}
     return kernel_call(
-        functools.partial(wgrad_body, block), [sds((8, block, C)), sds((8, block, C))],
-        (meta, ext, grad), "svv", scratch, CONV_FLOPS // 2, "wgrad",
-    )
+        functools.partial(wgrad_body, block, task), shapes, args, places, scratch,
+        CONV_FLOPS // 2, "wgrad", deps, "aa", alias,
+    )
+
+
+def merge(parts, rows, deps=(), name="merge"):
+    spans, args, place = [], [], 0
+    for part in parts:
+        if isinstance(part, tuple):
+            spans.append((len(args), part[1], rows, place))
+            args.append(part[0])
+            place += 1
+        else:
+            spans.append((len(args), None, part.shape[0], place))
+            args.append(part)
+            place += part.shape[0]
+    return kernel_call(
+        functools.partial(merge_body, tuple(spans)),
+        [sds((place, rows, C // 2), BF)],
+        tuple(args),
+        "a" * len(args),
+        [pltpu.SemaphoreType.DMA((len(spans),))],
+        name=name,
+        deps=deps,
+        outs="a",
+    )[0]
 
 
 def sync(stats, edge1=None, edge2=None):
@@ -992,56 +1086,46 @@
     return stats, first, second
 
 
-def gather_pieces(shard):
-    half = C // 2
-    two = jnp.stack([shard, swap(shard, 16)])
-    four = jnp.concatenate([two, swap(two, 8)])
-    left, right = four[:, :, :half], four[:, :, half:]
-    left8 = jnp.concatenate([left, swap(left, 4)])
-    right8 = jnp.concatenate([right, swap(right, 2)])
-    left_far, right_far = swap(left8, 2), swap(right8, 4)
-    return (
-        left8, left_far, swap(left8, 1), swap(left_far, 1),
-        right8, right_far, swap(right8, 1), swap(right_far, 1),
-    )
-
-
 def attention_rows(pieces, block, me):
-    tails = [p[:, block:] for p in pieces]
-    left = jnp.concatenate(tails[:4])
-    right = jnp.concatenate(tails[4:])
-    base_a = [x * 4 + a * 8 + b * 16 for x in range(2) for a in range(2) for b in range(2)]
-    base_b = [y * 2 + a * 8 + b * 16 for y in range(2) for a in range(2) for b in range(2)]
-    order_a = [m ^ e for e in (0, 2, 1, 3) for m in base_a]
-    order_b = [m ^ e for e in (0, 4, 1, 5) for m in base_b]
-    spot_a = [order_a.index(m) for m in range(32)]
-    spot_b = [order_b.index(m) for m in range(32)]
-    owners = me ^ jnp.arange(32)
-    left = jnp.take(left, jnp.array(spot_a)[owners], axis=0)
-    right = jnp.take(right, jnp.array(spot_b)[owners], axis=0)
-    return jnp.concatenate([left, right], axis=-1)
-
-
-def pick(value, index):
-    return lax.dynamic_index_in_dim(value, index, 0, keepdims=False)
-
-
-def scatter_sum(keep, send, bits, x_first):
-    total = keep + swap(send, 1)
-    x, y, a = bits
-    rows = total.shape[1:]
-    if x_first:
-        total = total.reshape((2, 4) + rows)
-        total = pick(total, x) + swap(pick(total, 1 - x).astype(BF), 4).astype(F32)
-        total = total.reshape((2, 2) + rows)
-        total = pick(total, y) + swap(pick(total, 1 - y).astype(BF), 2).astype(F32)
-    else:
-        total = total.reshape((2, 2, 2) + rows)
-        total = lax.dynamic_index_in_dim(total, y, 1, keepdims=False) + swap(
-            lax.dynamic_index_in_dim(total, 1 - y, 1, keepdims=False).astype(BF), 2
-        ).astype(F32)
-        total = pick(total, x) + swap(pick(total, 1 - x).astype(BF), 4).astype(F32)
-    return pick(total, a) + swap(pick(total, 1 - a).astype(BF), 8).astype(F32)
+    tails = jnp.concatenate([p[:, block:] for p in pieces])
+    owner = jnp.arange(32)
+    spots = []
+    for column in range(2):
+        far_core = (me & 1) ^ column
+        device = me ^ far_core
+        relative = device ^ owner
+        near = 4 if column == 0 else 2
+        spot = (
+            (relative & 1)
+            + 2 * ((relative >> 4) & 1)
+            + 4 * ((relative >> 3) & 1)
+            + 8 * jnp.where((relative & near) > 0, 1, 0)
+            + 16 * jnp.where((relative & (6 - near)) > 0, 1, 0)
+            + 32 * far_core
+        )
+        spots.append(spot)
+    return jnp.concatenate([jnp.take(tails, spot, axis=0) for spot in spots], axis=-1)
+
+
+def scatter_stage(keep, send, even, odd):
+    got = swap(send, even, odd)
+    half = keep.shape[1] // 2
+    send = (keep[:, half:] + got[:, half:].astype(F32)).astype(BF)
+    return keep[:, :half] + got[:, :half].astype(F32), send
+
+
+def scatter_last(keep, send):
+    return keep + swap(send, 8).astype(F32)
+
+
+def join_columns(total, core):
+    got = swap(total[:, 1], 1)
+    mine = total[:, 0]
+    return jnp.where(
+        core == 0,
+        jnp.concatenate([mine, got], axis=-1),
+        jnp.concatenate([got, mine], axis=-1),
+    )
 
 
 def order_pair(own, other, top):
@@ -1050,31 +1134,29 @@
     )
 
 
-def image_ext(images, rows, band):
+def with_rims(images, cotangent, rows, band):
     valid = (jnp.arange(BAND) < rows).astype(BF)[:, None, None]
     own = images[0] * valid
-    last = lax.dynamic_index_in_dim(own, rows - 1, 0, keepdims=False)
+    seed = cotangent[:, 0]
+    cells = seed.shape[2]
+    last = jnp.concatenate(
+        [
+            lax.dynamic_index_in_dim(own, rows - 1, 0, keepdims=False),
+            lax.dynamic_index_in_dim(seed, rows // 2 - 1, 1, keepdims=False).reshape(-1, C),
+        ]
+    )
+    head = jnp.concatenate([own[0], seed[:, 0].reshape(-1, C)])
     odd = band % 2 == 1
-    first = swap(jnp.where(odd, own[0], last), 1)
-    second = swap(jnp.where(odd, last, own[0]), 3)
+    first = swap(jnp.where(odd, head, last), 1)
+    second = swap(jnp.where(odd, last, head), 3)
     up = jnp.where(band > 0, jnp.where(odd, first, second), 0)
     down = jnp.where(band < 3, jnp.where(odd, second, first), 0)
-    ext = jnp.concatenate([up[None], own, jnp.zeros_like(up)[None]])
-    ext = lax.dynamic_update_index_in_dim(ext, down, rows + 1, 0)
-    return ext.reshape(EXT, C)
-
-
-def cotangent_ext(cotangent, rows, band):
-    own = cotangent[:, 0]
-    last = lax.dynamic_index_in_dim(own, rows // 2 - 1, 1, keepdims=False)
-    odd = band % 2 == 1
-    first = swap(jnp.where(odd, own[:, 0], last), 1)
-    second = swap(jnp.where(odd, last, own[:, 0]), 3)
-    up = jnp.where(odd, first, second)
-    down = jnp.where(odd, second, first)
-    ext = jnp.concatenate([up[:, None], own, jnp.zeros_like(up)[:, None]], axis=1)
-    ext = lax.dynamic_update_index_in_dim(ext, down, rows // 2 + 1, 1)
-    return ext.reshape(TASK_COUNT, -1, C)
+    pixels = jnp.concatenate([up[None, :WID], own, jnp.zeros_like(up)[None, :WID]])
+    pixels = lax.dynamic_update_index_in_dim(pixels, down[:WID], rows + 1, 0)
+    up, down = (v[WID:].reshape(TASK_COUNT, cells, C) for v in (up, down))
+    seeds = jnp.concatenate([up[:, None], seed, jnp.zeros_like(up)[:, None]], axis=1)
+    seeds = lax.dynamic_update_index_in_dim(seeds, down, rows // 2 + 1, 1)
+    return pixels.reshape(EXT, C), seeds.reshape(TASK_COUNT, -1, C)
 
 
 def local_pairs(
@@ -1098,10 +1180,21 @@
     me = slot * 4 + band
     top = slot // 4
     low_slot = slot % 4
+    core = me & 1
+    half = C // 2
     block = kernels.shape[2] // C
     kernel_low = kernels[0].astype(BF).reshape(2 + TASK_COUNT, block, C)
-    attend_low = attention[0].astype(BF)
-    extra = attend_low.size // C
+    attend_low = attention[0].astype(BF).reshape(-1, C)
+    extra = attend_low.shape[0]
+    shard = jnp.concatenate(
+        [kernel_low[:2].reshape(-1, C), attend_low, kernel_low[2:].reshape(-1, C)]
+    )
+    shard_mine = jnp.where(core == 0, shard[:, :half], shard[:, half:])
+    shard_rest = jnp.where(core == 0, shard[:, half:], shard[:, :half])
+    shard_got = swap(shard_rest, 1)
+    starts = [0, block] + [(2 + t) * block + extra for t in range(TASK_COUNT)]
+    counts = [block, block + extra] + [block] * TASK_COUNT
+
     rows_pair = jnp.stack([heights[low_slot], heights[low_slot + 4]]) // 4
     group_pair = jnp.stack([groups[low_slot], groups[low_slot + 4]])
     meta = jnp.concatenate(
@@ -1110,18 +1203,38 @@
     lam = TASK_COUNT * jax.nn.softmax(ratios / SOFTMAX_TEMP)
     own_rows = heights[slot] // 4
 
-    own_ext = image_ext(images, own_rows, band)
-    x0 = order_pair(own_ext, swap(own_ext, TOP), top)
-    pieces = [gather_pieces(kernel_low[0])]
-    pieces.append(
-        gather_pieces(jnp.concatenate([kernel_low[1], attend_low.reshape(extra, C)], axis=0))
-    )
-    for k in range(2, 2 + TASK_COUNT):
-        pieces.append(gather_pieces(kernel_low[k]))
-    own_cot = cotangent_ext(task_cotangent, own_rows, band)
+    def near_chips(k, deps=()):
+        chip = merge([(shard_mine, starts[k]), (shard_got, starts[k])], counts[k], deps)
+        got = swap(chip, 16)
+        four = merge([chip, got], counts[k])
+        return got, four, swap(four, 8)
+
+    def far_chips(k, four, got, deps=(), late=()):
+        eight = merge([four, got], counts[k], deps)
+        sixteen = merge([eight, swap(eight, 4, 2)], counts[k], late)
+        far = swap(sixteen, 2, 4)
+        return sixteen, far
+
+    def both_cores(sixteen, far):
+        return sixteen, far, swap(sixteen, 1), swap(far, 1)
+
+    z_got, z_four, z_eight = near_chips(0)
+    own_ext, own_cot = with_rims(images, task_cotangent, own_rows, band)
+    x0 = order_pair(own_ext, swap(own_ext, TOP), top)[None]
     cot = jnp.moveaxis(order_pair(own_cot[None], swap(own_cot, TOP)[None], top), 0, 1)
-
-    z1, st, e1, e2 = conv_call(meta, x0, pieces[0], block)
+    reached = far_chips(0, z_four, z_eight)
+    pieces = [both_cores(*reached)]
+    z_next = near_chips(1, (z_got,))
+
+    z1, st, e1, e2 = conv_call(meta, x0.reshape(1, PAIR * EXT, C), 0, pieces[0], block)
+    x0 = x0.reshape(1, PAIR * EXT, C)
+    for k in range(1, 2 + TASK_COUNT):
+        z_got, z_four, z_eight = z_next
+        if k < 1 + TASK_COUNT:
+            z_next = near_chips(k + 1, (z_got,))
+        reached = far_chips(k, z_four, z_eight, (reached[1],), (st,) if k == 1 else ())
+        pieces.append(both_cores(*reached))
+
     s1, z1r1, z1r2 = sync(st, e1, e2)
     tails = attention_rows(pieces[1], block, me)
     kind_rows = extra // 2
@@ -1129,7 +1242,7 @@
     up_w = tails[:, kind_rows:].reshape(TASK_COUNT, B, C)
     a1, hidden, hst = kernel_call(
         squeeze_body,
-        [sds((PAIR * EXT, C), BF), sds((PAIR * EXT, HIDDEN)), sds((8, C))],
+        [sds((1, PAIR * EXT, C), BF), sds((PAIR * EXT, HIDDEN)), sds((8, C))],
         (meta, z1, s1, z1r1, z1r2, affine, down),
         "svvvvvv",
         [pltpu.VMEM((PAIR * EXT, C), F32)],
@@ -1137,7 +1250,7 @@
         "squeeze",
     )
     hstats, _, _ = sync(hst)
-    z2, st2, e1, e2 = conv_call(meta, a1, pieces[1], block)
+    z2, st2, e1, e2 = conv_call(meta, a1, 0, pieces[1], block)
     squeezed, expanded, ust = kernel_call(
         expand_body,
         [sds((PAIR * EXT, HIDDEN), BF), sds((TASK_COUNT, PAIR * EXT, C)), sds((8, C))],
@@ -1149,18 +1262,19 @@
     s2, z2r1, z2r2 = sync(st2 + ust, e1, e2)
     selected = kernel_call(
         select_body,
-        [sds((PAIR * EXT, C), BF)] * TASK_COUNT,
+        [sds((TASK_COUNT, PAIR * EXT, C), BF)],
         (meta, z2, z2r1, z2r2, s2, expanded, affine),
         "svvvvvv",
         [pltpu.VMEM((PAIR * EXT, C), F32)],
         name="select",
-    )
+    )[0]
     z3, st3, e31, e32 = zip(
-        *[conv_call(meta, selected[t], pieces[2 + t], block) for t in range(TASK_COUNT)]
+        *[conv_call(meta, selected, t, pieces[2 + t], block) for t in range(TASK_COUNT)]
     )
     s3, _, _ = sync(jnp.concatenate([s[:2] for s in st3] + [jnp.zeros((2, C), F32)]))
     z3r1 = swap(jnp.concatenate(e31), 1)
     z3r2 = swap(jnp.concatenate(e32), 3)
+    x0_far, a1_far, selected_far = swap(x0, 1), swap(a1, 1), swap(selected, 1)
     pooled, bst = kernel_call(
         pool_body,
         [sds((TASK_COUNT, PIX // 4, C)), sds((8, C))],
@@ -1171,13 +1285,14 @@
     b3, _, _ = sync(bst)
     dz3 = kernel_call(
         task_grad_body,
-        [sds((PAIR * EXT, C), BF)] * TASK_COUNT,
+        [sds((TASK_COUNT, PAIR * EXT, C), BF)],
         (meta, lam) + z3 + (z3r1, z3r2, s3, b3, cot, affine),
         "ssvvvvvvvvv",
         [pltpu.VMEM((PAIR * EXT, C), F32)],
         name="task_grad",
-    )
-    ds = [dgrad_call(meta, dz3[t], pieces[2 + t], block) for t in range(TASK_COUNT)]
+    )[0]
+    dz3_far = swap(dz3, 1)
+    ds = [dgrad_call(meta, dz3, t, pieces[2 + t], block) for t in range(TASK_COUNT)]
     dpu, dp2, bst, e1, e2 = kernel_call(
         branch_grad_body,
         [
@@ -1192,6 +1307,12 @@
         name="branch_grad",
     )
     b2, dp2r1, dp2r2 = sync(bst, e1, e2)
+    sums = None
+    for t in range(TASK_COUNT):
+        sums = wgrad_call(
+            meta, selected, selected_far, dz3, dz3_far, block, TASK_COUNT, t, sums, (bst,)
+        )
+    task_keep, task_send = scatter_stage(*sums, 4, 2)
     dup, dph, hbst = kernel_call(
         expand_grad_body,
         [sds((TASK_COUNT, B, C)), sds((PAIR * PIX, HIDDEN)), sds((8, C))],
@@ -1199,18 +1320,20 @@
         "svvvvvvvvv",
         flops=4 * PAIR * PIX * C * HIDDEN,
         name="expand_grad",
+        deps=(sums[1],),
     )
     hback, _, _ = sync(hbst)
     ext_scratch = [pltpu.VMEM((PAIR * EXT, C), F32), pltpu.VMEM((PAIR * EXT, C), F32)]
     dz2 = kernel_call(
         functools.partial(norm_grad_body, C),
-        [sds((PAIR * EXT, C), BF)],
+        [sds((1, PAIR * EXT, C), BF)],
         (meta, dp2, dp2r1, dp2r2, z2, z2r1, z2r2, s2, b2, affine),
         "svvvvvvvvv",
         ext_scratch,
         name="norm_grad",
     )[0]
-    da1 = dgrad_call(meta, dz2, pieces[1], block)
+    dz2_far = swap(dz2, 1)
+    da1 = dgrad_call(meta, dz2, 0, pieces[1], block)
     dp1, bst, e1, e2, ddown = kernel_call(
         squeeze_grad_body,
         [
@@ -1220,44 +1343,54 @@
             sds((PAIR * WID, C)),
             sds((C, HIDDEN)),
         ],
-        (meta, dph, hidden, hstats, hback, down, a1, da1, z1, s1, affine),
+        (meta, dph, hidden, hstats, hback, down, a1.reshape(PAIR * EXT, C), da1, z1, s1, affine),
         "svvvvvvvvvv",
         flops=4 * PAIR * PIX * C * HIDDEN,
         name="squeeze_grad",
     )
     b1, dp1r1, dp1r2 = sync(bst, e1, e2)
+    keep, send = wgrad_call(meta, a1, a1_far, dz2, dz2_far, block, deps=(bst,))
     dz1 = kernel_call(
         functools.partial(norm_grad_body, 0),
-        [sds((PAIR * EXT, C), BF)],
+        [sds((1, PAIR * EXT, C), BF)],
         (meta, dp1, dp1r1, dp1r2, z1, z1r1, z1r2, s1, b1, affine),
         "svvvvvvvvv",
         ext_scratch,
         name="norm_grad",
+        deps=(task_send, send),
     )[0]
-    dx = dgrad_call(meta, dz1, pieces[0], block)
+    dz1_far = swap(dz1, 1)
+    first_sums = wgrad_call(meta, x0, x0_far, dz1, dz1_far, block)
+    dx = dgrad_call(meta, dz1, 0, pieces[0], block, (first_sums[1],))
     image_grad = lax.dynamic_slice_in_dim(dx, top * PIX, PIX, 0).reshape(1, BAND, WID, C)
     valid = (jnp.arange(BAND) < own_rows).astype(F32)[None, :, None, None]
     image_grad = image_grad * valid
 
-    bits = ((me >> 2) & 1, (me >> 1) & 1, (me >> 3) & 1)
-    inputs = (x0, a1) + tuple(selected)
-    grads = (dz1, dz2) + tuple(dz3)
-    shards = [None] * (2 + TASK_COUNT)
-    for k in (2, 3, 4, 1, 0):
-        keep, send = wgrad_call(meta, inputs[k], grads[k], block)
-        shards[k] = scatter_sum(keep, send, bits, k % 2 == 0)
+    task_sums = scatter_last(*scatter_stage(task_keep, task_send, 2, 4))
+    task_shards = join_columns(task_sums, core)
 
     ddown = ddown.reshape(C, TASK_COUNT, B).transpose(1, 0, 2)
-    attend = jnp.stack([ddown.reshape(-1), dup.reshape(-1)]).reshape(2, 2, 2, 2, 2, 2, -1)
+    attend = jnp.stack([ddown.reshape(-1), dup.reshape(-1)]).reshape(2, 2, 16, -1, C)
     attend = lax.dynamic_index_in_dim(attend, top, 1, keepdims=False)
-    attend = attend.transpose(2, 3, 1, 4, 0, 5).reshape(2, 2, 2, 2, -1, C)
-    attend = attend.reshape(8, 2, -1, C)
-    core = me & 1
-    keep = lax.dynamic_index_in_dim(attend, core, 1, keepdims=False)
-    send = lax.dynamic_index_in_dim(attend, 1 - core, 1, keepdims=False)
-    attend_shard = scatter_sum(keep, send, bits, True).reshape(1, 2, -1)
-
-    kernel_shard = jnp.stack(shards).reshape(1, 2 + TASK_COUNT, -1)
+    attend = attend.transpose(1, 0, 2, 3).reshape(16, -1, C)
+    mine = jnp.where(core == 0, attend[..., :half], attend[..., half:])
+    rest = jnp.where(core == 0, attend[..., half:], attend[..., :half])
+    attend = mine + swap(rest, 1)
+    spot = jnp.arange(16)
+    near = jnp.where(core == 0, 4, 2)
+    order = (
+        (spot & 1) + 8 * ((spot >> 1) & 1) + (6 - near) * ((spot >> 2) & 1) + near * (spot >> 3)
+    )
+    attend = jnp.take(attend, order ^ (me & 15), axis=0).reshape(2, 1, 8, -1, half)
+    keep = jnp.concatenate([keep, attend[0]], axis=2)
+    send = jnp.concatenate([send, attend[1].astype(BF)], axis=2)
+    second = scatter_last(*scatter_stage(*scatter_stage(keep, send, 4, 2), 2, 4))
+    second = join_columns(second, core)
+    attend_shard = second[0, block:].reshape(1, 2, -1)
+    first = scatter_last(*scatter_stage(*scatter_stage(*first_sums, 4, 2), 2, 4))
+    first = join_columns(first, core)
+    kernel_shard = jnp.concatenate([first, second[:, :block], task_shards])
+    kernel_shard = kernel_shard.reshape(1, 2 + TASK_COUNT, -1)
     gain_grads = jnp.concatenate(
         [b1[0], b2[0], hback[0, :HIDDEN], b2[2], b2[4], b2[6], b3[0], b3[2], b3[4]]
     )

time: 535 us -> 897 us (1.68)
  Pallas kernels: 131 us -> 495 us
  waiting for transfers between devices: 179 us -> 214 us
  starting transfers between devices: 83.9 us -> 55.9 us
  other arithmetic: 75.8 us -> 52.8 us
  local copies, waits for them, and re-layouts: 54.2 us -> 67.9 us
    pallas_call x25 -> x45, Pallas kernels: 131 us -> 495 us  [kernel_call(): pl.pallas_call(run, out_shape=out_shapes, grid=grid, in_specs=[spec(p, a)...]
    ppermute x114 -> x88, waiting for transfers between devices: 179 us -> 214 us  [swap(): return lax.ppermute(value, AXES, pairs)]
    ppermute x114 -> x88, starting transfers between devices: 83.9 us -> 55.9 us  [swap(): return lax.ppermute(value, AXES, pairs)]
    unnamed x189 -> x157, local copies, waits for them, and re-layouts: 8.59 us -> 26.4 us
    add x24 -> x5, other arithmetic: 20.3 us -> 4.52 us  [the longest x1 2.82 us: scatter_stage(): return (keep[:, :half] + got[:, :half].astype(F32), send)]
  transfers between devices with their start and end apart: 114 -> 88, of which waited for: 43 -> 47; matrix products, arithmetic and copies ran while one was open for 19% -> 9% of each run, Pallas kernels for 19% -> 29%
where the time goes in v2:
time: 897 us; the launch traced here: 890 us
  Pallas kernels  495 us (55%)
  waiting for transfers between devices  214 us (24%)
  local copies, waits for them, and re-layouts  67.9 us (8%)
  starting transfers between devices  55.9 us (6%)
  other arithmetic  52.8 us (6%)
    pallas_call x45, Pallas kernels, kernel_call(): pl.pallas_call(run, out_shape=out_shapes, grid=grid, in_specs=[spec(p, a)...  495 us
    ppermute x88, waiting for transfers between devices, swap(): return lax.ppermute(value, AXES, pairs)  214 us
    ppermute x88, starting transfers between devices, swap(): return lax.ppermute(value, AXES, pairs)  55.9 us
    unnamed x157, local copies, waits for them, and re-layouts  26.4 us
  transfers between devices with their start and end apart: 88, of which 47 were waited for; matrix products, arithmetic and copies ran while one was open for 9% of the time, Pallas kernels for 29%

profile of v2, /device:TPU:0, one launch (start us, length us, event | category | flops | bytes accessed | tf_op | source)
XLA Modules:
  0.0 890.5 jit_solution(5516775996554018294)
XLA Ops:
  12.1 5.6 merge.20.refs_0_
  21.7 7.5 collective-permute-done.4.refs_1_.refs_2_
  29.9 10.1 %merge.21.refs_0_ = bf16[4,144,256]{2,1,0:T(8,128)(2,1)} custom-call(bf16[2,144,256]{2,1,0:T(8,128)(2,1)} %merge.20.refs_0_, bf16[2,144,256]{2,1,0:T(8,128)(2,1)} %copy-done.28), custom_call_target="tpu_custom_call" | custom-call | bytes 589824 | tf_op jit(solution)/shard_map/merge/pallas_call | solution.py:475
  40.9 7.9 collective-permute-done.5.refs_1_
  49.6 19.0 %merge.22.refs_0_ = bf16[8,144,256]{2,1,0:T(8,128)(2,1)} custom-call(bf16[4,144,256]{2,1,0:T(8,128)(2,1)} %merge.21.refs_0_, bf16[4,144,256]{2,1,0:T(8,128)(2,1)} %copy-done.35), custom_call_target="tpu_custom_call" | custom-call | bytes 1179648 | tf_op jit(solution)/shard_map/merge/pallas_call | solution.py:475
  69.8 8.9 collective-permute-done.6.refs_1_
  79.5 36.9 %merge.23.refs_2_ = bf16[16,144,256]{2,1,0:T(8,128)(2,1)} custom-call(bf16[8,144,256]{2,1,0:T(8,128)(2,1)} %merge.22.refs_0_, bf16[8,144,256]{2,1,0:T(8,128)(2,1)} %copy-done.26), custom_call_target="tpu_custom_call" | custom-call | bytes 2359296 | tf_op jit(solution)/shard_map/merge/pallas_call | solution.py:475
  121.8 6.3 merge.24.refs_0_
  138.7 11.5 %merge.25.refs_0_ = bf16[4,168,256]{2,1,0:T(8,128)(2,1)} custom-call(bf16[2,168,256]{2,1,0:T(8,128)(2,1)} %merge.24.refs_0_, bf16[2,168,256]{2,1,0:T(8,128)(2,1)} %copy-done.22), custom_call_target="tpu_custom_call" | custom-call | bytes 688128 | tf_op jit(solution)/shard_map/merge/pallas_call | solution.py:475
  152.4 7.1 collective-permute-done.15.refs_1_
  160.3 22.0 %merge.26.refs_0_ = bf16[8,168,256]{2,1,0:T(8,128)(2,1)} custom-call(bf16[4,168,256]{2,1,0:T(8,128)(2,1)} %merge.25.refs_0_, bf16[4,168,256]{2,1,0:T(8,128)(2,1)} %copy-done.31, bf16[16,144,256]{2,1,0:T(8,128)(2,1)} %copy-done.11), custom_call_target="tpu_custom_call" | custom-call | bytes 1376256 | tf_op jit(solution)/shard_map/merge/pallas_call | solution.py:475
  199.1 5.7 conv.5
  204.8 42.8 %merge.27.refs_2_ = bf16[16,168,256]{2,1,0:T(8,128)(2,1)} custom-call(bf16[8,168,256]{2,1,0:T(8,128)(2,1)} %merge.26.refs_0_, bf16[8,168,256]{2,1,0:T(8,128)(2,1)} %collective-permute-done.16.refs_1_, f32[8,512]{1,0:T(8,128)} %get-tuple-element.64.refs_2_), custom_call_target="tpu_custom_call" | custom-call | bytes 2752512 | tf_op jit(solution)/shard_map/merge/pallas_call | solution.py:475
  254.2 9.3 %collective-permute-done.28.refs_1_.refs_2_ = bf16[2,144,256]{2,1,0:T(8,128)(2,1)S(1)} collective-permute-done((bf16[2,144,256]{2,1,0:T(8,128)(2,1)}, bf16[2,144,256]{2,1,0:T(8,128)(2,1)S(1)}, u32[]{:S(2)}, u32[]{:S(2)}) %collective-permute-start.28) | collective-permute-done | bytes 147488 | tf_op jit(solution)/shard_map/ppermute | solution.py:453
  264.2 10.1 %merge.29.refs_0_ = bf16[4,144,256]{2,1,0:T(8,128)(2,1)} custom-call(bf16[2,144,256]{2,1,0:T(8,128)(2,1)} %merge.28.refs_0_, bf16[2,144,256]{2,1,0:T(8,128)(2,1)} %copy-done.30), custom_call_target="tpu_custom_call" | custom-call | bytes 589824 | tf_op jit(solution)/shard_map/merge/pallas_call | solution.py:475
  274.3 8.2 collective-permute-done.29.refs_1_
  284.3 19.0 %merge.30.refs_0_ = bf16[8,144,256]{2,1,0:T(8,128)(2,1)} custom-call(bf16[4,144,256]{2,1,0:T(8,128)(2,1)} %merge.29.refs_0_, bf16[4,144,256]{2,1,0:T(8,128)(2,1)} %copy-done.33, bf16[16,168,256]{2,1,0:T(8,128)(2,1)} %copy-done.5), custom_call_target="tpu_custom_call" | custom-call | bytes 1179648 | tf_op jit(solution)/shard_map/merge/pallas_call | solution.py:475
  305.5 8.1 collective-permute-done.30.refs_1_
  314.5 36.9 %merge.31.refs_2_ = bf16[16,144,256]{2,1,0:T(8,128)(2,1)} custom-call(bf16[8,144,256]{2,1,0:T(8,128)(2,1)} %merge.30.refs_0_, bf16[8,144,256]{2,1,0:T(8,128)(2,1)} %copy-done.27), custom_call_target="tpu_custom_call" | custom-call | bytes 2359296 | tf_op jit(solution)/shard_map/merge/pallas_call | solution.py:475
  351.4 5.6 merge.32.refs_0_
  357.9 9.4 %collective-permute-done.34.refs_1_.refs_2_ = bf16[2,144,256]{2,1,0:T(8,128)(2,1)S(1)} collective-permute-done((bf16[2,144,256]{2,1,0:T(8,128)(2,1)}, bf16[2,144,256]{2,1,0:T(8,128)(2,1)S(1)}, u32[]{:S(2)}, u32[]{:S(2)}) %collective-permute-start.34) | collective-permute-done | bytes 147488 | tf_op jit(solution)/shard_map/ppermute | solution.py:453
  367.9 10.1 %merge.33.refs_0_ = bf16[4,144,256]{2,1,0:T(8,128)(2,1)} custom-call(bf16[2,144,256]{2,1,0:T(8,128)(2,1)} %merge.32.refs_0_, bf16[2,144,256]{2,1,0:T(8,128)(2,1)} %copy-done.29), custom_call_target="tpu_custom_call" | custom-call | bytes 589824 | tf_op jit(solution)/shard_map/merge/pallas_call | solution.py:475
  378.1 9.1 %collective-permute-done.35.refs_1_ = bf16[4,144,256]{2,1,0:T(8,128)(2,1)S(1)} collective-permute-done((bf16[4,144,256]{2,1,0:T(8,128)(2,1)}, bf16[4,144,256]{2,1,0:T(8,128)(2,1)S(1)}, u32[]{:S(2)}, u32[]{:S(2)}) %collective-permute-start.35) | collective-permute-done | bytes 294944 | tf_op jit(solution)/shard_map/ppermute | solution.py:453
  388.9 19.0 %merge.34.refs_0_ = bf16[8,144,256]{2,1,0:T(8,128)(2,1)} custom-call(bf16[4,144,256]{2,1,0:T(8,128)(2,1)} %merge.33.refs_0_, bf16[4,144,256]{2,1,0:T(8,128)(2,1)} %copy-done.34, bf16[16,144,256]{2,1,0:T(8,128)(2,1)} %copy-done.7), custom_call_target="tpu_custom_call" | custom-call | bytes 1179648 | tf_op jit(solution)/shard_map/merge/pallas_call | solution.py:475
  408.6 9.5 %collective-permute-done.36.refs_1_ = bf16[8,144,256]{2,1,0:T(8,128)(2,1)S(1)} collective-permute-done((bf16[8,144,256]{2,1,0:T(8,128)(2,1)}, bf16[8,144,256]{2,1,0:T(8,128)(2,1)S(1)}, u32[]{:S(2)}, u32[]{:S(2)}) %collective-permute-start.36) | collective-permute-done | bytes 589856 | tf_op jit(solution)/shard_map/ppermute | solution.py:453
  418.9 36.9 %merge.35.refs_2_ = bf16[16,144,256]{2,1,0:T(8,128)(2,1)} custom-call(bf16[8,144,256]{2,1,0:T(8,128)(2,1)} %merge.34.refs_0_, bf16[8,144,256]{2,1,0:T(8,128)(2,1)} %copy-done.25), custom_call_target="tpu_custom_call" | custom-call | bytes 2359296 | tf_op jit(solution)/shard_map/merge/pallas_call | solution.py:475
  456.0 5.6 merge.36.refs_0_
  464.1 7.7 collective-permute-done.40.refs_1_
  472.5 10.1 %merge.37.refs_0_ = bf16[4,144,256]{2,1,0:T(8,128)(2,1)} custom-call(bf16[2,144,256]{2,1,0:T(8,128)(2,1)} %merge.36.refs_0_, bf16[2,144,256]{2,1,0:T(8,128)(2,1)} %copy-done.45), custom_call_target="tpu_custom_call" | custom-call | bytes 589824 | tf_op jit(solution)/shard_map/merge/pallas_call | solution.py:475
  495.5 19.0 %merge.38.refs_0_ = bf16[8,144,256]{2,1,0:T(8,128)(2,1)} custom-call(bf16[4,144,256]{2,1,0:T(8,128)(2,1)} %merge.37.refs_0_, bf16[4,144,256]{2,1,0:T(8,128)(2,1)} %copy-done.32, bf16[16,144,256]{2,1,0:T(8,128)(2,1)} %collective-permute-done.37.refs_3_.refs_2_), custom_call_target="tpu_custom_call" | custom-call | bytes 1179648 | tf_op jit(solution)/shard_map/merge/pallas_call | solution.py:475
  516.1 8.6 collective-permute-done.42.refs_1_
  525.5 36.9 %merge.39.refs_2_ = bf16[16,144,256]{2,1,0:T(8,128)(2,1)} custom-call(bf16[8,144,256]{2,1,0:T(8,128)(2,1)} %merge.38.refs_0_, bf16[8,144,256]{2,1,0:T(8,128)(2,1)} %copy-done.24), custom_call_target="tpu_custom_call" | custom-call | bytes 2359296 | tf_op jit(solution)/shard_map/merge/pallas_call | solution.py:475
  571.7 7.0 collective-permute-done.21
  582.8 5.8 conv.6
  628.8 5.7 conv.7
  635.2 5.7 conv.8
  641.6 16.7 %conv.9 = (f32[256,512]{1,0:T(8,128)}, f32[8,512]{1,0:T(8,128)}, f32[32,512]{1,0:T(8,128)}, f32[32,512]{1,0:T(8,128)}) custom-call(s32[8]{0:T(128)} %concatenate.175.refs_0_, bf16[3,320,512]{2,1,0:T(8,128)(2,1)} %select.21.refs_1_, bf16[16,144,256]{2,1,0:T(8,128)(2,1)} %merge.39.refs_2_, bf16[16,144,256]{2,1,0:T(8,128)(2,1)} %collective-permute-done.43.refs_3_, ...), custom_call_target="tpu_custom_call" | custom-call | flops 1207959552 | bytes 6373408 | tf_op jit(solution)/shard_map/conv/pallas_call | solution.py:475
  671.9 5.7 pool.1
  697.2 5.6 dgrad.5.refs_1_
  702.8 5.6 dgrad.6.refs_2_
  708.4 5.6 dgrad.7.refs_3_
  714.1 5.7 branch_grad.1
  762.2 5.8 dgrad.8.refs_7_
  804.6 9.0 %collective-permute-done.81 = bf16[1,8,168,256]{3,2,1,0:T(8,128)(2,1)S(1)} collective-permute-done((bf16[1,8,168,256]{3,2,1,0:T(8,128)(2,1)S(1)}, bf16[1,8,168,256]{3,2,1,0:T(8,128)(2,1)S(1)}, u32[]{:S(2)}, u32[]{:S(2)}) %collective-permute-start.81) | collective-permute-done | bytes 688160 | tf_op jit(solution)/shard_map/ppermute | solution.py:453
  814.6 6.4 collective-permute-done.82
  841.8 10.3 %collective-permute-done.76 = bf16[1,8,144,256]{3,2,1,0:T(8,128)(2,1)} collective-permute-done((bf16[1,8,144,256]{3,2,1,0:T(8,128)(2,1)}, bf16[1,8,144,256]{3,2,1,0:T(8,128)(2,1)}, u32[]{:S(2)}, u32[]{:S(2)}) %collective-permute-start.76) | collective-permute-done | bytes 589856 | tf_op jit(solution)/shard_map/ppermute | solution.py:453
  856.0 5.6 dgrad.9
  875.2 7.2 copy_subtract_fusion
  (491 shorter events, 302.0 us)
Async XLA Ops:
  17.7 11.5 %collective-permute-start.4 = (bf16[2,144,256]{2,1,0:T(8,128)(2,1)}, bf16[2,144,256]{2,1,0:T(8,128)(2,1)S(1)}, u32[]{:S(2)}, u32[]{:S(2)}) collective-permute-start(bf16[2,144,256]{2,1,0:T(8,128)(2,1)} %merge.20.refs_0_), channel_id=1, source_target_pairs={{0,16},{1,17},{2,18},{3,19},{4,20},{5,21},{6,22},{7,23},{8,24},{9,... | collective-permute-start | bytes 442376 | tf_op jit(solution)/shard_map/ppermute | solution.py:453
  40.0 8.8 collective-permute-start.5
  68.6 10.2 %collective-permute-start.6 = (bf16[8,144,256]{2,1,0:T(8,128)(2,1)}, bf16[8,144,256]{2,1,0:T(8,128)(2,1)S(1)}, u32[]{:S(2)}, u32[]{:S(2)}) collective-permute-start(bf16[8,144,256]{2,1,0:T(8,128)(2,1)} %merge.22.refs_0_), channel_id=1, source_target_pairs={{0,4},{1,3},{2,6},{3,1},{4,0},{5,7},{6,2},{7,5},{8,12},{9,11},{10,... | collective-permute-start | bytes 1769480 | tf_op jit(solution)/shard_map/ppermute | solution.py:453
  116.4 34.7 %collective-permute-start.7 = (bf16[16,144,256]{2,1,0:T(8,128)(2,1)}, bf16[16,144,256]{2,1,0:T(8,128)(2,1)S(1)}, u32[]{:S(2)}, u32[]{:S(2)}) collective-permute-start(bf16[16,144,256]{2,1,0:T(8,128)(2,1)} %merge.23.refs_2_), channel_id=1, source_target_pairs={{0,2},{1,5},{2,0},{3,7},{4,6},{5,1},{6,4},{7,3},{8,10},{9,13},{10,... | collective-permute-start | bytes 3538952 | tf_op jit(solution)/shard_map/ppermute | solution.py:453
  128.1 9.9 %collective-permute-start.14 = (bf16[2,168,256]{2,1,0:T(8,128)(2,1)}, bf16[2,168,256]{2,1,0:T(8,128)(2,1)S(1)}, u32[]{:S(2)}, u32[]{:S(2)}) collective-permute-start(bf16[2,168,256]{2,1,0:T(8,128)(2,1)} %merge.24.refs_0_), channel_id=1, source_target_pairs={{0,16},{1,17},{2,18},{3,19},{4,20},{5,21},{6,22},{7,23},{8,24},{9,... | collective-permute-start | bytes 516104 | tf_op jit(solution)/shard_map/ppermute | solution.py:453
  131.9 19.7 %collective-permute-start.1 = (bf16[40,512]{1,0:T(8,128)(2,1)}, bf16[40,512]{1,0:T(8,128)(2,1)}, u32[]{:S(2)}, u32[]{:S(2)}) collective-permute-start(bf16[40,512]{1,0:T(8,128)(2,1)} %get-tuple-element.184), channel_id=1, source_target_pairs={{0,3},{1,2},{2,1},{3,0},{4,7},{5,6},{6,5},{7,4},{8,11},{9,10},{10,... | collective-permute-start | bytes 122888 | tf_op jit(solution)/shard_map/ppermute | solution.py:453
  131.9 19.7 %collective-permute-start = (bf16[40,512]{1,0:T(8,128)(2,1)}, bf16[40,512]{1,0:T(8,128)(2,1)}, u32[]{:S(2)}, u32[]{:S(2)}) collective-permute-start(bf16[40,512]{1,0:T(8,128)(2,1)} %get-tuple-element.185), channel_id=1, source_target_pairs={{0,1},{1,0},{2,3},{3,2},{4,5},{5,4},{6,7},{7,6},{8,9},{9,8},{10,11... | collective-permute-start | bytes 122888 | tf_op jit(solution)/shard_map/ppermute | solution.py:453
  150.2 9.3 %collective-permute-start.15 = (bf16[4,168,256]{2,1,0:T(8,128)(2,1)}, bf16[4,168,256]{2,1,0:T(8,128)(2,1)S(1)}, u32[]{:S(2)}, u32[]{:S(2)}) collective-permute-start(bf16[4,168,256]{2,1,0:T(8,128)(2,1)} %merge.25.refs_0_), channel_id=1, source_target_pairs={{0,8},{1,9},{2,10},{3,11},{4,12},{5,13},{6,14},{7,15},{8,0},{9,1},... | collective-permute-start | bytes 1032200 | tf_op jit(solution)/shard_map/ppermute | solution.py:453
  151.1 47.0 %collective-permute-start.8 = (bf16[16,144,256]{2,1,0:T(8,128)(2,1)S(1)}, bf16[16,144,256]{2,1,0:T(8,128)(2,1)S(1)}, u32[]{:S(2)}, u32[]{:S(2)}) collective-permute-start(bf16[16,144,256]{2,1,0:T(8,128)(2,1)S(1)} %copy-done.12), channel_id=1, source_target_pairs={{0,1},{1,0},{2,3},{3,2},{4,5},{5,4},{6,7},{7,6},{8,9},{9,8},{10,11... | collective-permute-start | bytes 3538952 | tf_op jit(solution)/shard_map/ppermute | solution.py:453
  151.1 47.0 %collective-permute-start.9 = (bf16[16,144,256]{2,1,0:T(8,128)(2,1)S(1)}, bf16[16,144,256]{2,1,0:T(8,128)(2,1)}, u32[]{:S(2)}, u32[]{:S(2)}) collective-permute-start(bf16[16,144,256]{2,1,0:T(8,128)(2,1)S(1)} %collective-permute-done.7.refs_3_.refs_2_), channel_id=1, source_target_pairs={{0,1},{1,0},{2,3},{3,2},{4,5},{5,4},{6,7},{7,6},{8,9},{9,8},{10,11... | collective-permute-start | bytes 3538952 | tf_op jit(solution)/shard_map/ppermute | solution.py:453
  182.2 22.6 %collective-permute-start.16 = (bf16[8,168,256]{2,1,0:T(8,128)(2,1)}, bf16[8,168,256]{2,1,0:T(8,128)(2,1)}, u32[]{:S(2)}, u32[]{:S(2)}) collective-permute-start(bf16[8,168,256]{2,1,0:T(8,128)(2,1)} %merge.26.refs_0_), channel_id=1, source_target_pairs={{0,4},{1,3},{2,6},{3,1},{4,0},{5,7},{6,2},{7,5},{8,12},{9,11},{10,... | collective-permute-start | bytes 2064392 | tf_op jit(solution)/shard_map/ppermute | solution.py:453
  184.6 11.5 %collective-permute-start.2 = (bf16[160,512]{1,0:T(8,128)(2,1)}, bf16[160,512]{1,0:T(8,128)(2,1)}, u32[]{:S(2)}, u32[]{:S(2)}) collective-permute-start(bf16[160,512]{1,0:T(8,128)(2,1)} %bitcast.14), channel_id=1, source_target_pairs={{0,16},{1,17},{2,18},{3,19},{4,20},{5,21},{6,22},{7,23},{8,24},{9,... | collective-permute-start | bytes 491528 | tf_op jit(solution)/shard_map/ppermute | solution.py:453
  247.6 34.9 %collective-permute-start.17 = (bf16[16,168,256]{2,1,0:T(8,128)(2,1)}, bf16[16,168,256]{2,1,0:T(8,128)(2,1)S(1)}, u32[]{:S(2)}, u32[]{:S(2)}) collective-permute-start(bf16[16,168,256]{2,1,0:T(8,128)(2,1)} %merge.27.refs_2_), channel_id=1, source_target_pairs={{0,2},{1,5},{2,0},{3,7},{4,6},{5,1},{6,4},{7,3},{8,10},{9,13},{10,... | collective-permute-start | bytes 4128776 | tf_op jit(solution)/shard_map/ppermute | solution.py:453
  254.1 9.4 %collective-permute-start.28 = (bf16[2,144,256]{2,1,0:T(8,128)(2,1)}, bf16[2,144,256]{2,1,0:T(8,128)(2,1)S(1)}, u32[]{:S(2)}, u32[]{:S(2)}) collective-permute-start(bf16[2,144,256]{2,1,0:T(8,128)(2,1)} %merge.28.refs_0_), channel_id=1, source_target_pairs={{0,16},{1,17},{2,18},{3,19},{4,20},{5,21},{6,22},{7,23},{8,24},{9,... | collective-permute-start | bytes 442376 | tf_op jit(solution)/shard_map/ppermute | solution.py:453
  303.3 10.3 %collective-permute-start.30 = (bf16[8,144,256]{2,1,0:T(8,128)(2,1)}, bf16[8,144,256]{2,1,0:T(8,128)(2,1)S(1)}, u32[]{:S(2)}, u32[]{:S(2)}) collective-permute-start(bf16[8,144,256]{2,1,0:T(8,128)(2,1)} %merge.30.refs_0_), channel_id=1, source_target_pairs={{0,4},{1,3},{2,6},{3,1},{4,0},{5,7},{6,2},{7,5},{8,12},{9,11},{10,... | collective-permute-start | bytes 1769480 | tf_op jit(solution)/shard_map/ppermute | solution.py:453
  351.3 35.8 %collective-permute-start.31 = (bf16[16,144,256]{2,1,0:T(8,128)(2,1)}, bf16[16,144,256]{2,1,0:T(8,128)(2,1)S(1)}, u32[]{:S(2)}, u32[]{:S(2)}) collective-permute-start(bf16[16,144,256]{2,1,0:T(8,128)(2,1)} %merge.31.refs_2_), channel_id=1, source_target_pairs={{0,2},{1,5},{2,0},{3,7},{4,6},{5,1},{6,4},{7,3},{8,10},{9,13},{10,... | collective-permute-start | bytes 3538952 | tf_op jit(solution)/shard_map/ppermute | solution.py:453
  357.0 10.3 %collective-permute-start.34 = (bf16[2,144,256]{2,1,0:T(8,128)(2,1)}, bf16[2,144,256]{2,1,0:T(8,128)(2,1)S(1)}, u32[]{:S(2)}, u32[]{:S(2)}) collective-permute-start(bf16[2,144,256]{2,1,0:T(8,128)(2,1)} %merge.32.refs_0_), channel_id=1, source_target_pairs={{0,16},{1,17},{2,18},{3,19},{4,20},{5,21},{6,22},{7,23},{8,24},{9,... | collective-permute-start | bytes 442376 | tf_op jit(solution)/shard_map/ppermute | solution.py:453
  378.0 9.2 %collective-permute-start.35 = (bf16[4,144,256]{2,1,0:T(8,128)(2,1)}, bf16[4,144,256]{2,1,0:T(8,128)(2,1)S(1)}, u32[]{:S(2)}, u32[]{:S(2)}) collective-permute-start(bf16[4,144,256]{2,1,0:T(8,128)(2,1)} %merge.33.refs_0_), channel_id=1, source_target_pairs={{0,8},{1,9},{2,10},{3,11},{4,12},{5,13},{6,14},{7,15},{8,0},{9,1},... | collective-permute-start | bytes 884744 | tf_op jit(solution)/shard_map/ppermute | solution.py:453
  407.9 10.2 %collective-permute-start.36 = (bf16[8,144,256]{2,1,0:T(8,128)(2,1)}, bf16[8,144,256]{2,1,0:T(8,128)(2,1)S(1)}, u32[]{:S(2)}, u32[]{:S(2)}) collective-permute-start(bf16[8,144,256]{2,1,0:T(8,128)(2,1)} %merge.34.refs_0_), channel_id=1, source_target_pairs={{0,4},{1,3},{2,6},{3,1},{4,0},{5,7},{6,2},{7,5},{8,12},{9,11},{10,... | collective-permute-start | bytes 1769480 | tf_op jit(solution)/shard_map/ppermute | solution.py:453
  408.0 84.8 %collective-permute-start.18 = (bf16[16,168,256]{2,1,0:T(8,128)(2,1)S(1)}, bf16[16,168,256]{2,1,0:T(8,128)(2,1)}, u32[]{:S(2)}, u32[]{:S(2)}) collective-permute-start(bf16[16,168,256]{2,1,0:T(8,128)(2,1)S(1)} %copy-done.4), channel_id=1, source_target_pairs={{0,1},{1,0},{2,3},{3,2},{4,5},{5,4},{6,7},{7,6},{8,9},{9,8},{10,11... | collective-permute-start | bytes 4128776 | tf_op jit(solution)/shard_map/ppermute | solution.py:453
  408.1 85.7 %collective-permute-start.19 = (bf16[16,168,256]{2,1,0:T(8,128)(2,1)S(1)}, bf16[16,168,256]{2,1,0:T(8,128)(2,1)}, u32[]{:S(2)}, u32[]{:S(2)}) collective-permute-start(bf16[16,168,256]{2,1,0:T(8,128)(2,1)S(1)} %copy-done.6), channel_id=1, source_target_pairs={{0,1},{1,0},{2,3},{3,2},{4,5},{5,4},{6,7},{7,6},{8,9},{9,8},{10,11... | collective-permute-start | bytes 4128776 | tf_op jit(solution)/shard_map/ppermute | solution.py:453
  455.8 39.1 %collective-permute-start.37 = (bf16[16,144,256]{2,1,0:T(8,128)(2,1)}, bf16[16,144,256]{2,1,0:T(8,128)(2,1)}, u32[]{:S(2)}, u32[]{:S(2)}) collective-permute-start(bf16[16,144,256]{2,1,0:T(8,128)(2,1)} %merge.35.refs_2_), channel_id=1, source_target_pairs={{0,2},{1,5},{2,0},{3,7},{4,6},{5,1},{6,4},{7,3},{8,10},{9,13},{10,... | collective-permute-start | bytes 3538952 | tf_op jit(solution)/shard_map/ppermute | solution.py:453
  461.6 10.3 %collective-permute-start.40 = (bf16[2,144,256]{2,1,0:T(8,128)(2,1)}, bf16[2,144,256]{2,1,0:T(8,128)(2,1)S(1)}, u32[]{:S(2)}, u32[]{:S(2)}) collective-permute-start(bf16[2,144,256]{2,1,0:T(8,128)(2,1)} %merge.36.refs_0_), channel_id=1, source_target_pairs={{0,16},{1,17},{2,18},{3,19},{4,20},{5,21},{6,22},{7,23},{8,24},{9,... | collective-permute-start | bytes 442376 | tf_op jit(solution)/shard_map/ppermute | solution.py:453
  462.2 20.4 %collective-permute-start.11 = (f32[40,512]{1,0:T(8,128)S(1)}, f32[40,512]{1,0:T(8,128)S(1)}, u32[]{:S(2)}, u32[]{:S(2)}) collective-permute-start(f32[40,512]{1,0:T(8,128)S(1)} %pad_maximum_fusion.8), channel_id=1, source_target_pairs={{0,3},{1,2},{2,1},{3,0},{4,7},{5,6},{6,5},{7,4},{8,11},{9,10},{10,... | collective-permute-start | bytes 245768 | tf_op jit(solution)/shard_map/ppermute | solution.py:453
  482.6 12.2 %collective-permute-start.41 = (bf16[4,144,256]{2,1,0:T(8,128)(2,1)}, bf16[4,144,256]{2,1,0:T(8,128)(2,1)S(1)}, u32[]{:S(2)}, u32[]{:S(2)}) collective-permute-start(bf16[4,144,256]{2,1,0:T(8,128)(2,1)} %merge.37.refs_0_), channel_id=1, source_target_pairs={{0,8},{1,9},{2,10},{3,11},{4,12},{5,13},{6,14},{7,15},{8,0},{9,1},... | collective-permute-start | bytes 884744 | tf_op jit(solution)/shard_map/ppermute | solution.py:453
  493.8 117.0 %collective-permute-start.32 = (bf16[16,144,256]{2,1,0:T(8,128)(2,1)}, bf16[16,144,256]{2,1,0:T(8,128)(2,1)}, u32[]{:S(2)}, u32[]{:S(2)}) collective-permute-start(bf16[16,144,256]{2,1,0:T(8,128)(2,1)} %merge.31.refs_2_), channel_id=1, source_target_pairs={{0,1},{1,0},{2,3},{3,2},{4,5},{5,4},{6,7},{7,6},{8,9},{9,8},{10,11... | collective-permute-start | bytes 3538952 | tf_op jit(solution)/shard_map/ppermute | solution.py:453
  514.5 10.2 %collective-permute-start.42 = (bf16[8,144,256]{2,1,0:T(8,128)(2,1)}, bf16[8,144,256]{2,1,0:T(8,128)(2,1)S(1)}, u32[]{:S(2)}, u32[]{:S(2)}) collective-permute-start(bf16[8,144,256]{2,1,0:T(8,128)(2,1)} %merge.38.refs_0_), channel_id=1, source_target_pairs={{0,4},{1,3},{2,6},{3,1},{4,0},{5,7},{6,2},{7,5},{8,12},{9,11},{10,... | collective-permute-start | bytes 1769480 | tf_op jit(solution)/shard_map/ppermute | solution.py:453
  562.4 48.9 %collective-permute-start.43 = (bf16[16,144,256]{2,1,0:T(8,128)(2,1)}, bf16[16,144,256]{2,1,0:T(8,128)(2,1)}, u32[]{:S(2)}, u32[]{:S(2)}) collective-permute-start(bf16[16,144,256]{2,1,0:T(8,128)(2,1)} %merge.39.refs_2_), channel_id=1, source_target_pairs={{0,2},{1,5},{2,0},{3,7},{4,6},{5,1},{6,4},{7,3},{8,10},{9,13},{10,... | collective-permute-start | bytes 3538952 | tf_op jit(solution)/shard_map/ppermute | solution.py:453
  599.6 27.2 %collective-permute-start.33 = (bf16[16,144,256]{2,1,0:T(8,128)(2,1)S(1)}, bf16[16,144,256]{2,1,0:T(8,128)(2,1)}, u32[]{:S(2)}, u32[]{:S(2)}) collective-permute-start(bf16[16,144,256]{2,1,0:T(8,128)(2,1)S(1)} %copy-done.8), channel_id=1, source_target_pairs={{0,1},{1,0},{2,3},{3,2},{4,5},{5,4},{6,7},{7,6},{8,9},{9,8},{10,11... | collective-permute-start | bytes 3538952 | tf_op jit(solution)/shard_map/ppermute | solution.py:453
  608.8 26.4 %collective-permute-start.38 = (bf16[16,144,256]{2,1,0:T(8,128)(2,1)S(1)}, bf16[16,144,256]{2,1,0:T(8,128)(2,1)}, u32[]{:S(2)}, u32[]{:S(2)}) collective-permute-start(bf16[16,144,256]{2,1,0:T(8,128)(2,1)S(1)} %copy-done.9), channel_id=1, source_target_pairs={{0,1},{1,0},{2,3},{3,2},{4,5},{5,4},{6,7},{7,6},{8,9},{9,8},{10,11... | collective-permute-start | bytes 3538952 | tf_op jit(solution)/shard_map/ppermute | solution.py:453
  610.8 24.4 %collective-permute-start.39 = (bf16[16,144,256]{2,1,0:T(8,128)(2,1)}, bf16[16,144,256]{2,1,0:T(8,128)(2,1)}, u32[]{:S(2)}, u32[]{:S(2)}) collective-permute-start(bf16[16,144,256]{2,1,0:T(8,128)(2,1)} %collective-permute-done.37.refs_3_.refs_2_), channel_id=1, source_target_pairs={{0,1},{1,0},{2,3},{3,2},{4,5},{5,4},{6,7},{7,6},{8,9},{9,8},{10,11... | collective-permute-start | bytes 3538952 | tf_op jit(solution)/shard_map/ppermute | solution.py:453
  610.8 30.8 %collective-permute-start.44 = (bf16[16,144,256]{2,1,0:T(8,128)(2,1)S(1)}, bf16[16,144,256]{2,1,0:T(8,128)(2,1)}, u32[]{:S(2)}, u32[]{:S(2)}) collective-permute-start(bf16[16,144,256]{2,1,0:T(8,128)(2,1)S(1)} %copy-done.10), channel_id=1, source_target_pairs={{0,1},{1,0},{2,3},{3,2},{4,5},{5,4},{6,7},{7,6},{8,9},{9,8},{10,11... | collective-permute-start | bytes 3538952 | tf_op jit(solution)/shard_map/ppermute | solution.py:453
  611.4 30.2 %collective-permute-start.45 = (bf16[16,144,256]{2,1,0:T(8,128)(2,1)}, bf16[16,144,256]{2,1,0:T(8,128)(2,1)}, u32[]{:S(2)}, u32[]{:S(2)}) collective-permute-start(bf16[16,144,256]{2,1,0:T(8,128)(2,1)} %collective-permute-done.43.refs_3_), channel_id=1, source_target_pairs={{0,1},{1,0},{2,3},{3,2},{4,5},{5,4},{6,7},{7,6},{8,9},{9,8},{10,11... | collective-permute-start | bytes 3538952 | tf_op jit(solution)/shard_map/ppermute | solution.py:453
  626.8 41.1 %collective-permute-start.50 = (bf16[3,48,512]{2,1,0:T(8,128)(2,1)S(1)}, bf16[3,48,512]{2,1,0:T(8,128)(2,1)S(1)}, u32[]{:S(2)}, u32[]{:S(2)}) collective-permute-start(bf16[3,48,512]{2,1,0:T(8,128)(2,1)S(1)} %bitcast.95), channel_id=1, source_target_pairs={{0,16},{1,17},{2,18},{3,19},{4,20},{5,21},{6,22},{7,23},{8,24},{9,... | collective-permute-start | bytes 442376 | tf_op jit(solution)/shard_map/ppermute | solution.py:453
  660.1 30.9 %collective-permute-start.51 = (f32[96,512]{1,0:T(8,128)S(1)}, f32[96,512]{1,0:T(8,128)S(1)}, u32[]{:S(2)}, u32[]{:S(2)}) collective-permute-start(f32[96,512]{1,0:T(8,128)S(1)} %pad_maximum_fusion.5), channel_id=1, source_target_pairs={{0,1},{1,0},{2,3},{3,2},{4,5},{5,4},{6,7},{7,6},{8,9},{9,8},{10,11... | collective-permute-start | bytes 589832 | tf_op jit(solution)/shard_map/ppermute | solution.py:453
  661.9 29.1 %collective-permute-start.52 = (f32[96,512]{1,0:T(8,128)S(1)}, f32[96,512]{1,0:T(8,128)S(1)}, u32[]{:S(2)}, u32[]{:S(2)}) collective-permute-start(f32[96,512]{1,0:T(8,128)S(1)} %pad_maximum_fusion.6), channel_id=1, source_target_pairs={{0,3},{1,2},{2,1},{3,0},{4,7},{5,6},{6,5},{7,4},{8,11},{9,10},{10,... | collective-permute-start | bytes 589832 | tf_op jit(solution)/shard_map/ppermute | solution.py:453
  720.7 15.3 %collective-permute-start.61 = (bf16[3,320,512]{2,1,0:T(8,128)(2,1)S(1)}, bf16[3,320,512]{2,1,0:T(8,128)(2,1)S(1)}, u32[]{:S(2)}, u32[]{:S(2)}) collective-permute-start(bf16[3,320,512]{2,1,0:T(8,128)(2,1)S(1)} %copy-done.1), channel_id=1, source_target_pairs={{0,1},{1,0},{2,3},{3,2},{4,5},{5,4},{6,7},{7,6},{8,9},{9,8},{10,11... | collective-permute-start | bytes 2949128 | tf_op jit(solution)/shard_map/ppermute | solution.py:453
  721.2 14.8 %collective-permute-start.62 = (bf16[3,320,512]{2,1,0:T(8,128)(2,1)S(1)}, bf16[3,320,512]{2,1,0:T(8,128)(2,1)}, u32[]{:S(2)}, u32[]{:S(2)}) collective-permute-start(bf16[3,320,512]{2,1,0:T(8,128)(2,1)S(1)} %copy-done), channel_id=1, source_target_pairs={{0,1},{1,0},{2,3},{3,2},{4,5},{5,4},{6,7},{7,6},{8,9},{9,8},{10,11... | collective-permute-start | bytes 2949128 | tf_op jit(solution)/shard_map/ppermute | solution.py:453
  752.9 81.4 %collective-permute-start.74 = (bf16[1,320,512]{2,1,0:T(8,128)(2,1)}, bf16[1,320,512]{2,1,0:T(8,128)(2,1)}, u32[]{:S(2)}, u32[]{:S(2)}) collective-permute-start(bf16[1,320,512]{2,1,0:T(8,128)(2,1)} %maximum_select_fusion.2.refs_1_), channel_id=1, source_target_pairs={{0,1},{1,0},{2,3},{3,2},{4,5},{5,4},{6,7},{7,6},{8,9},{9,8},{10,11... | collective-permute-start | bytes 983048 | tf_op jit(solution)/shard_map/ppermute | solution.py:453
  753.5 40.8 %collective-permute-start.72 = (bf16[1,320,512]{2,1,0:T(8,128)(2,1)S(1)}, bf16[1,320,512]{2,1,0:T(8,128)(2,1)}, u32[]{:S(2)}, u32[]{:S(2)}) collective-permute-start(bf16[1,320,512]{2,1,0:T(8,128)(2,1)S(1)} %copy-done.20), channel_id=1, source_target_pairs={{0,1},{1,0},{2,3},{3,2},{4,5},{5,4},{6,7},{7,6},{8,9},{9,8},{10,11... | collective-permute-start | bytes 983048 | tf_op jit(solution)/shard_map/ppermute | solution.py:453
  760.8 35.2 %collective-permute-start.73 = (bf16[1,320,512]{2,1,0:T(8,128)(2,1)}, bf16[1,320,512]{2,1,0:T(8,128)(2,1)}, u32[]{:S(2)}, u32[]{:S(2)}) collective-permute-start(bf16[1,320,512]{2,1,0:T(8,128)(2,1)} %norm_grad.2.refs_1_.refs_3_), channel_id=1, source_target_pairs={{0,1},{1,0},{2,3},{3,2},{4,5},{5,4},{6,7},{7,6},{8,9},{9,8},{10,11... | collective-permute-start | bytes 983048 | tf_op jit(solution)/shard_map/ppermute | solution.py:453
  768.0 58.8 %collective-permute-start.71 = (bf16[3,8,144,256]{3,2,1,0:T(8,128)(2,1)S(1)}, bf16[3,8,144,256]{3,2,1,0:T(8,128)(2,1)}, u32[]{:S(2)}, u32[]{:S(2)}) collective-permute-start(bf16[3,8,144,256]{3,2,1,0:T(8,128)(2,1)S(1)} %copy-done.3), channel_id=1, source_target_pairs={{0,4},{1,3},{2,6},{3,1},{4,0},{5,7},{6,2},{7,5},{8,12},{9,11},{10,... | collective-permute-start | bytes 5308424 | tf_op jit(solution)/shard_map/ppermute | solution.py:453
  775.3 8.5 collective-permute-start.67
  802.6 11.0 %collective-permute-start.81 = (bf16[1,8,168,256]{3,2,1,0:T(8,128)(2,1)S(1)}, bf16[1,8,168,256]{3,2,1,0:T(8,128)(2,1)S(1)}, u32[]{:S(2)}, u32[]{:S(2)}) collective-permute-start(bf16[1,8,168,256]{3,2,1,0:T(8,128)(2,1)S(1)} %pad_maximum_fusion.3), channel_id=1, source_target_pairs={{0,4},{1,3},{2,6},{3,1},{4,0},{5,7},{6,2},{7,5},{8,12},{9,11},{10,... | collective-permute-start | bytes 2064392 | tf_op jit(solution)/shard_map/ppermute | solution.py:453
  833.5 20.9 %collective-permute-start.85 = (bf16[3,4,144,256]{3,2,1,0:T(8,128)(2,1)S(1)}, bf16[3,4,144,256]{3,2,1,0:T(8,128)(2,1)}, u32[]{:S(2)}, u32[]{:S(2)}) collective-permute-start(bf16[3,4,144,256]{3,2,1,0:T(8,128)(2,1)S(1)} %copy-done.18), channel_id=1, source_target_pairs={{0,2},{1,5},{2,0},{3,7},{4,6},{5,1},{6,4},{7,3},{8,10},{9,13},{10,... | collective-permute-start | bytes 2654216 | tf_op jit(solution)/shard_map/ppermute | solution.py:453
  838.1 14.1 %collective-permute-start.76 = (bf16[1,8,144,256]{3,2,1,0:T(8,128)(2,1)}, bf16[1,8,144,256]{3,2,1,0:T(8,128)(2,1)}, u32[]{:S(2)}, u32[]{:S(2)}) collective-permute-start(bf16[1,8,144,256]{3,2,1,0:T(8,128)(2,1)} %get-tuple-element.109.refs_6_), channel_id=1, source_target_pairs={{0,4},{1,3},{2,6},{3,1},{4,0},{5,7},{6,2},{7,5},{8,12},{9,11},{10,... | collective-permute-start | bytes 1769480 | tf_op jit(solution)/shard_map/ppermute | solution.py:453
  853.7 8.9 %collective-permute-start.77 = (bf16[1,4,144,256]{3,2,1,0:T(8,128)(2,1)S(1)}, bf16[1,4,144,256]{3,2,1,0:T(8,128)(2,1)S(1)}, u32[]{:S(2)}, u32[]{:S(2)}) collective-permute-start(bf16[1,4,144,256]{3,2,1,0:T(8,128)(2,1)S(1)} %get-tuple-element.166), channel_id=1, source_target_pairs={{0,2},{1,5},{2,0},{3,7},{4,6},{5,1},{6,4},{7,3},{8,10},{9,13},{10,... | collective-permute-start | bytes 884744 | tf_op jit(solution)/shard_map/ppermute | solution.py:453
  855.5 12.5 %collective-permute-start.86 = (bf16[3,2,144,256]{3,2,1,0:T(8,128)(2,1)S(1)}, bf16[3,2,144,256]{3,2,1,0:T(8,128)(2,1)S(1)}, u32[]{:S(2)}, u32[]{:S(2)}) collective-permute-start(bf16[3,2,144,256]{3,2,1,0:T(8,128)(2,1)S(1)} %fusion.5), channel_id=1, source_target_pairs={{0,8},{1,9},{2,10},{3,11},{4,12},{5,13},{6,14},{7,15},{8,0},{9,1},... | collective-permute-start | bytes 1327112 | tf_op jit(solution)/shard_map/ppermute | solution.py:453
  (108 other events, 1187.8 us)

commit v3 on v2

--- a/solution.py
+++ b/solution.py
@@ -443,6 +443,9 @@
 UP_AT = DOWN_AT + TASK_COUNT * B
 CONV_AT = UP_AT + TASK_COUNT * C
 HIDDEN = TASK_COUNT * B
+STATS = 8
+RIM = PAIR * WID
+MESSAGE = STATS + RIM
 M_ROWS, M_GROUP, M_BAND, M_TOP, M_TOTAL, M_DEV = 0, 2, 4, 5, 6, 7
 
 
@@ -537,7 +540,8 @@
     return mean, inverse, gain, bias
 
 
-def rims(meta, first, second):
+def rims(meta, first, second, start=STATS):
+    first, second = first[start:], second[start:]
     band = meta[M_BAND]
     odd = (band % 2) == 1
     up = jnp.where(odd, first, second)
@@ -557,13 +561,13 @@
     ext[pl.ds(at, WID)] = down[slot * WID : (slot + 1) * WID]
 
 
-def put_edges(meta, ref, first, second):
+def put_edges(meta, ref, message, second):
     odd = (meta[M_BAND] % 2) == 1
     for slot in range(PAIR):
         last = PIX * slot + WID * (meta[M_ROWS + slot] - 1)
         head = PIX * slot
         at = pl.multiple_of(jnp.where(odd, head, last), WID)
-        first[slot * WID : (slot + 1) * WID] = ref[pl.ds(at, WID)]
+        message[STATS + slot * WID : STATS + (slot + 1) * WID] = ref[pl.ds(at, WID)]
         at = pl.multiple_of(jnp.where(odd, last, head), WID)
         second[slot * WID : (slot + 1) * WID] = ref[pl.ds(at, WID)]
 
@@ -622,7 +626,7 @@
 
 
 def conv_body(block, meta, ext, *rest):
-    pieces, (out, stats, edge1, edge2), (kernel, patch, sem) = rest[:4], rest[4:8], rest[8:]
+    pieces, (out, message, edge2), (kernel, patch, sem) = rest[:4], rest[4:7], rest[7:]
     weights_start(meta, pieces, kernel, sem, block)
     for slot in range(PAIR):
         value = ext[slot * EXT : (slot + 1) * EXT].astype(F32)
@@ -640,10 +644,10 @@
         masked = value * own_mask(meta, slot)
         first = first + jnp.sum(masked, axis=0, keepdims=True)
         second = second + jnp.sum(masked * value, axis=0, keepdims=True)
-    stats[...] = jnp.zeros_like(stats)
-    stats[0:1] = first
-    stats[1:2] = second
-    put_edges(meta, out, edge1, edge2)
+    put_edges(meta, out, message, edge2)
+    message[0:STATS] = jnp.zeros((STATS, C), F32)
+    message[0:1] = first
+    message[1:2] = second
 
 
 def dgrad_body(block, meta, ext, *rest):
@@ -755,14 +759,14 @@
     stats[1:2, 0:HIDDEN] = second
 
 
-def expand_body(meta, hidden, hstats, affine, up_w, squeezed, expanded, stats):
+def expand_body(meta, hidden, hstats, affine, up_w, message, squeezed, expanded, stats):
     total = total_of(meta)
     mean, inverse, gain, bias = norm_terms(hstats, 0, 0, HIDDEN, affine, DOWN_AT, total)
     for slot in range(PAIR):
         at = slice(slot * EXT, (slot + 1) * EXT)
         value = gelu((hidden[at] - mean) * inverse * gain + bias)
         squeezed[at] = (value * outer_mask(meta, slot, HIDDEN)).astype(BF)
-    stats[...] = jnp.zeros_like(stats)
+    stats[...] = message[...]
     for task in range(TASK_COUNT):
         part = jnp.dot(
             squeezed[:, task * B : (task + 1) * B], up_w[task], preferred_element_type=F32
@@ -858,7 +862,7 @@
         )
         dgain, dbias = back[2 * task : 2 * task + 1], back[2 * task + 1 : 2 * task + 2]
         at = slice(task * PAIR * WID, (task + 1) * PAIR * WID)
-        up, dn = rims(meta, rec1[at], rec2[at])
+        up, dn = rims(meta, rec1[at], rec2[at], 0)
         for slot in range(PAIR):
             put_ext(meta, ext, slot, z3[slot * PIX : (slot + 1) * PIX], up, dn)
             at = slice(slot * EXT, (slot + 1) * EXT)
@@ -871,7 +875,7 @@
 
 
 def branch_grad_body(
-    meta, ds0, ds1, ds2, expanded, z2, stats, affine, dpu, dp2, back, edge1, edge2
+    meta, ds0, ds1, ds2, expanded, z2, stats, affine, dpu, dp2, back, edge2
 ):
     total = total_of(meta)
     mean, inverse, gain, bias = norm_terms(stats, 0, 0, C, affine, C, total)
@@ -904,7 +908,7 @@
         sums[1] += jnp.sum(value, axis=0, keepdims=True)
     for i in range(8):
         back[i : i + 1] = sums[i]
-    put_edges(meta, dp2, edge1, edge2)
+    put_edges(meta, dp2, back, edge2)
 
 
 def expand_grad_body(
@@ -970,7 +974,7 @@
 
 
 def squeeze_grad_body(
-    meta, dph, hidden, hstats, hback, down, a1, da1, z1, s1, affine, dp1, back, edge1, edge2, ddown
+    meta, dph, hidden, hstats, hback, down, a1, da1, z1, s1, affine, dp1, back, edge2, ddown
 ):
     total = total_of(meta)
     mean, inverse, gain, _ = norm_terms(hstats, 0, 0, HIDDEN, affine, DOWN_AT, total)
@@ -998,17 +1002,17 @@
         dp1[own] = value
         first = first + jnp.sum(value * normed, axis=0, keepdims=True)
         second = second + jnp.sum(value, axis=0, keepdims=True)
-    back[...] = jnp.zeros_like(back)
+    put_edges(meta, dp1, back, edge2)
+    back[0:STATS] = jnp.zeros((STATS, C), F32)
     back[0:1] = first
     back[1:2] = second
-    put_edges(meta, dp1, edge1, edge2)
 
 
 CONV_FLOPS = 2 * PAIR * PIX * 9 * C * C
 
 
 def conv_call(meta, ext, entry, pieces, block, deps=()):
-    shapes = [sds((PAIR * PIX, C)), sds((8, C)), sds((PAIR * WID, C)), sds((PAIR * WID, C))]
+    shapes = [sds((PAIR * PIX, C)), sds((MESSAGE, C)), sds((RIM, C))]
     scratch = [
         pltpu.VMEM((9 * C, C), BF),
         pltpu.VMEM((PAIR * PIX, 9 * C), BF),
@@ -1066,24 +1070,32 @@
         [pltpu.SemaphoreType.DMA((len(spans),))],
         name=name,
         deps=deps,
-        outs="a",
     )[0]
 
 
-def sync(stats, edge1=None, edge2=None):
-    rows = stats.shape[0]
-    if edge1 is None:
-        stats = stats + swap(stats, 1)
-        stats = stats + swap(stats, 3)
-        first = second = None
-    else:
-        got = swap(jnp.concatenate([stats, edge1], axis=0), 1)
-        stats, first = stats + got[:rows], got[rows:]
-        got = swap(jnp.concatenate([stats, edge2], axis=0), 3)
-        stats, second = stats + got[:rows], got[rows:]
-    stats = stats + swap(stats, 4)
-    stats = stats + swap(stats, 8)
-    return stats, first, second
+def combine_body(own, got, *rest):
+    out = rest[-1]
+    out[0:STATS] = own[0:STATS] + got[0:STATS]
+    if len(rest) > 1:
+        out[STATS:] = rest[0][...]
+
+
+def combine(own, got, tail=None, deps=()):
+    rows = STATS if tail is None else STATS + tail.shape[0]
+    args = (own, got) if tail is None else (own, got, tail)
+    return kernel_call(
+        combine_body, [sds((rows, C))], args, "v" * len(args), name="combine", deps=deps
+    )[0]
+
+
+def sync(message, tail=None, between=()):
+    value, got = message, []
+    for stage, mask in enumerate((1, 3, 4, 8)):
+        arrived = swap(value, mask)
+        deps = between[stage](value) if stage < len(between) and between[stage] else ()
+        value = combine(value, arrived, tail if stage == 0 else None, deps)
+        got.append(arrived)
+    return value, got[0], got[1]
 
 
 def attention_rows(pieces, block, me):
@@ -1107,15 +1119,23 @@
     return jnp.concatenate([jnp.take(tails, spot, axis=0) for spot in spots], axis=-1)
 
 
-def scatter_stage(keep, send, even, odd):
-    got = swap(send, even, odd)
+def fold_body(keep, got, keep_out, *send):
     half = keep.shape[1] // 2
-    send = (keep[:, half:] + got[:, half:].astype(F32)).astype(BF)
-    return keep[:, :half] + got[:, :half].astype(F32), send
-
-
-def scatter_last(keep, send):
-    return keep + swap(send, 8).astype(F32)
+    for i in range(keep.shape[0]):
+        for place in range(keep.shape[1]):
+            value = keep[i, place] + got[i, place].astype(F32)
+            if not send or place < half:
+                keep_out[i, place] = value
+            else:
+                send[0][i, place - half] = value.astype(BF)
+
+
+def fold(keep, got, last=False, deps=()):
+    count, places, rows, width = keep.shape
+    shapes = [sds(keep.shape)]
+    if not last:
+        shapes = [sds((count, places // 2, rows, width), t) for t in (F32, BF)]
+    return kernel_call(fold_body, shapes, (keep, got), "vv", name="fold", deps=deps)
 
 
 def join_columns(total, core):
@@ -1128,35 +1148,83 @@
     )
 
 
-def order_pair(own, other, top):
-    return jnp.where(
-        top == 0, jnp.concatenate([own, other]), jnp.concatenate([other, own])
-    )
-
-
-def with_rims(images, cotangent, rows, band):
-    valid = (jnp.arange(BAND) < rows).astype(BF)[:, None, None]
-    own = images[0] * valid
-    seed = cotangent[:, 0]
-    cells = seed.shape[2]
-    last = jnp.concatenate(
-        [
-            lax.dynamic_index_in_dim(own, rows - 1, 0, keepdims=False),
-            lax.dynamic_index_in_dim(seed, rows // 2 - 1, 1, keepdims=False).reshape(-1, C),
-        ]
-    )
-    head = jnp.concatenate([own[0], seed[:, 0].reshape(-1, C)])
-    odd = band % 2 == 1
-    first = swap(jnp.where(odd, head, last), 1)
-    second = swap(jnp.where(odd, last, head), 3)
-    up = jnp.where(band > 0, jnp.where(odd, first, second), 0)
-    down = jnp.where(band < 3, jnp.where(odd, second, first), 0)
-    pixels = jnp.concatenate([up[None, :WID], own, jnp.zeros_like(up)[None, :WID]])
-    pixels = lax.dynamic_update_index_in_dim(pixels, down[:WID], rows + 1, 0)
-    up, down = (v[WID:].reshape(TASK_COUNT, cells, C) for v in (up, down))
-    seeds = jnp.concatenate([up[:, None], seed, jnp.zeros_like(up)[:, None]], axis=1)
-    seeds = lax.dynamic_update_index_in_dim(seeds, down, rows // 2 + 1, 1)
-    return pixels.reshape(EXT, C), seeds.reshape(TASK_COUNT, -1, C)
+def edge_body(meta, images, seeds, first, second, pixels, cells):
+    rows = meta[M_ROWS + meta[M_TOP]]
+    odd = (meta[M_BAND] % 2) == 1
+    ids = pixel_ids(PIX)
+    pixels[...] = jnp.where(ids < rows * WID, images[...].astype(F32), 0.0)
+    cells[...] = seeds[...].astype(F32)
+    wide = WID // 2
+    last = pl.multiple_of(WID * (rows - 1), WID)
+    last_cell = pl.multiple_of(wide * (rows // 2 - 1), wide)
+    tail = [pixels[pl.ds(last, WID)]]
+    head = [pixels[0:WID]]
+    for task in range(TASK_COUNT):
+        tail.append(cells[task, pl.ds(last_cell, wide)])
+        head.append(cells[task, 0:wide])
+    blank = jnp.zeros((wide, C), F32)
+    tail = jnp.concatenate(tail + [blank], axis=0)
+    head = jnp.concatenate(head + [blank], axis=0)
+    first[...] = jnp.where(odd, head, tail).astype(BF)
+    second[...] = jnp.where(odd, tail, head).astype(BF)
+
+
+def rim_body(meta, images, seeds, got1, got2, ext, cot, pixels, cells):
+    rows = meta[M_ROWS + meta[M_TOP]]
+    up, down = rims(meta, got1[...].astype(F32), got2[...].astype(F32), 0)
+    ids = pixel_ids(PIX)
+    wide = WID // 2
+    pixels[0:WID] = up[0:WID]
+    pixels[WID : WID + PIX] = jnp.where(ids < rows * WID, images[...].astype(F32), 0.0)
+    pixels[WID + PIX : EXT] = jnp.zeros((WID, C), F32)
+    pixels[pl.ds(pl.multiple_of(WID * (rows + 1), WID), WID)] = down[0:WID]
+    ext[...] = pixels[...].astype(BF)
+    count = seeds.shape[1]
+    for task in range(TASK_COUNT):
+        at = slice(WID + task * wide, WID + (task + 1) * wide)
+        cells[task, 0:wide] = up[at]
+        cells[task, wide : wide + count] = seeds[task].astype(F32)
+        cells[task, wide + count :] = jnp.zeros((wide, C), F32)
+        cells[task, pl.ds(pl.multiple_of(wide * (rows // 2 + 1), wide), wide)] = down[at]
+    cot[...] = cells[...].astype(BF)
+
+
+def pair_body(meta, own, got, out):
+    top = meta[M_TOP]
+
+    def place(flip):
+        out[:, flip] = own[...]
+        out[:, 1 - flip] = got[...]
+
+    for flip in range(2):
+        pl.when(top == flip)(functools.partial(place, flip))
+
+
+def pair(meta, own, got, deps=()):
+    shape = (own.shape[0], PAIR) + own.shape[1:]
+    return kernel_call(
+        pair_body, [sds(shape, own.dtype)], (meta, own, got), "svv", name="pair", deps=deps
+    )[0]
+
+
+def adam_body(rate, weights, grad, moment, square, out_weights, out_moment, out_square):
+    updated = adamw(weights[...], grad[...], moment[...], square[...], rate)
+    out_weights[...], out_moment[...], out_square[...] = updated
+
+
+def adam_call(weights, grad, moment, square, rate, steps):
+    width = weights.shape[2] // steps
+    block = pl.BlockSpec(weights.shape[:2] + (width,), lambda i: (0, 0, i))
+    size = weights.size * 4
+    return pl.pallas_call(
+        functools.partial(adam_body, rate),
+        out_shape=[sds(weights.shape)] * 3,
+        grid=(steps,),
+        in_specs=[block] * 4,
+        out_specs=[block] * 3,
+        cost_estimate=pl.CostEstimate(flops=0, bytes_accessed=7 * size, transcendentals=0),
+        name="adam",
+    )(weights, grad, moment, square)
 
 
 def local_pairs(
@@ -1203,63 +1271,129 @@
     lam = TASK_COUNT * jax.nn.softmax(ratios / SOFTMAX_TEMP)
     own_rows = heights[slot] // 4
 
-    def near_chips(k, deps=()):
-        chip = merge([(shard_mine, starts[k]), (shard_got, starts[k])], counts[k], deps)
-        got = swap(chip, 16)
-        four = merge([chip, got], counts[k])
-        return got, four, swap(four, 8)
-
-    def far_chips(k, four, got, deps=(), late=()):
-        eight = merge([four, got], counts[k], deps)
-        sixteen = merge([eight, swap(eight, 4, 2)], counts[k], late)
-        far = swap(sixteen, 2, 4)
-        return sixteen, far
+    def m1(k, deps=()):
+        return merge([(shard_mine, starts[k]), (shard_got, starts[k])], counts[k], deps, "m1")
+
+    def grow(k, have, got, deps=()):
+        return merge([have, got], counts[k], deps, "m" + str(2 * have.shape[0]))
 
     def both_cores(sixteen, far):
         return sixteen, far, swap(sixteen, 1), swap(far, 1)
 
-    z_got, z_four, z_eight = near_chips(0)
-    own_ext, own_cot = with_rims(images, task_cotangent, own_rows, band)
-    x0 = order_pair(own_ext, swap(own_ext, TOP), top)[None]
-    cot = jnp.moveaxis(order_pair(own_cot[None], swap(own_cot, TOP)[None], top), 0, 1)
-    reached = far_chips(0, z_four, z_eight)
-    pieces = [both_cores(*reached)]
-    z_next = near_chips(1, (z_got,))
-
-    z1, st, e1, e2 = conv_call(meta, x0.reshape(1, PAIR * EXT, C), 0, pieces[0], block)
-    x0 = x0.reshape(1, PAIR * EXT, C)
-    for k in range(1, 2 + TASK_COUNT):
-        z_got, z_four, z_eight = z_next
-        if k < 1 + TASK_COUNT:
-            z_next = near_chips(k + 1, (z_got,))
-        reached = far_chips(k, z_four, z_eight, (reached[1],), (st,) if k == 1 else ())
-        pieces.append(both_cores(*reached))
-
-    s1, z1r1, z1r2 = sync(st, e1, e2)
+    flat_images = images.reshape(PIX, C)
+    flat_seeds = task_cotangent.reshape(TASK_COUNT, -1, C)
+    cells = flat_seeds.shape[1]
+    chip0 = m1(0)
+    edge1, edge2 = kernel_call(
+        edge_body,
+        [sds((3 * WID, C), BF), sds((3 * WID, C), BF)],
+        (meta, flat_images, flat_seeds),
+        "svv",
+        [pltpu.VMEM((PIX, C), F32), pltpu.VMEM((TASK_COUNT, cells, C), F32)],
+        name="edge",
+        deps=(chip0,),
+    )
+    edge1, edge2 = swap(edge1, 1), swap(edge2, 3)
+    four0 = grow(0, chip0, swap(chip0, 16))
+    chip1 = m1(1, (four0,))
+    own_ext, own_cot = kernel_call(
+        rim_body,
+        [sds((EXT, C), BF), sds((TASK_COUNT, cells + WID, C), BF)],
+        (meta, flat_images, flat_seeds, edge1, edge2),
+        "svvvv",
+        [pltpu.VMEM((EXT, C), F32), pltpu.VMEM((TASK_COUNT, cells + WID, C), F32)],
+        name="rim",
+        deps=(four0,),
+    )
+    got_ext = swap(own_ext, TOP)
+    eight0 = grow(0, four0, swap(four0, 8), (own_ext,))
+    near0 = swap(eight0, 4, 2)
+    four1 = grow(1, chip1, swap(chip1, 16), (eight0,))
+    x0 = pair(meta, own_ext[None], got_ext[None], (four1,)).reshape(1, PAIR * EXT, C)
+    sixteen0 = grow(0, eight0, near0, (x0,))
+    far0 = swap(sixteen0, 2, 4)
+    eight1 = grow(1, four1, swap(four1, 8), (sixteen0,))
+    chip2 = m1(2, (eight1,))
+    got_cot = swap(own_cot, TOP)
+    cot = pair(meta, own_cot, got_cot, (chip2,))
+    four2 = grow(2, chip2, swap(chip2, 16), (cot,))
+    pieces = [both_cores(sixteen0, far0)]
+    near1 = swap(eight1, 4, 2)
+    z1, msg, e2 = conv_call(meta, x0, 0, pieces[0], block, (four2,))
+
+    kept = {}
+
+    def sync1_a(value):
+        kept["16_1"] = grow(1, eight1, near1, (value,))
+        kept["far1"] = swap(kept["16_1"], 2, 4)
+        return (kept["16_1"],)
+
+    def sync1_b(value):
+        kept["8_2"] = grow(2, four2, swap(four2, 8), (value,))
+        kept["1_3"] = m1(3, (kept["8_2"],))
+        return (kept["1_3"],)
+
+    def sync1_c(value):
+        kept["4_3"] = grow(3, kept["1_3"], swap(kept["1_3"], 16), (value,))
+        return (kept["4_3"],)
+
+    s1, z1r1, z1r2 = sync(msg, e2, (None, sync1_a, sync1_b, sync1_c))
+    pieces.append(both_cores(kept["16_1"], kept["far1"]))
+    near2 = swap(kept["8_2"], 4, 2)
     tails = attention_rows(pieces[1], block, me)
     kind_rows = extra // 2
     down = tails[:, :kind_rows].reshape(TASK_COUNT, C, B).transpose(1, 0, 2).reshape(C, HIDDEN)
     up_w = tails[:, kind_rows:].reshape(TASK_COUNT, B, C)
     a1, hidden, hst = kernel_call(
         squeeze_body,
-        [sds((1, PAIR * EXT, C), BF), sds((PAIR * EXT, HIDDEN)), sds((8, C))],
+        [sds((1, PAIR * EXT, C), BF), sds((PAIR * EXT, HIDDEN)), sds((STATS, C))],
         (meta, z1, s1, z1r1, z1r2, affine, down),
         "svvvvvv",
         [pltpu.VMEM((PAIR * EXT, C), F32)],
         2 * PAIR * EXT * C * HIDDEN,
         "squeeze",
     )
-    hstats, _, _ = sync(hst)
-    z2, st2, e1, e2 = conv_call(meta, a1, 0, pieces[1], block)
-    squeezed, expanded, ust = kernel_call(
+
+    def syncs_a(value):
+        kept["z2"] = conv_call(meta, a1, 0, pieces[1], block, (value,))
+        return (kept["z2"][1],)
+
+    def syncs_b(value):
+        kept["16_2"] = grow(2, kept["8_2"], near2, (value,))
+        kept["far2"] = swap(kept["16_2"], 2, 4)
+        kept["8_3"] = grow(3, kept["4_3"], swap(kept["4_3"], 8), (kept["16_2"],))
+        return (kept["8_3"],)
+
+    def syncs_c(value):
+        kept["1_4"] = m1(4, (value,))
+        return (kept["1_4"],)
+
+    hstats, _, _ = sync(hst, None, (None, syncs_a, syncs_b, syncs_c))
+    z2, msg, e2 = kept["z2"]
+    squeezed, expanded, msg = kernel_call(
         expand_body,
-        [sds((PAIR * EXT, HIDDEN), BF), sds((TASK_COUNT, PAIR * EXT, C)), sds((8, C))],
-        (meta, hidden, hstats, affine, up_w),
-        "svvvv",
+        [sds((PAIR * EXT, HIDDEN), BF), sds((TASK_COUNT, PAIR * EXT, C)), sds((MESSAGE, C))],
+        (meta, hidden, hstats, affine, up_w, msg),
+        "svvvvv",
         flops=2 * PAIR * EXT * C * HIDDEN,
         name="expand",
     )
-    s2, z2r1, z2r2 = sync(st2 + ust, e1, e2)
+    near3 = swap(kept["8_3"], 4, 2)
+
+    def syncu_a(value):
+        kept["4_4"] = grow(4, kept["1_4"], swap(kept["1_4"], 16), (value,))
+        return (kept["4_4"],)
+
+    def syncu_c(value):
+        kept["16_3"] = grow(3, kept["8_3"], near3, (value,))
+        kept["far3"] = swap(kept["16_3"], 2, 4)
+        kept["8_4"] = grow(4, kept["4_4"], swap(kept["4_4"], 8), (kept["16_3"],))
+        return (kept["8_4"],)
+
+    s2, z2r1, z2r2 = sync(msg, e2, (None, syncu_a, None, syncu_c))
+    near4 = swap(kept["8_4"], 4, 2)
+    pieces.append(both_cores(kept["16_2"], kept["far2"]))
+    pieces.append(both_cores(kept["16_3"], kept["far3"]))
     selected = kernel_call(
         select_body,
         [sds((TASK_COUNT, PAIR * EXT, C), BF)],
@@ -1268,16 +1402,21 @@
         [pltpu.VMEM((PAIR * EXT, C), F32)],
         name="select",
     )[0]
-    z3, st3, e31, e32 = zip(
-        *[conv_call(meta, selected, t, pieces[2 + t], block) for t in range(TASK_COUNT)]
-    )
-    s3, _, _ = sync(jnp.concatenate([s[:2] for s in st3] + [jnp.zeros((2, C), F32)]))
-    z3r1 = swap(jnp.concatenate(e31), 1)
-    z3r2 = swap(jnp.concatenate(e32), 3)
+    z30, msg0, e20 = conv_call(meta, selected, 0, pieces[2], block)
+    sixteen4 = grow(4, kept["8_4"], near4, (msg0,))
+    far4 = swap(sixteen4, 2, 4)
+    z31, msg1, e21 = conv_call(meta, selected, 1, pieces[3], block, (sixteen4,))
+    pieces.append(both_cores(sixteen4, far4))
+    z32, msg2, e22 = conv_call(meta, selected, 2, pieces[4], block)
+    z3 = (z30, z31, z32)
+    msg = jnp.concatenate([msg0[:2], msg1[:2], msg2[:2], jnp.zeros((2, C), F32)])
+    s3, _, _ = sync(msg)
+    z3r1 = swap(jnp.concatenate([msg0[STATS:], msg1[STATS:], msg2[STATS:]]), 1)
+    z3r2 = swap(jnp.concatenate([e20, e21, e22]), 3)
     x0_far, a1_far, selected_far = swap(x0, 1), swap(a1, 1), swap(selected, 1)
     pooled, bst = kernel_call(
         pool_body,
-        [sds((TASK_COUNT, PIX // 4, C)), sds((8, C))],
+        [sds((TASK_COUNT, PIX // 4, C)), sds((STATS, C))],
         (meta, lam) + z3 + (s3, cot, affine),
         "ssvvvvvv",
         name="pool",
@@ -1293,54 +1432,66 @@
     )[0]
     dz3_far = swap(dz3, 1)
     ds = [dgrad_call(meta, dz3, t, pieces[2 + t], block) for t in range(TASK_COUNT)]
-    dpu, dp2, bst, e1, e2 = kernel_call(
+    dpu, dp2, bst, e2 = kernel_call(
         branch_grad_body,
         [
             sds((TASK_COUNT, PAIR * PIX, C)),
             sds((PAIR * PIX, C)),
-            sds((8, C)),
-            sds((PAIR * WID, C)),
-            sds((PAIR * WID, C)),
+            sds((MESSAGE, C)),
+            sds((RIM, C)),
         ],
         (meta,) + tuple(ds) + (expanded, z2, s2, affine),
         "svvvvvvv",
         name="branch_grad",
     )
-    b2, dp2r1, dp2r2 = sync(bst, e1, e2)
-    sums = None
-    for t in range(TASK_COUNT):
-        sums = wgrad_call(
-            meta, selected, selected_far, dz3, dz3_far, block, TASK_COUNT, t, sums, (bst,)
-        )
-    task_keep, task_send = scatter_stage(*sums, 4, 2)
+
+    def task_sum(t):
+        def place(value):
+            kept["sums"] = wgrad_call(
+                meta, selected, selected_far, dz3, dz3_far, block, TASK_COUNT, t,
+                kept.get("sums"), (value,),
+            )
+            return (kept["sums"][1],)
+
+        return place
+
+    b2, dp2r1, dp2r2 = sync(bst, e2, (None, task_sum(0), task_sum(1), task_sum(2)))
+    task_keep, task_got = kept["sums"][0], swap(kept["sums"][1], 4, 2)
     dup, dph, hbst = kernel_call(
         expand_grad_body,
-        [sds((TASK_COUNT, B, C)), sds((PAIR * PIX, HIDDEN)), sds((8, C))],
+        [sds((TASK_COUNT, B, C)), sds((PAIR * PIX, HIDDEN)), sds((STATS, C))],
         (meta, dpu, expanded, s2, b2, squeezed, hidden, hstats, up_w, affine),
         "svvvvvvvvv",
         flops=4 * PAIR * PIX * C * HIDDEN,
         name="expand_grad",
-        deps=(sums[1],),
-    )
-    hback, _, _ = sync(hbst)
+    )
     ext_scratch = [pltpu.VMEM((PAIR * EXT, C), F32), pltpu.VMEM((PAIR * EXT, C), F32)]
-    dz2 = kernel_call(
-        functools.partial(norm_grad_body, C),
-        [sds((1, PAIR * EXT, C), BF)],
-        (meta, dp2, dp2r1, dp2r2, z2, z2r1, z2r2, s2, b2, affine),
-        "svvvvvvvvv",
-        ext_scratch,
-        name="norm_grad",
-    )[0]
+
+    def syncd_a(value):
+        kept["dz2"] = kernel_call(
+            functools.partial(norm_grad_body, C),
+            [sds((1, PAIR * EXT, C), BF)],
+            (meta, dp2, dp2r1, dp2r2, z2, z2r1, z2r2, s2, b2, affine),
+            "svvvvvvvvv",
+            ext_scratch,
+            name="norm_grad",
+            deps=(value,),
+        )[0]
+        return (kept["dz2"],)
+
+    def syncd_b(value):
+        kept["da1"] = dgrad_call(meta, kept["dz2"], 0, pieces[1], block, (value,))
+        return (kept["da1"],)
+
+    hback, _, _ = sync(hbst, None, (None, syncd_a, syncd_b))
+    dz2, da1 = kept["dz2"], kept["da1"]
     dz2_far = swap(dz2, 1)
-    da1 = dgrad_call(meta, dz2, 0, pieces[1], block)
-    dp1, bst, e1, e2, ddown = kernel_call(
+    dp1, bst, e2, ddown = kernel_call(
         squeeze_grad_body,
         [
             sds((PAIR * PIX, C)),
-            sds((8, C)),
-            sds((PAIR * WID, C)),
-            sds((PAIR * WID, C)),
+            sds((MESSAGE, C)),
+            sds((RIM, C)),
             sds((C, HIDDEN)),
         ],
         (meta, dph, hidden, hstats, hback, down, a1.reshape(PAIR * EXT, C), da1, z1, s1, affine),
@@ -1348,8 +1499,18 @@
         flops=4 * PAIR * PIX * C * HIDDEN,
         name="squeeze_grad",
     )
-    b1, dp1r1, dp1r2 = sync(bst, e1, e2)
-    keep, send = wgrad_call(meta, a1, a1_far, dz2, dz2_far, block, deps=(bst,))
+
+    def syncf_a(value):
+        kept["second"] = wgrad_call(meta, a1, a1_far, dz2, dz2_far, block, deps=(value,))
+        return (kept["second"][1],)
+
+    def syncf_b(value):
+        kept["task"] = fold(task_keep, task_got, deps=(value,))
+        return (kept["task"][1],)
+
+    b1, dp1r1, dp1r2 = sync(bst, e2, (None, syncf_a, syncf_b))
+    task_keep, task_send = kept["task"]
+    task_got = swap(task_send, 2, 4)
     dz1 = kernel_call(
         functools.partial(norm_grad_body, 0),
         [sds((1, PAIR * EXT, C), BF)],
@@ -1357,17 +1518,20 @@
         "svvvvvvvvv",
         ext_scratch,
         name="norm_grad",
-        deps=(task_send, send),
     )[0]
     dz1_far = swap(dz1, 1)
-    first_sums = wgrad_call(meta, x0, x0_far, dz1, dz1_far, block)
-    dx = dgrad_call(meta, dz1, 0, pieces[0], block, (first_sums[1],))
+    keep0, send0 = wgrad_call(meta, x0, x0_far, dz1, dz1_far, block)
+    dx = dgrad_call(meta, dz1, 0, pieces[0], block, (send0,))
     image_grad = lax.dynamic_slice_in_dim(dx, top * PIX, PIX, 0).reshape(1, BAND, WID, C)
     valid = (jnp.arange(BAND) < own_rows).astype(F32)[None, :, None, None]
     image_grad = image_grad * valid
 
-    task_sums = scatter_last(*scatter_stage(task_keep, task_send, 2, 4))
-    task_shards = join_columns(task_sums, core)
+    def finish(keep, got, middle=(), late=()):
+        keep, send = fold(keep, got, deps=middle)
+        keep = fold(keep, swap(send, 8), True, late)[0]
+        return join_columns(keep, core)
+
+    task_shards = finish(task_keep, task_got, (send0,))
 
     ddown = ddown.reshape(C, TASK_COUNT, B).transpose(1, 0, 2)
     attend = jnp.stack([ddown.reshape(-1), dup.reshape(-1)]).reshape(2, 2, 16, -1, C)
@@ -1382,13 +1546,14 @@
         (spot & 1) + 8 * ((spot >> 1) & 1) + (6 - near) * ((spot >> 2) & 1) + near * (spot >> 3)
     )
     attend = jnp.take(attend, order ^ (me & 15), axis=0).reshape(2, 1, 8, -1, half)
+    keep, send = kept["second"]
     keep = jnp.concatenate([keep, attend[0]], axis=2)
     send = jnp.concatenate([send, attend[1].astype(BF)], axis=2)
-    second = scatter_last(*scatter_stage(*scatter_stage(keep, send, 4, 2), 2, 4))
-    second = join_columns(second, core)
+    keep, send = fold(keep, swap(send, 4, 2))
+    second = finish(keep, swap(send, 2, 4))
     attend_shard = second[0, block:].reshape(1, 2, -1)
-    first = scatter_last(*scatter_stage(*scatter_stage(*first_sums, 4, 2), 2, 4))
-    first = join_columns(first, core)
+    keep, send = fold(keep0, swap(send0, 4, 2))
+    first = finish(keep, swap(send, 2, 4))
     kernel_shard = jnp.concatenate([first, second[:, :block], task_shards])
     kernel_shard = kernel_shard.reshape(1, 2 + TASK_COUNT, -1)
     gain_grads = jnp.concatenate(
@@ -1400,7 +1565,7 @@
     affine_grad = jnp.stack([gain_grads, bias_grads])
     return (
         (pooled.reshape(TASK_COUNT, 1, BAND // 2, WID // 2, C), image_grad)
-        + adamw(kernels, kernel_shard, moment_kernels, square_kernels, RATE_KERNEL)
+        + tuple(adam_call(kernels, kernel_shard, moment_kernels, square_kernels, RATE_KERNEL, 8))
         + adamw(attention, attend_shard, moment_attention, square_attention, RATE_ATTEND)
         + adamw(affine, affine_grad, moment_affine, square_affine, RATE_AFFINE)
     )

time: 897 us -> 616 us (0.69)
  Pallas kernels: 495 us -> 236 us
  other arithmetic: 52.8 us -> 19 us
  waiting for transfers between devices: 214 us -> 182 us
  local copies, waits for them, and re-layouts: 67.9 us -> 93.7 us
  starting transfers between devices: 55.9 us -> 68.6 us
    pallas_call x45 -> x90, Pallas kernels: 495 us -> 227 us  [kernel_call(): pl.pallas_call(run, out_shape=out_shapes, grid=grid, in_specs=[spec(p, a)...]
    unnamed x157 -> x258, local copies, waits for them, and re-layouts: 26.4 us -> 65.9 us
    ppermute x88, waiting for transfers between devices: 214 us -> 182 us  [swap(): return lax.ppermute(value, AXES, pairs)]
    add x37 -> x0, other arithmetic: 13.5 us -> none  [the longest x8 5.7 us: sync(): stats = stats + swap(stats, 8)]
    ppermute x88, starting transfers between devices: 55.9 us -> 68.6 us  [swap(): return lax.ppermute(value, AXES, pairs)]
    pallas_call x0 -> x1, Pallas kernels: none -> 9.21 us  [adam_call(): pl.pallas_call(functools.partial(adam_body, rate), out_shape=[sds(weights...]
  transfers between devices with their start and end apart: 88 -> 88, of which waited for: 47 -> 39; matrix products, arithmetic and copies ran while one was open for 9% -> 7% of each run, Pallas kernels for 29% -> 32%
where the time goes in v3:
time: 616 us; the launch traced here: 604 us
  Pallas kernels  236 us (38%)
  waiting for transfers between devices  182 us (30%)
  local copies, waits for them, and re-layouts  93.7 us (15%)
  starting transfers between devices  68.6 us (11%)
  other arithmetic  19 us (3%)
    pallas_call x90, Pallas kernels, kernel_call(): pl.pallas_call(run, out_shape=out_shapes, grid=grid, in_specs=[spec(p, a)...  227 us
    ppermute x88, waiting for transfers between devices, swap(): return lax.ppermute(value, AXES, pairs)  182 us
    ppermute x88, starting transfers between devices, swap(): return lax.ppermute(value, AXES, pairs)  68.6 us
    unnamed x258, local copies, waits for them, and re-layouts  65.9 us
  transfers between devices with their start and end apart: 88, of which 39 were waited for; matrix products, arithmetic and copies ran while one was open for 7% of the time, Pallas kernels for 32%

profile of v3, /device:TPU:0, one launch (start us, length us, event | category | flops | bytes accessed | tf_op | source)
XLA Modules:
  0.0 604.4 jit_solution(17753101112190822146)
XLA Ops:
  5.0 2.8 slice_reduce_fusion
  13.7 4.0 collective-permute-start.3
  17.8 7.5 %collective-permute-done.3.refs_1_ = bf16[2,144,256]{2,1,0:T(8,128)(2,1)S(1)} collective-permute-done((bf16[2,144,256]{2,1,0:T(8,128)(2,1)}, bf16[2,144,256]{2,1,0:T(8,128)(2,1)S(1)}, u32[]{:S(2)}, u32[]{:S(2)}) %collective-permute-start.3) | collective-permute-done | bytes 147488 | tf_op jit(solution)/shard_map/ppermute | solution.py:456
  47.4 3.3 collective-permute-start.5
  50.8 12.3 %collective-permute-done.5.refs_1_ = bf16[2,168,256]{2,1,0:T(8,128)(2,1)S(1)} collective-permute-done((bf16[2,168,256]{2,1,0:T(8,128)(2,1)}, bf16[2,168,256]{2,1,0:T(8,128)(2,1)S(1)}, u32[]{:S(2)}, u32[]{:S(2)}) %collective-permute-start.5) | collective-permute-done | bytes 172064 | tf_op jit(solution)/shard_map/ppermute | solution.py:456
  72.6 15.9 %collective-permute-done.8.refs_3_ = bf16[16,144,256]{2,1,0:T(8,128)(2,1)S(1)} collective-permute-done((bf16[16,144,256]{2,1,0:T(8,128)(2,1)}, bf16[16,144,256]{2,1,0:T(8,128)(2,1)S(1)}, u32[]{:S(2)}, u32[]{:S(2)}) %collective-permute-start.8) | collective-permute-done | bytes 1179680 | tf_op jit(solution)/shard_map/ppermute | solution.py:456
  88.6 10.4 %collective-permute-done.11.refs_1_ = bf16[4,168,256]{2,1,0:T(8,128)(2,1)S(1)} collective-permute-done((bf16[4,168,256]{2,1,0:T(8,128)(2,1)S(1)}, bf16[4,168,256]{2,1,0:T(8,128)(2,1)S(1)}, u32[]{:S(2)}, u32[]{:S(2)}) %collective-permute-start.11) | collective-permute-done | bytes 344096 | tf_op jit(solution)/shard_map/ppermute | solution.py:456
  107.0 7.7 %collective-permute-done.13.refs_2_ = bf16[3,48,512]{2,1,0:T(8,128)(2,1)S(1)} collective-permute-done((bf16[3,48,512]{2,1,0:T(8,128)(2,1)S(1)}, bf16[3,48,512]{2,1,0:T(8,128)(2,1)S(1)}, u32[]{:S(2)}, u32[]{:S(2)}) %collective-permute-start.13) | collective-permute-done | bytes 147488 | tf_op jit(solution)/shard_map/ppermute | solution.py:456
  122.2 5.7 conv.5
  136.4 17.1 %collective-permute-done.21.refs_3_ = bf16[16,168,256]{2,1,0:T(8,128)(2,1)S(1)} collective-permute-done((bf16[16,168,256]{2,1,0:T(8,128)(2,1)}, bf16[16,168,256]{2,1,0:T(8,128)(2,1)S(1)}, u32[]{:S(2)}, u32[]{:S(2)}) %collective-permute-start.21) | collective-permute-done | bytes 1376288 | tf_op jit(solution)/shard_map/ppermute | solution.py:456
  155.2 2.7 collective-permute-done.15.refs_1_.refs_4_.refs_6_
  187.5 2.8 squeeze.107
  194.9 5.7 conv.6
  205.6 15.7 %collective-permute-done.37.refs_3_ = bf16[16,144,256]{2,1,0:T(8,128)(2,1)S(1)} collective-permute-done((bf16[16,144,256]{2,1,0:T(8,128)(2,1)}, bf16[16,144,256]{2,1,0:T(8,128)(2,1)S(1)}, u32[]{:S(2)}, u32[]{:S(2)}) %collective-permute-start.37) | collective-permute-done | bytes 1179680 | tf_op jit(solution)/shard_map/ppermute | solution.py:456
  226.1 8.2 %collective-permute-done.26.refs_1_ = f32[8,512]{1,0:T(8,128)S(1)} collective-permute-done((f32[8,512]{1,0:T(8,128)S(1)}, f32[8,512]{1,0:T(8,128)S(1)}, u32[]{:S(2)}, u32[]{:S(2)}) %collective-permute-start.26) | collective-permute-done | bytes 16416 | tf_op jit(solution)/shard_map/ppermute | solution.py:456
  238.0 2.8 collective-permute-start.29
  244.7 3.2 expand.1
  255.8 4.4 collective-permute-done.31.refs_1_.refs_3_.refs_6_
  263.4 2.9 collective-permute-done.33.refs_1_
  275.4 2.7 collective-permute-done.34.refs_1_
  280.0 4.1 select.15.refs_1_
  286.2 5.6 conv.7
  296.6 14.8 %collective-permute-done.44.refs_3_ = bf16[16,144,256]{2,1,0:T(8,128)(2,1)S(1)} collective-permute-done((bf16[16,144,256]{2,1,0:T(8,128)(2,1)}, bf16[16,144,256]{2,1,0:T(8,128)(2,1)S(1)}, u32[]{:S(2)}, u32[]{:S(2)}) %collective-permute-start.44) | collective-permute-done | bytes 1179680 | tf_op jit(solution)/shard_map/ppermute | solution.py:456
  314.5 5.7 conv.8
  321.9 5.7 conv.9
  350.0 6.1 %pool.1 = (f32[3,32,512]{2,1,0:T(8,128)}, f32[8,512]{1,0:T(8,128)}) custom-call(s32[8]{0:T(128)} %concatenate.82.refs_0_, f32[3]{0:T(128)} %divide_multiply_fusion.refs_1_, f32[256,512]{1,0:T(8,128)} %get-tuple-element.90.refs_2_, f32[256,512]{1,0:T(8,128)} %get-tuple-element.92.refs_3_, f32[256,512]{1,0:T(8,128)} %get-tuple-element.93.refs_4_, ...), custom_call_target="tpu_custom_call" | custom-call | bytes 2133036 | tf_op jit(solution)/shard_map/pool/pallas_call | solution.py:478
  365.8 2.9 collective-permute-done.55.refs_1_
  370.7 3.9 collective-permute-done.56.refs_1_
  378.0 4.7 task_grad.1.refs_1_.refs_3_
  382.7 5.7 dgrad.5.refs_1_
  388.3 5.7 dgrad.6.refs_2_
  394.0 5.6 dgrad.7.refs_3_
  399.6 5.7 branch_grad.1
  412.1 4.0 wgrad.5
  419.3 3.7 wgrad.6
  425.0 3.9 wgrad.7
  430.9 4.1 expand_grad.1
  444.6 5.6 dgrad.8.refs_2_.refs_7_
  458.1 3.4 squeeze_grad.1
  468.7 4.0 wgrad.8
  476.2 19.1 %collective-permute-done.81.refs_1_ = bf16[1,8,168,256]{3,2,1,0:T(8,128)(2,1)S(1)} collective-permute-done((bf16[1,8,168,256]{3,2,1,0:T(8,128)(2,1)S(1)}, bf16[1,8,168,256]{3,2,1,0:T(8,128)(2,1)S(1)}, u32[]{:S(2)}, u32[]{:S(2)}) %collective-permute-start.81) | collective-permute-done | bytes 688160 | tf_op jit(solution)/shard_map/ppermute | solution.py:456
  504.8 3.9 copy.61.moment
  523.5 4.3 fold.9
  541.6 4.1 wgrad.9
  548.6 2.9 fold.16
  561.4 5.6 dgrad.9
  585.0 9.2 %adam.1 = (f32[1,5,73728]{2,1,0:T(8,128)}, f32[1,5,73728]{2,1,0:T(8,128)}, f32[1,5,73728]{2,1,0:T(8,128)}) custom-call(f32[1,5,73728]{2,1,0:T(8,128)} %copy.60.weights, f32[1,5,73728]{2,1,0:T(8,128)} %pad_maximum_fusion.grad, f32[1,5,73728]{2,1,0:T(8,128)} %copy.61.moment, f32[1,5,73728]{2,1,0:T(8,128)} %copy.62.square), custom_call_target="tpu_custom_call" | custom-call | bytes 10321920 | tf_op jit(solution)/shard_map/adam/pallas_call | solution.py:1219
  594.2 4.4 copy.64
  (567 shorter events, 302.3 us)
Async XLA Ops:
  13.7 11.5 %collective-permute-start.3 = (bf16[2,144,256]{2,1,0:T(8,128)(2,1)}, bf16[2,144,256]{2,1,0:T(8,128)(2,1)S(1)}, u32[]{:S(2)}, u32[]{:S(2)}) collective-permute-start(bf16[2,144,256]{2,1,0:T(8,128)(2,1)} %m1.5.refs_3_.refs_0_), channel_id=1, source_target_pairs={{0,16},{1,17},{2,18},{3,19},{4,20},{5,21},{6,22},{7,23},{8,24},{9,... | collective-permute-start | bytes 442376 | tf_op jit(solution)/shard_map/ppermute | solution.py:456
  27.7 13.9 %collective-permute-start.6 = (bf16[4,144,256]{2,1,0:T(8,128)(2,1)}, bf16[4,144,256]{2,1,0:T(8,128)(2,1)S(1)}, u32[]{:S(2)}, u32[]{:S(2)}) collective-permute-start(bf16[4,144,256]{2,1,0:T(8,128)(2,1)} %m4.5.refs_5_.refs_2_.refs_0_), channel_id=1, source_target_pairs={{0,8},{1,9},{2,10},{3,11},{4,12},{5,13},{6,14},{7,15},{8,0},{9,1},... | collective-permute-start | bytes 884744 | tf_op jit(solution)/shard_map/ppermute | solution.py:456
  44.2 24.7 %collective-permute-start.7 = (bf16[8,144,256]{2,1,0:T(8,128)(2,1)}, bf16[8,144,256]{2,1,0:T(8,128)(2,1)S(1)}, u32[]{:S(2)}, u32[]{:S(2)}) collective-permute-start(bf16[8,144,256]{2,1,0:T(8,128)(2,1)} %m8.5.refs_2_.refs_0_), channel_id=1, source_target_pairs={{0,4},{1,3},{2,6},{3,1},{4,0},{5,7},{6,2},{7,5},{8,12},{9,11},{10,... | collective-permute-start | bytes 1769480 | tf_op jit(solution)/shard_map/ppermute | solution.py:456
  47.4 15.7 %collective-permute-start.5 = (bf16[2,168,256]{2,1,0:T(8,128)(2,1)}, bf16[2,168,256]{2,1,0:T(8,128)(2,1)S(1)}, u32[]{:S(2)}, u32[]{:S(2)}) collective-permute-start(bf16[2,168,256]{2,1,0:T(8,128)(2,1)} %m1.6.refs_0_), channel_id=1, source_target_pairs={{0,16},{1,17},{2,18},{3,19},{4,20},{5,21},{6,22},{7,23},{8,24},{9,... | collective-permute-start | bytes 516104 | tf_op jit(solution)/shard_map/ppermute | solution.py:456
  50.7 15.7 %collective-permute-start.4 = (bf16[160,512]{1,0:T(8,128)(2,1)S(1)}, bf16[160,512]{1,0:T(8,128)(2,1)S(1)}, u32[]{:S(2)}, u32[]{:S(2)}) collective-permute-start(bf16[160,512]{1,0:T(8,128)(2,1)S(1)} %copy-done.44), channel_id=1, source_target_pairs={{0,16},{1,17},{2,18},{3,19},{4,20},{5,21},{6,22},{7,23},{8,24},{9,... | collective-permute-start | bytes 491528 | tf_op jit(solution)/shard_map/ppermute | solution.py:456
  72.0 16.5 %collective-permute-start.8 = (bf16[16,144,256]{2,1,0:T(8,128)(2,1)}, bf16[16,144,256]{2,1,0:T(8,128)(2,1)S(1)}, u32[]{:S(2)}, u32[]{:S(2)}) collective-permute-start(bf16[16,144,256]{2,1,0:T(8,128)(2,1)} %m16.5.refs_2_), channel_id=1, source_target_pairs={{0,2},{1,5},{2,0},{3,7},{4,6},{5,1},{6,4},{7,3},{8,10},{9,13},{10,... | collective-permute-start | bytes 3538952 | tf_op jit(solution)/shard_map/ppermute | solution.py:456
  72.6 47.5 %collective-permute-start.9 = (bf16[16,144,256]{2,1,0:T(8,128)(2,1)}, bf16[16,144,256]{2,1,0:T(8,128)(2,1)S(1)}, u32[]{:S(2)}, u32[]{:S(2)}) collective-permute-start(bf16[16,144,256]{2,1,0:T(8,128)(2,1)} %m16.5.refs_2_), channel_id=1, source_target_pairs={{0,1},{1,0},{2,3},{3,2},{4,5},{5,4},{6,7},{7,6},{8,9},{9,8},{10,11... | collective-permute-start | bytes 3538952 | tf_op jit(solution)/shard_map/ppermute | solution.py:456
  88.5 31.6 %collective-permute-start.10 = (bf16[16,144,256]{2,1,0:T(8,128)(2,1)S(1)}, bf16[16,144,256]{2,1,0:T(8,128)(2,1)S(1)}, u32[]{:S(2)}, u32[]{:S(2)}) collective-permute-start(bf16[16,144,256]{2,1,0:T(8,128)(2,1)S(1)} %collective-permute-done.8.refs_3_), channel_id=1, source_target_pairs={{0,1},{1,0},{2,3},{3,2},{4,5},{5,4},{6,7},{7,6},{8,9},{9,8},{10,11... | collective-permute-start | bytes 3538952 | tf_op jit(solution)/shard_map/ppermute | solution.py:456
  88.5 10.5 %collective-permute-start.11 = (bf16[4,168,256]{2,1,0:T(8,128)(2,1)S(1)}, bf16[4,168,256]{2,1,0:T(8,128)(2,1)S(1)}, u32[]{:S(2)}, u32[]{:S(2)}) collective-permute-start(bf16[4,168,256]{2,1,0:T(8,128)(2,1)S(1)} %copy-done.22), channel_id=1, source_target_pairs={{0,8},{1,9},{2,10},{3,11},{4,12},{5,13},{6,14},{7,15},{8,0},{9,1},... | collective-permute-start | bytes 1032200 | tf_op jit(solution)/shard_map/ppermute | solution.py:456
  101.7 30.0 %collective-permute-start.16 = (bf16[8,168,256]{2,1,0:T(8,128)(2,1)}, bf16[8,168,256]{2,1,0:T(8,128)(2,1)S(1)}, u32[]{:S(2)}, u32[]{:S(2)}) collective-permute-start(bf16[8,168,256]{2,1,0:T(8,128)(2,1)} %m8.6.refs_2_.refs_0_), channel_id=1, source_target_pairs={{0,4},{1,3},{2,6},{3,1},{4,0},{5,7},{6,2},{7,5},{8,12},{9,11},{10,... | collective-permute-start | bytes 2064392 | tf_op jit(solution)/shard_map/ppermute | solution.py:456
  102.4 12.3 %collective-permute-start.13 = (bf16[3,48,512]{2,1,0:T(8,128)(2,1)S(1)}, bf16[3,48,512]{2,1,0:T(8,128)(2,1)S(1)}, u32[]{:S(2)}, u32[]{:S(2)}) collective-permute-start(bf16[3,48,512]{2,1,0:T(8,128)(2,1)S(1)} %copy-done.70), channel_id=1, source_target_pairs={{0,16},{1,17},{2,18},{3,19},{4,20},{5,21},{6,22},{7,23},{8,24},{9,... | collective-permute-start | bytes 442376 | tf_op jit(solution)/shard_map/ppermute | solution.py:456
  105.4 12.4 %collective-permute-start.12 = (bf16[2,144,256]{2,1,0:T(8,128)(2,1)}, bf16[2,144,256]{2,1,0:T(8,128)(2,1)S(1)}, u32[]{:S(2)}, u32[]{:S(2)}) collective-permute-start(bf16[2,144,256]{2,1,0:T(8,128)(2,1)} %m1.7.refs_3_.refs_0_), channel_id=1, source_target_pairs={{0,16},{1,17},{2,18},{3,19},{4,20},{5,21},{6,22},{7,23},{8,24},{9,... | collective-permute-start | bytes 442376 | tf_op jit(solution)/shard_map/ppermute | solution.py:456
  134.9 18.6 %collective-permute-start.21 = (bf16[16,168,256]{2,1,0:T(8,128)(2,1)}, bf16[16,168,256]{2,1,0:T(8,128)(2,1)S(1)}, u32[]{:S(2)}, u32[]{:S(2)}) collective-permute-start(bf16[16,168,256]{2,1,0:T(8,128)(2,1)} %m16.6.refs_2_), channel_id=1, source_target_pairs={{0,2},{1,5},{2,0},{3,7},{4,6},{5,1},{6,4},{7,3},{8,10},{9,13},{10,... | collective-permute-start | bytes 4128776 | tf_op jit(solution)/shard_map/ppermute | solution.py:456
  136.4 44.3 %collective-permute-start.22 = (bf16[16,168,256]{2,1,0:T(8,128)(2,1)}, bf16[16,168,256]{2,1,0:T(8,128)(2,1)S(1)}, u32[]{:S(2)}, u32[]{:S(2)}) collective-permute-start(bf16[16,168,256]{2,1,0:T(8,128)(2,1)} %m16.6.refs_2_), channel_id=1, source_target_pairs={{0,1},{1,0},{2,3},{3,2},{4,5},{5,4},{6,7},{7,6},{8,9},{9,8},{10,11... | collective-permute-start | bytes 4128776 | tf_op jit(solution)/shard_map/ppermute | solution.py:456
  153.5 27.2 %collective-permute-start.23 = (bf16[16,168,256]{2,1,0:T(8,128)(2,1)S(1)}, bf16[16,168,256]{2,1,0:T(8,128)(2,1)}, u32[]{:S(2)}, u32[]{:S(2)}) collective-permute-start(bf16[16,168,256]{2,1,0:T(8,128)(2,1)S(1)} %collective-permute-done.21.refs_3_), channel_id=1, source_target_pairs={{0,1},{1,0},{2,3},{3,2},{4,5},{5,4},{6,7},{7,6},{8,9},{9,8},{10,11... | collective-permute-start | bytes 4128776 | tf_op jit(solution)/shard_map/ppermute | solution.py:456
  153.5 9.5 %collective-permute-start.18 = (bf16[4,144,256]{2,1,0:T(8,128)(2,1)S(1)}, bf16[4,144,256]{2,1,0:T(8,128)(2,1)}, u32[]{:S(2)}, u32[]{:S(2)}) collective-permute-start(bf16[4,144,256]{2,1,0:T(8,128)(2,1)S(1)} %copy-done.26), channel_id=1, source_target_pairs={{0,8},{1,9},{2,10},{3,11},{4,12},{5,13},{6,14},{7,15},{8,0},{9,1},... | collective-permute-start | bytes 884744 | tf_op jit(solution)/shard_map/ppermute | solution.py:456
  166.6 9.7 %collective-permute-start.20 = (bf16[2,144,256]{2,1,0:T(8,128)(2,1)}, bf16[2,144,256]{2,1,0:T(8,128)(2,1)S(1)}, u32[]{:S(2)}, u32[]{:S(2)}) collective-permute-start(bf16[2,144,256]{2,1,0:T(8,128)(2,1)} %m1.8.refs_2_.refs_0_), channel_id=1, source_target_pairs={{0,16},{1,17},{2,18},{3,19},{4,20},{5,21},{6,22},{7,23},{8,24},{9,... | collective-permute-start | bytes 442376 | tf_op jit(solution)/shard_map/ppermute | solution.py:456
  172.7 29.9 %collective-permute-start.28 = (bf16[8,144,256]{2,1,0:T(8,128)(2,1)S(1)}, bf16[8,144,256]{2,1,0:T(8,128)(2,1)}, u32[]{:S(2)}, u32[]{:S(2)}) collective-permute-start(bf16[8,144,256]{2,1,0:T(8,128)(2,1)S(1)} %copy-done.9), channel_id=1, source_target_pairs={{0,4},{1,3},{2,6},{3,1},{4,0},{5,7},{6,2},{7,5},{8,12},{9,11},{10,... | collective-permute-start | bytes 1769480 | tf_op jit(solution)/shard_map/ppermute | solution.py:456
  204.9 16.5 %collective-permute-start.37 = (bf16[16,144,256]{2,1,0:T(8,128)(2,1)}, bf16[16,144,256]{2,1,0:T(8,128)(2,1)S(1)}, u32[]{:S(2)}, u32[]{:S(2)}) collective-permute-start(bf16[16,144,256]{2,1,0:T(8,128)(2,1)} %m16.7.refs_2_), channel_id=1, source_target_pairs={{0,2},{1,5},{2,0},{3,7},{4,6},{5,1},{6,4},{7,3},{8,10},{9,13},{10,... | collective-permute-start | bytes 3538952 | tf_op jit(solution)/shard_map/ppermute | solution.py:456
  205.5 15.9 %collective-permute-start.27 = (bf16[4,144,256]{2,1,0:T(8,128)(2,1)S(1)}, bf16[4,144,256]{2,1,0:T(8,128)(2,1)S(1)}, u32[]{:S(2)}, u32[]{:S(2)}) collective-permute-start(bf16[4,144,256]{2,1,0:T(8,128)(2,1)S(1)} %copy-done.25), channel_id=1, source_target_pairs={{0,8},{1,9},{2,10},{3,11},{4,12},{5,13},{6,14},{7,15},{8,0},{9,1},... | collective-permute-start | bytes 884744 | tf_op jit(solution)/shard_map/ppermute | solution.py:456
  205.5 78.6 %collective-permute-start.38 = (bf16[16,144,256]{2,1,0:T(8,128)(2,1)}, bf16[16,144,256]{2,1,0:T(8,128)(2,1)S(1)}, u32[]{:S(2)}, u32[]{:S(2)}) collective-permute-start(bf16[16,144,256]{2,1,0:T(8,128)(2,1)} %m16.7.refs_2_), channel_id=1, source_target_pairs={{0,1},{1,0},{2,3},{3,2},{4,5},{5,4},{6,7},{7,6},{8,9},{9,8},{10,11... | collective-permute-start | bytes 3538952 | tf_op jit(solution)/shard_map/ppermute | solution.py:456
  221.4 62.8 %collective-permute-start.39 = (bf16[16,144,256]{2,1,0:T(8,128)(2,1)S(1)}, bf16[16,144,256]{2,1,0:T(8,128)(2,1)S(1)}, u32[]{:S(2)}, u32[]{:S(2)}) collective-permute-start(bf16[16,144,256]{2,1,0:T(8,128)(2,1)S(1)} %collective-permute-done.37.refs_3_), channel_id=1, source_target_pairs={{0,1},{1,0},{2,3},{3,2},{4,5},{5,4},{6,7},{7,6},{8,9},{9,8},{10,11... | collective-permute-start | bytes 3538952 | tf_op jit(solution)/shard_map/ppermute | solution.py:456
  224.0 44.3 %collective-permute-start.36 = (bf16[8,144,256]{2,1,0:T(8,128)(2,1)}, bf16[8,144,256]{2,1,0:T(8,128)(2,1)}, u32[]{:S(2)}, u32[]{:S(2)}) collective-permute-start(bf16[8,144,256]{2,1,0:T(8,128)(2,1)} %m8.8.refs_2_.refs_0_), channel_id=1, source_target_pairs={{0,4},{1,3},{2,6},{3,1},{4,0},{5,7},{6,2},{7,5},{8,12},{9,11},{10,... | collective-permute-start | bytes 1769480 | tf_op jit(solution)/shard_map/ppermute | solution.py:456
  224.7 9.7 %collective-permute-start.26 = (f32[8,512]{1,0:T(8,128)S(1)}, f32[8,512]{1,0:T(8,128)S(1)}, u32[]{:S(2)}, u32[]{:S(2)}) collective-permute-start(f32[8,512]{1,0:T(8,128)S(1)} %copy-done.69), channel_id=1, source_target_pairs={{0,4},{1,5},{2,6},{3,7},{4,0},{5,1},{6,2},{7,3},{8,12},{9,13},{10,... | collective-permute-start | bytes 49160 | tf_op jit(solution)/shard_map/ppermute | solution.py:456
  237.9 13.7 %collective-permute-start.32 = (bf16[2,144,256]{2,1,0:T(8,128)(2,1)}, bf16[2,144,256]{2,1,0:T(8,128)(2,1)}, u32[]{:S(2)}, u32[]{:S(2)}) collective-permute-start(bf16[2,144,256]{2,1,0:T(8,128)(2,1)} %m1.9.refs_2_.refs_0_), channel_id=1, source_target_pairs={{0,16},{1,17},{2,18},{3,19},{4,20},{5,21},{6,22},{7,23},{8,24},{9,... | collective-permute-start | bytes 442376 | tf_op jit(solution)/shard_map/ppermute | solution.py:456
  253.3 17.4 %collective-permute-start.35 = (bf16[4,144,256]{2,1,0:T(8,128)(2,1)}, bf16[4,144,256]{2,1,0:T(8,128)(2,1)S(1)}, u32[]{:S(2)}, u32[]{:S(2)}) collective-permute-start(bf16[4,144,256]{2,1,0:T(8,128)(2,1)} %m4.9.refs_2_.refs_0_), channel_id=1, source_target_pairs={{0,8},{1,9},{2,10},{3,11},{4,12},{5,13},{6,14},{7,15},{8,0},{9,1},... | collective-permute-start | bytes 884744 | tf_op jit(solution)/shard_map/ppermute | solution.py:456
  273.3 18.6 %collective-permute-start.43 = (bf16[8,144,256]{2,1,0:T(8,128)(2,1)}, bf16[8,144,256]{2,1,0:T(8,128)(2,1)S(1)}, u32[]{:S(2)}, u32[]{:S(2)}) collective-permute-start(bf16[8,144,256]{2,1,0:T(8,128)(2,1)} %m8.9.refs_2_.refs_0_), channel_id=1, source_target_pairs={{0,4},{1,3},{2,6},{3,1},{4,0},{5,7},{6,2},{7,5},{8,12},{9,11},{10,... | collective-permute-start | bytes 1769480 | tf_op jit(solution)/shard_map/ppermute | solution.py:456
  274.3 21.7 %collective-permute-start.40 = (bf16[16,144,256]{2,1,0:T(8,128)(2,1)S(1)}, bf16[16,144,256]{2,1,0:T(8,128)(2,1)S(1)}, u32[]{:S(2)}, u32[]{:S(2)}) collective-permute-start(bf16[16,144,256]{2,1,0:T(8,128)(2,1)S(1)} %copy-done.2), channel_id=1, source_target_pairs={{0,2},{1,5},{2,0},{3,7},{4,6},{5,1},{6,4},{7,3},{8,10},{9,13},{10,... | collective-permute-start | bytes 3538952 | tf_op jit(solution)/shard_map/ppermute | solution.py:456
  295.0 16.5 %collective-permute-start.44 = (bf16[16,144,256]{2,1,0:T(8,128)(2,1)}, bf16[16,144,256]{2,1,0:T(8,128)(2,1)S(1)}, u32[]{:S(2)}, u32[]{:S(2)}) collective-permute-start(bf16[16,144,256]{2,1,0:T(8,128)(2,1)} %m16.9.refs_6_.refs_2_), channel_id=1, source_target_pairs={{0,2},{1,5},{2,0},{3,7},{4,6},{5,1},{6,4},{7,3},{8,10},{9,13},{10,... | collective-permute-start | bytes 3538952 | tf_op jit(solution)/shard_map/ppermute | solution.py:456
  296.1 16.3 %collective-permute-start.41 = (bf16[16,144,256]{2,1,0:T(8,128)(2,1)S(1)}, bf16[16,144,256]{2,1,0:T(8,128)(2,1)S(1)}, u32[]{:S(2)}, u32[]{:S(2)}) collective-permute-start(bf16[16,144,256]{2,1,0:T(8,128)(2,1)S(1)} %copy-done.2), channel_id=1, source_target_pairs={{0,1},{1,0},{2,3},{3,2},{4,5},{5,4},{6,7},{7,6},{8,9},{9,8},{10,11... | collective-permute-start | bytes 3538952 | tf_op jit(solution)/shard_map/ppermute | solution.py:456
  296.1 16.3 %collective-permute-start.42 = (bf16[16,144,256]{2,1,0:T(8,128)(2,1)S(1)}, bf16[16,144,256]{2,1,0:T(8,128)(2,1)S(1)}, u32[]{:S(2)}, u32[]{:S(2)}) collective-permute-start(bf16[16,144,256]{2,1,0:T(8,128)(2,1)S(1)} %collective-permute-done.40.refs_3_), channel_id=1, source_target_pairs={{0,1},{1,0},{2,3},{3,2},{4,5},{5,4},{6,7},{7,6},{8,9},{9,8},{10,11... | collective-permute-start | bytes 3538952 | tf_op jit(solution)/shard_map/ppermute | solution.py:456
  296.6 24.3 %collective-permute-start.45 = (bf16[16,144,256]{2,1,0:T(8,128)(2,1)}, bf16[16,144,256]{2,1,0:T(8,128)(2,1)S(1)}, u32[]{:S(2)}, u32[]{:S(2)}) collective-permute-start(bf16[16,144,256]{2,1,0:T(8,128)(2,1)} %m16.9.refs_6_.refs_2_), channel_id=1, source_target_pairs={{0,1},{1,0},{2,3},{3,2},{4,5},{5,4},{6,7},{7,6},{8,9},{9,8},{10,11... | collective-permute-start | bytes 3538952 | tf_op jit(solution)/shard_map/ppermute | solution.py:456
  311.5 9.4 %collective-permute-start.46 = (bf16[16,144,256]{2,1,0:T(8,128)(2,1)S(1)}, bf16[16,144,256]{2,1,0:T(8,128)(2,1)}, u32[]{:S(2)}, u32[]{:S(2)}) collective-permute-start(bf16[16,144,256]{2,1,0:T(8,128)(2,1)S(1)} %collective-permute-done.44.refs_3_), channel_id=1, source_target_pairs={{0,1},{1,0},{2,3},{3,2},{4,5},{5,4},{6,7},{7,6},{8,9},{9,8},{10,11... | collective-permute-start | bytes 3538952 | tf_op jit(solution)/shard_map/ppermute | solution.py:456
  333.5 43.1 %collective-permute-start.51 = (f32[96,512]{1,0:T(8,128)S(1)}, f32[96,512]{1,0:T(8,128)S(1)}, u32[]{:S(2)}, u32[]{:S(2)}) collective-permute-start(f32[96,512]{1,0:T(8,128)S(1)} %pad_maximum_fusion.5), channel_id=1, source_target_pairs={{0,1},{1,0},{2,3},{3,2},{4,5},{5,4},{6,7},{7,6},{8,9},{9,8},{10,11... | collective-permute-start | bytes 589832 | tf_op jit(solution)/shard_map/ppermute | solution.py:456
  340.1 36.5 %collective-permute-start.52 = (f32[96,512]{1,0:T(8,128)S(1)}, f32[96,512]{1,0:T(8,128)S(1)}, u32[]{:S(2)}, u32[]{:S(2)}) collective-permute-start(f32[96,512]{1,0:T(8,128)S(1)} %pad_maximum_fusion.6), channel_id=1, source_target_pairs={{0,3},{1,2},{2,1},{3,0},{4,7},{5,6},{6,5},{7,4},{8,11},{9,10},{10,... | collective-permute-start | bytes 589832 | tf_op jit(solution)/shard_map/ppermute | solution.py:456
  370.7 39.4 %collective-permute-start.59 = (bf16[3,320,512]{2,1,0:T(8,128)(2,1)S(1)}, bf16[3,320,512]{2,1,0:T(8,128)(2,1)S(1)}, u32[]{:S(2)}, u32[]{:S(2)}) collective-permute-start(bf16[3,320,512]{2,1,0:T(8,128)(2,1)S(1)} %copy-done), channel_id=1, source_target_pairs={{0,1},{1,0},{2,3},{3,2},{4,5},{5,4},{6,7},{7,6},{8,9},{9,8},{10,11... | collective-permute-start | bytes 2949128 | tf_op jit(solution)/shard_map/ppermute | solution.py:456
  382.7 27.4 %collective-permute-start.60 = (bf16[3,320,512]{2,1,0:T(8,128)(2,1)}, bf16[3,320,512]{2,1,0:T(8,128)(2,1)S(1)}, u32[]{:S(2)}, u32[]{:S(2)}) collective-permute-start(bf16[3,320,512]{2,1,0:T(8,128)(2,1)} %task_grad.1.refs_1_.refs_3_), channel_id=1, source_target_pairs={{0,1},{1,0},{2,3},{3,2},{4,5},{5,4},{6,7},{7,6},{8,9},{9,8},{10,11... | collective-permute-start | bytes 2949128 | tf_op jit(solution)/shard_map/ppermute | solution.py:456
  454.2 14.5 %collective-permute-start.69 = (bf16[1,320,512]{2,1,0:T(8,128)(2,1)S(1)}, bf16[1,320,512]{2,1,0:T(8,128)(2,1)}, u32[]{:S(2)}, u32[]{:S(2)}) collective-permute-start(bf16[1,320,512]{2,1,0:T(8,128)(2,1)S(1)} %copy-done.32), channel_id=1, source_target_pairs={{0,1},{1,0},{2,3},{3,2},{4,5},{5,4},{6,7},{7,6},{8,9},{9,8},{10,11... | collective-permute-start | bytes 983048 | tf_op jit(solution)/shard_map/ppermute | solution.py:456
  454.3 14.4 %collective-permute-start.70 = (bf16[1,320,512]{2,1,0:T(8,128)(2,1)S(1)}, bf16[1,320,512]{2,1,0:T(8,128)(2,1)}, u32[]{:S(2)}, u32[]{:S(2)}) collective-permute-start(bf16[1,320,512]{2,1,0:T(8,128)(2,1)S(1)} %copy-done.23), channel_id=1, source_target_pairs={{0,1},{1,0},{2,3},{3,2},{4,5},{5,4},{6,7},{7,6},{8,9},{9,8},{10,11... | collective-permute-start | bytes 983048 | tf_op jit(solution)/shard_map/ppermute | solution.py:456
  465.5 58.1 %collective-permute-start.72 = (bf16[3,8,144,256]{3,2,1,0:T(8,128)(2,1)S(1)}, bf16[3,8,144,256]{3,2,1,0:T(8,128)(2,1)}, u32[]{:S(2)}, u32[]{:S(2)}) collective-permute-start(bf16[3,8,144,256]{3,2,1,0:T(8,128)(2,1)S(1)} %copy-done.1), channel_id=1, source_target_pairs={{0,4},{1,3},{2,6},{3,1},{4,0},{5,7},{6,2},{7,5},{8,12},{9,11},{10,... | collective-permute-start | bytes 5308424 | tf_op jit(solution)/shard_map/ppermute | solution.py:456
  474.0 21.4 %collective-permute-start.81 = (bf16[1,8,168,256]{3,2,1,0:T(8,128)(2,1)S(1)}, bf16[1,8,168,256]{3,2,1,0:T(8,128)(2,1)S(1)}, u32[]{:S(2)}, u32[]{:S(2)}) collective-permute-start(bf16[1,8,168,256]{3,2,1,0:T(8,128)(2,1)S(1)} %pad_maximum_fusion.3), channel_id=1, source_target_pairs={{0,4},{1,3},{2,6},{3,1},{4,0},{5,7},{6,2},{7,5},{8,12},{9,11},{10,... | collective-permute-start | bytes 2064392 | tf_op jit(solution)/shard_map/ppermute | solution.py:456
  498.7 13.5 %collective-permute-start.82 = (bf16[1,4,168,256]{3,2,1,0:T(8,128)(2,1)}, bf16[1,4,168,256]{3,2,1,0:T(8,128)(2,1)}, u32[]{:S(2)}, u32[]{:S(2)}) collective-permute-start(bf16[1,4,168,256]{3,2,1,0:T(8,128)(2,1)} %get-tuple-element.129), channel_id=1, source_target_pairs={{0,2},{1,5},{2,0},{3,7},{4,6},{5,1},{6,4},{7,3},{8,10},{9,13},{10,... | collective-permute-start | bytes 1032200 | tf_op jit(solution)/shard_map/ppermute | solution.py:456
  511.1 28.3 %collective-permute-start.74 = (bf16[1,320,512]{2,1,0:T(8,128)(2,1)S(1)}, bf16[1,320,512]{2,1,0:T(8,128)(2,1)S(1)}, u32[]{:S(2)}, u32[]{:S(2)}) collective-permute-start(bf16[1,320,512]{2,1,0:T(8,128)(2,1)S(1)} %bitcast.66), channel_id=1, source_target_pairs={{0,1},{1,0},{2,3},{3,2},{4,5},{5,4},{6,7},{7,6},{8,9},{9,8},{10,11... | collective-permute-start | bytes 983048 | tf_op jit(solution)/shard_map/ppermute | solution.py:456
  518.5 9.3 %collective-permute-start.71 = (f32[8,512]{1,0:T(8,128)}, f32[8,512]{1,0:T(8,128)S(1)}, u32[]{:S(2)}, u32[]{:S(2)}) collective-permute-start(f32[8,512]{1,0:T(8,128)} %combine.61.refs_2_.refs_0_), channel_id=1, source_target_pairs={{0,4},{1,5},{2,6},{3,7},{4,0},{5,1},{6,2},{7,3},{8,12},{9,13},{10,... | collective-permute-start | bytes 49160 | tf_op jit(solution)/shard_map/ppermute | solution.py:456
  531.6 16.0 %collective-permute-start.84 = (f32[1,168,256]{2,1,0:T(8,128)S(1)}, f32[1,168,256]{2,1,0:T(8,128)S(1)}, u32[]{:S(2)}, u32[]{:S(2)}) collective-permute-start(f32[1,168,256]{2,1,0:T(8,128)S(1)} %get-tuple-element.192), channel_id=1, source_target_pairs={{0,1},{1,0},{2,3},{3,2},{4,5},{5,4},{6,7},{7,6},{8,9},{9,8},{10,11... | collective-permute-start | bytes 516104 | tf_op jit(solution)/shard_map/ppermute | solution.py:456
  531.7 16.0 %collective-permute-start.85 = (bf16[3,4,144,256]{3,2,1,0:T(8,128)(2,1)S(1)}, bf16[3,4,144,256]{3,2,1,0:T(8,128)(2,1)S(1)}, u32[]{:S(2)}, u32[]{:S(2)}) collective-permute-start(bf16[3,4,144,256]{3,2,1,0:T(8,128)(2,1)S(1)} %copy-done.34), channel_id=1, source_target_pairs={{0,2},{1,5},{2,0},{3,7},{4,6},{5,1},{6,4},{7,3},{8,10},{9,13},{10,... | collective-permute-start | bytes 2654216 | tf_op jit(solution)/shard_map/ppermute | solution.py:456
  545.7 10.2 %collective-permute-start.76 = (bf16[1,8,144,256]{3,2,1,0:T(8,128)(2,1)}, bf16[1,8,144,256]{3,2,1,0:T(8,128)(2,1)S(1)}, u32[]{:S(2)}, u32[]{:S(2)}) collective-permute-start(bf16[1,8,144,256]{3,2,1,0:T(8,128)(2,1)} %get-tuple-element.119.refs_6_.refs_2_), channel_id=1, source_target_pairs={{0,4},{1,3},{2,6},{3,1},{4,0},{5,7},{6,2},{7,5},{8,12},{9,11},{10,... | collective-permute-start | bytes 1769480 | tf_op jit(solution)/shard_map/ppermute | solution.py:456
  551.5 20.9 %collective-permute-start.86 = (bf16[3,2,144,256]{3,2,1,0:T(8,128)(2,1)}, bf16[3,2,144,256]{3,2,1,0:T(8,128)(2,1)S(1)}, u32[]{:S(2)}, u32[]{:S(2)}) collective-permute-start(bf16[3,2,144,256]{3,2,1,0:T(8,128)(2,1)} %get-tuple-element.134), channel_id=1, source_target_pairs={{0,8},{1,9},{2,10},{3,11},{4,12},{5,13},{6,14},{7,15},{8,0},{9,1},... | collective-permute-start | bytes 1327112 | tf_op jit(solution)/shard_map/ppermute | solution.py:456
  (157 other events, 759.2 us)
